TPU v7x, 256 devices: a whole 4x4x8 slice. The times are simulated.
256 devices in a mesh: frame: 32 (over x, z_hi, y), tile: 8 (over z_lo, core).
Axes of the slice: x: 4, y: 4, z: 8 (z_hi: 2, z_lo: 4; z = z_hi * 4 + z_lo), core: 2. Of those that a mesh axis runs over, the one named last changes fastest.
Arguments:
- features: bfloat16 [64, 30720, 256], P('frame', 'tile')
- query_frame: int32 [2048], replicated, may hold values from 0 to 63
- query_row: int32 [2048], replicated, may hold values from 0 to 63
- query_col: int32 [2048], replicated, may hold values from 0 to 479
- conv_weight: float32 [3, 4, 256], replicated, may hold values from -1.75 to 1.75
- conv_bias: float32 [256], replicated, may hold values from -4 to 4
- out_weight: float32 [3, 256], replicated, may hold values from -0.375 to 0.375
Outputs:
- tracks: float32 [64, 3, 2048], P('frame', None, 'tile')
All inputs are finite; a program needn't handle non-finite values.
Results may differ from a plain program's by a relative error of at most 0.00035.
Values may be sent and summed in bfloat16 or wider, within the bound.
No kernel may reach another device: no remote copies, remote signals or barrier semaphores. Data moves between devices by JAX's collectives and lax.ppermute only.
A program may use at most 64 MiB of HBM per device.

v0:
```python
import math

import jax
import jax.numpy as jnp
from jax import lax
from jax.sharding import PartitionSpec as P

W = 480


def merged_2(array, axis, combine):
    everything = jax.tree.map(lambda part: lax.all_gather(part, axis), array)
    initial = jax.tree.map(lambda part: part[0], everything)

    def step(k, so_far):
        return combine(so_far, jax.tree.map(lambda part: part[k], everything))

    return lax.fori_loop(1, lax.axis_size(axis), step, initial)


def with_halo(array, sides, width):
    for axis, dim in sides:
        devices, length = (lax.axis_size(axis), array.shape[dim])
        up = [(i, (i + 1) % devices) for i in range(devices - 1)]
        down = [(j, i) for i, j in up]
        last = lax.slice_in_dim(array, length - width, length, axis=dim)
        initial = lax.slice_in_dim(array, 0, width, axis=dim)
        before = lax.ppermute(last, axis, up)
        after = lax.ppermute(initial, axis, down)
        array = jnp.concatenate([before, array, after], axis=dim)
    return array


def combine_parts(first, second):
    peak = jnp.maximum(first[0], second[0])
    left = jnp.exp(first[0] - peak)
    right = jnp.exp(second[0] - peak)
    return (
        peak,
        first[1] * left + second[1] * right,
        first[2] * left + second[2] * right,
        first[3] * left + second[3] * right,
    )


def local(features, query_frame, query_row, query_col, conv_weight, conv_bias, out_weight):
    frame_count = features.shape[0]
    pix_count = features.shape[1]
    rows_here = pix_count // W
    tiles = lax.axis_size("tile")
    height = rows_here * tiles
    frame_idx = lax.axis_index("frame")
    tile_idx = lax.axis_index("tile")
    queries = query_frame.shape[0]
    owned = (query_frame // frame_count == frame_idx) & (query_row // rows_here == tile_idx)
    local_frame = jnp.clip(query_frame - frame_idx * frame_count, 0, frame_count - 1)
    local_pix = jnp.clip((query_row - tile_idx * rows_here) * W + query_col, 0, pix_count - 1)
    picked = features[local_frame, local_pix].astype(jnp.float32)
    term = jnp.where(owned[:, None], picked, 0.0)
    query_feat = lax.psum(term, ("frame", "tile")).astype(jnp.bfloat16)
    col_coord = jnp.arange(W).astype(jnp.float32) / W
    row_coord = (tile_idx * rows_here + jnp.arange(rows_here)).astype(jnp.float32) / height
    block = min(512, queries)
    blocks = query_feat.reshape(queries // block, block, query_feat.shape[1])
    peaks, totals, sums_x, sums_y = ([], [], [], [])
    for frame in range(frame_count):
        frame_feat = features[frame]

        def one_block(query_block):
            scores = (
                jnp.einsum("qc,pc->qp", query_block, frame_feat, preferred_element_type=jnp.float32)
                / 16.0
            )
            peak = jnp.max(scores, axis=1)
            expo = jnp.exp(scores - peak[:, None]).reshape(query_block.shape[0], rows_here, W)
            col_sum = jnp.sum(expo, axis=1)
            row_sum = jnp.sum(expo, axis=2)
            sum_x = jnp.sum(col_sum * col_coord[None, :], axis=1)
            sum_y = jnp.sum(row_sum * row_coord[None, :], axis=1)
            return (peak, jnp.sum(row_sum, axis=1), sum_x, sum_y)

        peak, total, sum_x, sum_y = lax.map(one_block, blocks)
        peaks.append(peak.reshape(queries))
        totals.append(total.reshape(queries))
        sums_x.append(sum_x.reshape(queries))
        sums_y.append(sum_y.reshape(queries))
    parts = (jnp.stack(peaks), jnp.stack(totals), jnp.stack(sums_x), jnp.stack(sums_y))
    share_len = queries // tiles
    merged = merged_2(parts, "tile", combine_parts)
    peak, total, sum_x, sum_y = [
        lax.dynamic_slice_in_dim(item, tile_idx * share_len, share_len, 1) for item in merged
    ]
    log_total = jnp.log(total)
    inputs = jnp.stack(
        [sum_x / total, sum_y / total, -log_total, peak + log_total - math.log(height * W)], axis=1
    )
    padded = with_halo(inputs, (("frame", 0),), 1)
    acc = conv_bias[None, :, None]
    for k in range(3):
        acc = acc + jnp.einsum(
            "tcq,ch->thq",
            padded[k : k + frame_count],
            conv_weight[k],
            precision=lax.Precision.HIGHEST,
        )
    hidden = jax.nn.gelu(acc)
    delta = jnp.einsum("thq,oh->toq", hidden, out_weight, precision=lax.Precision.HIGHEST)
    return inputs[:, 0:3] + delta


def solution(mesh):
    in_specs = (P("frame", "tile", None), P(), P(), P(), P(), P(), P())
    out_specs = P("frame", None, "tile")
    return jax.shard_map(local, mesh=mesh, in_specs=in_specs, out_specs=out_specs, check_vma=False)
```

profile of v0, /device:TPU:6, one launch (start us, length us, event | category | flops | bytes accessed | tf_op | source)
XLA Modules:
  0.0 420.7 jit_solution(14460496496460463035)
XLA Ops:
  0.0 3.7 slice_bitcast_fusion.1
  3.8 79.7 %gather_fusion = bf16[2048,256]{1,0:T(8,128)(2,1)} fusion(bf16[2,3840,256]{2,1,0:T(8,128)(2,1)} %param.13, s32[2048]{0:T(1024)S(1)} %fusion.53), kind=kCustom, calls=%fused_computation | custom fusion | bytes 2113536 | tf_op jit(solution)/shard_map/gather | solution.py:58
  83.5 2.9 convert_select_fusion
  86.4 93.0 %all-reduce.1 = bf16[2048,256]{1,0:T(8,128)(2,1)} all-reduce(f32[2048,256]{1,0:T(8,128)} %convert_select_fusion), channel_id=1, replica_groups=mesh['frame'=32,'tile'=8] {'frame','tile'}, use_global_device_ids=true, to_apply=%region_0.1 | all-reduce | flops 524288 | bytes 3145728 | tf_op jit(solution)/shard_map/psum | solution.py:60
  179.5 85.2 %while.56 = (s32[]{:T(128)}, f32[4,512]{1,0:T(4,128)S(1)}, f32[4,512]{1,0:T(4,128)S(1)}, f32[4,512]{1,0:T(4,128)S(1)}, f32[4,512]{1,0:T(4,128)S(1)}, /*index=5*/...) while((s32[]{:T(128)}, f32[4,512]{1,0:T(4,128)S(1)}, ...), condition=%wide.region_8.9_spmd.clone, body=%wide.region_1.8_spmd.clone.sunk | while | flops 1020644288 | bytes 51444152 | solution.py:82
  179.5 3.0 multiply_reduce_fusion.12
  182.4 4.4 %fusion.91 = (f32[512]{0:T(512)S(1)}, f32[512,3840]{1,0:T(8,128)}) fusion(f32[512]{0:T(512)S(1)} %get-tuple-element.619, f32[512,3840]{1,0:T(8,128)S(1)} %get-tuple-element.620), kind=kLoop, calls=%fused_computation.122.clone.1 | loop fusion | flops 5897728 | bytes 15732736 | tf_op jit(solution)/shard_map/while/body/eval_jaxpr/reduce_sum | solution.py:80
  186.9 9.1 %copy.39 = f32[512,3840]{0,1:T(8,128)} copy(f32[512,3840]{1,0:T(8,128)} %get-tuple-element.622) | data formatting | bytes 15728640 | tf_op jit(solution)/shard_map/while/body/eval_jaxpr/exp | solution.py:75
  195.9 4.4 %fusion.92 = (f32[512,8]{0,1:T(8,128)S(1)}, f32[512,480]{0,1:T(8,128)S(1)}) fusion(f32[512,8,480]{0,2,1:T(8,128)} %bitcast.153), kind=kLoop, calls=%fused_computation.120.clone.1 | loop fusion | flops 3682304 | bytes 8863744 | tf_op jit(solution)/shard_map/while/body/eval_jaxpr/reduce_sum | solution.py:77
  200.8 2.9 multiply_reduce_fusion.12
  203.7 4.4 %fusion.91 = (f32[512]{0:T(512)S(1)}, f32[512,3840]{1,0:T(8,128)}) fusion(f32[512]{0:T(512)S(1)} %get-tuple-element.619, f32[512,3840]{1,0:T(8,128)S(1)} %get-tuple-element.620), kind=kLoop, calls=%fused_computation.122.clone.1 | loop fusion | flops 5897728 | bytes 15732736 | tf_op jit(solution)/shard_map/while/body/eval_jaxpr/reduce_sum | solution.py:80
  208.2 9.1 %copy.39 = f32[512,3840]{0,1:T(8,128)} copy(f32[512,3840]{1,0:T(8,128)} %get-tuple-element.622) | data formatting | bytes 15728640 | tf_op jit(solution)/shard_map/while/body/eval_jaxpr/exp | solution.py:75
  217.2 4.4 %fusion.92 = (f32[512,8]{0,1:T(8,128)S(1)}, f32[512,480]{0,1:T(8,128)S(1)}) fusion(f32[512,8,480]{0,2,1:T(8,128)} %bitcast.153), kind=kLoop, calls=%fused_computation.120.clone.1 | loop fusion | flops 3682304 | bytes 8863744 | tf_op jit(solution)/shard_map/while/body/eval_jaxpr/reduce_sum | solution.py:77
  222.1 3.0 multiply_reduce_fusion.12
  225.0 4.4 %fusion.91 = (f32[512]{0:T(512)S(1)}, f32[512,3840]{1,0:T(8,128)}) fusion(f32[512]{0:T(512)S(1)} %get-tuple-element.619, f32[512,3840]{1,0:T(8,128)S(1)} %get-tuple-element.620), kind=kLoop, calls=%fused_computation.122.clone.1 | loop fusion | flops 5897728 | bytes 15732736 | tf_op jit(solution)/shard_map/while/body/eval_jaxpr/reduce_sum | solution.py:80
  229.4 9.1 %copy.39 = f32[512,3840]{0,1:T(8,128)} copy(f32[512,3840]{1,0:T(8,128)} %get-tuple-element.622) | data formatting | bytes 15728640 | tf_op jit(solution)/shard_map/while/body/eval_jaxpr/exp | solution.py:75
  238.5 4.4 %fusion.92 = (f32[512,8]{0,1:T(8,128)S(1)}, f32[512,480]{0,1:T(8,128)S(1)}) fusion(f32[512,8,480]{0,2,1:T(8,128)} %bitcast.153), kind=kLoop, calls=%fused_computation.120.clone.1 | loop fusion | flops 3682304 | bytes 8863744 | tf_op jit(solution)/shard_map/while/body/eval_jaxpr/reduce_sum | solution.py:77
  243.4 3.0 multiply_reduce_fusion.12
  246.3 4.4 %fusion.91 = (f32[512]{0:T(512)S(1)}, f32[512,3840]{1,0:T(8,128)}) fusion(f32[512]{0:T(512)S(1)} %get-tuple-element.619, f32[512,3840]{1,0:T(8,128)S(1)} %get-tuple-element.620), kind=kLoop, calls=%fused_computation.122.clone.1 | loop fusion | flops 5897728 | bytes 15732736 | tf_op jit(solution)/shard_map/while/body/eval_jaxpr/reduce_sum | solution.py:80
  250.7 9.1 %copy.39 = f32[512,3840]{0,1:T(8,128)} copy(f32[512,3840]{1,0:T(8,128)} %get-tuple-element.622) | data formatting | bytes 15728640 | tf_op jit(solution)/shard_map/while/body/eval_jaxpr/exp | solution.py:75
  259.8 4.4 %fusion.92 = (f32[512,8]{0,1:T(8,128)S(1)}, f32[512,480]{0,1:T(8,128)S(1)}) fusion(f32[512,8,480]{0,2,1:T(8,128)} %bitcast.153), kind=kLoop, calls=%fused_computation.120.clone.1 | loop fusion | flops 3682304 | bytes 8863744 | tf_op jit(solution)/shard_map/while/body/eval_jaxpr/reduce_sum | solution.py:77
  264.7 82.5 %while.57 = (s32[]{:T(128)}, f32[4,512]{1,0:T(4,128)S(1)}, f32[4,512]{1,0:T(4,128)S(1)}, f32[4,512]{1,0:T(4,128)S(1)}, f32[4,512]{1,0:T(4,128)S(1)}, /*index=5*/...) while((s32[]{:T(128)}, f32[4,512]{1,0:T(4,128)S(1)}, ...), condition=%wide.region_16.17_spmd.clone, body=%wide.region_9.16_spmd.clone.sunk | while | flops 1020644288 | bytes 51444152 | solution.py:82
  264.8 2.3 multiply_reduce_fusion.15
  267.0 4.4 %fusion.94 = (f32[512]{0:T(512)S(1)}, f32[512,3840]{1,0:T(8,128)}) fusion(f32[512]{0:T(512)S(1)} %get-tuple-element.633, f32[512,3840]{1,0:T(8,128)S(1)} %get-tuple-element.634), kind=kLoop, calls=%fused_computation.123.clone.1 | loop fusion | flops 5897728 | bytes 15732736 | tf_op jit(solution)/shard_map/while/body/eval_jaxpr/reduce_sum | solution.py:80
  271.5 9.1 %copy.40 = f32[512,3840]{0,1:T(8,128)} copy(f32[512,3840]{1,0:T(8,128)} %get-tuple-element.636) | data formatting | bytes 15728640 | tf_op jit(solution)/shard_map/while/body/eval_jaxpr/exp | solution.py:75
  280.5 4.4 %fusion.95 = (f32[512,8]{0,1:T(8,128)S(1)}, f32[512,480]{0,1:T(8,128)S(1)}) fusion(f32[512,8,480]{0,2,1:T(8,128)} %bitcast.154), kind=kLoop, calls=%fused_computation.121.clone.1 | loop fusion | flops 3682304 | bytes 8863744 | tf_op jit(solution)/shard_map/while/body/eval_jaxpr/reduce_sum | solution.py:77
  285.4 2.3 multiply_reduce_fusion.15
  287.7 4.4 %fusion.94 = (f32[512]{0:T(512)S(1)}, f32[512,3840]{1,0:T(8,128)}) fusion(f32[512]{0:T(512)S(1)} %get-tuple-element.633, f32[512,3840]{1,0:T(8,128)S(1)} %get-tuple-element.634), kind=kLoop, calls=%fused_computation.123.clone.1 | loop fusion | flops 5897728 | bytes 15732736 | tf_op jit(solution)/shard_map/while/body/eval_jaxpr/reduce_sum | solution.py:80
  292.1 9.1 %copy.40 = f32[512,3840]{0,1:T(8,128)} copy(f32[512,3840]{1,0:T(8,128)} %get-tuple-element.636) | data formatting | bytes 15728640 | tf_op jit(solution)/shard_map/while/body/eval_jaxpr/exp | solution.py:75
  301.2 4.4 %fusion.95 = (f32[512,8]{0,1:T(8,128)S(1)}, f32[512,480]{0,1:T(8,128)S(1)}) fusion(f32[512,8,480]{0,2,1:T(8,128)} %bitcast.154), kind=kLoop, calls=%fused_computation.121.clone.1 | loop fusion | flops 3682304 | bytes 8863744 | tf_op jit(solution)/shard_map/while/body/eval_jaxpr/reduce_sum | solution.py:77
  306.0 2.3 multiply_reduce_fusion.15
  308.3 4.4 %fusion.94 = (f32[512]{0:T(512)S(1)}, f32[512,3840]{1,0:T(8,128)}) fusion(f32[512]{0:T(512)S(1)} %get-tuple-element.633, f32[512,3840]{1,0:T(8,128)S(1)} %get-tuple-element.634), kind=kLoop, calls=%fused_computation.123.clone.1 | loop fusion | flops 5897728 | bytes 15732736 | tf_op jit(solution)/shard_map/while/body/eval_jaxpr/reduce_sum | solution.py:80
  312.7 9.1 %copy.40 = f32[512,3840]{0,1:T(8,128)} copy(f32[512,3840]{1,0:T(8,128)} %get-tuple-element.636) | data formatting | bytes 15728640 | tf_op jit(solution)/shard_map/while/body/eval_jaxpr/exp | solution.py:75
  321.8 4.4 %fusion.95 = (f32[512,8]{0,1:T(8,128)S(1)}, f32[512,480]{0,1:T(8,128)S(1)}) fusion(f32[512,8,480]{0,2,1:T(8,128)} %bitcast.154), kind=kLoop, calls=%fused_computation.121.clone.1 | loop fusion | flops 3682304 | bytes 8863744 | tf_op jit(solution)/shard_map/while/body/eval_jaxpr/reduce_sum | solution.py:77
  326.7 2.3 multiply_reduce_fusion.15
  328.9 4.4 %fusion.94 = (f32[512]{0:T(512)S(1)}, f32[512,3840]{1,0:T(8,128)}) fusion(f32[512]{0:T(512)S(1)} %get-tuple-element.633, f32[512,3840]{1,0:T(8,128)S(1)} %get-tuple-element.634), kind=kLoop, calls=%fused_computation.123.clone.1 | loop fusion | flops 5897728 | bytes 15732736 | tf_op jit(solution)/shard_map/while/body/eval_jaxpr/reduce_sum | solution.py:80
  333.4 9.1 %copy.40 = f32[512,3840]{0,1:T(8,128)} copy(f32[512,3840]{1,0:T(8,128)} %get-tuple-element.636) | data formatting | bytes 15728640 | tf_op jit(solution)/shard_map/while/body/eval_jaxpr/exp | solution.py:75
  342.4 4.4 %fusion.95 = (f32[512,8]{0,1:T(8,128)S(1)}, f32[512,480]{0,1:T(8,128)S(1)}) fusion(f32[512,8,480]{0,2,1:T(8,128)} %bitcast.154), kind=kLoop, calls=%fused_computation.121.clone.1 | loop fusion | flops 3682304 | bytes 8863744 | tf_op jit(solution)/shard_map/while/body/eval_jaxpr/reduce_sum | solution.py:77
  347.3 14.3 %all-gather.7 = f32[8,2,2048]{2,1,0:T(2,128)S(1)} all-gather(f32[1,2,2048]{2,1,0:T(2,128)S(1)} %maximum_bitcast_fusion.3), channel_id=5, replica_groups=mesh['frame'=32,'tile'=8] {'tile'}, dimensions={0}, use_global_device_ids=true | all-gather | bytes 147456 | tf_op jit(solution)/shard_map/all_gather | solution.py:12
  361.6 14.0 %all-gather.6 = f32[8,2,2048]{2,1,0:T(2,128)S(1)} all-gather(f32[1,2,2048]{2,1,0:T(2,128)S(1)} %maximum_bitcast_fusion.2), channel_id=4, replica_groups=mesh['frame'=32,'tile'=8] {'tile'}, dimensions={0}, use_global_device_ids=true | all-gather | bytes 147456 | tf_op jit(solution)/shard_map/all_gather | solution.py:12
  375.7 14.0 %all-gather.5 = f32[8,2,2048]{2,1,0:T(2,128)S(1)} all-gather(f32[1,2,2048]{2,1,0:T(2,128)S(1)} %maximum_bitcast_fusion.1), channel_id=3, replica_groups=mesh['frame'=32,'tile'=8] {'tile'}, dimensions={0}, use_global_device_ids=true | all-gather | bytes 147456 | tf_op jit(solution)/shard_map/all_gather | solution.py:12
  389.7 14.0 %all-gather.4 = f32[8,2,2048]{2,1,0:T(2,128)S(1)} all-gather(f32[1,2,2048]{2,1,0:T(2,128)S(1)} %maximum_bitcast_fusion), channel_id=2, replica_groups=mesh['frame'=32,'tile'=8] {'tile'}, dimensions={0}, use_global_device_ids=true | all-gather | bytes 147456 | tf_op jit(solution)/shard_map/all_gather | solution.py:12
  403.7 0.9 while.55
  404.7 3.8 collective-permute-start
  408.5 8.9 %collective-permute-start.1 = (f32[1,4,256]{2,1,0:T(4,128)S(1)}, f32[1,4,256]{2,1,0:T(4,128)S(1)}, u32[]{:S(2)}, u32[]{:S(2)}) collective-permute-start(f32[1,4,256]{2,1,0:T(4,128)S(1)} %get-tuple-element.452), channel_id=1, source_target_pairs={{8,0},{16,8},{24,16},{32,24},{40,32},{48,40},{56,48},{64,56},{72,6... | collective-permute-start | bytes 12296 | tf_op jit(solution)/shard_map/ppermute | solution.py:29
  417.5 0.6 fusion.62
  418.1 0.6 fusion.21
  418.8 0.8 fusion.28
  (134 shorter events, 5.6 us)
Async XLA Ops:
  0.0 419.6 %copy-start = (f32[3,256]{1,0:T(4,128)S(1)}, f32[3,256]{1,0:T(4,128)}, u32[]{:S(2)}) copy-start(f32[3,256]{1,0:T(4,128)} %param.19) | copy-start | bytes 9220
  0.0 3.7 copy-start.2
  0.0 3.7 copy-start.1
  0.0 3.7 copy-start.3
  264.7 152.7 %copy-start.4 = (f32[3,4,256]{2,1,0:T(4,128)S(1)}, f32[3,4,256]{2,1,0:T(4,128)}, u32[]{:S(2)}) copy-start(f32[3,4,256]{2,1,0:T(4,128)} %param.17) | copy-start | bytes 36868
  264.7 153.4 %copy-start.5 = (f32[256]{0:T(256)S(1)}, f32[256]{0:T(256)}, u32[]{:S(2)}) copy-start(f32[256]{0:T(256)} %param.18) | copy-start | bytes 3076
  404.7 13.4 %collective-permute-start = (f32[1,4,256]{2,1,0:T(4,128)S(1)}, f32[1,4,256]{2,1,0:T(4,128)S(1)}, u32[]{:S(2)}, u32[]{:S(2)}) collective-permute-start(f32[1,4,256]{2,1,0:T(4,128)S(1)} %get-tuple-element.453), channel_id=1, source_target_pairs={{0,8},{8,16},{16,24},{24,32},{32,40},{40,48},{48,56},{56,64},{64,7... | collective-permute-start | bytes 12296 | tf_op jit(solution)/shard_map/ppermute | solution.py:28
  408.5 10.3 %collective-permute-start.1 = (f32[1,4,256]{2,1,0:T(4,128)S(1)}, f32[1,4,256]{2,1,0:T(4,128)S(1)}, u32[]{:S(2)}, u32[]{:S(2)}) collective-permute-start(f32[1,4,256]{2,1,0:T(4,128)S(1)} %get-tuple-element.452), channel_id=1, source_target_pairs={{8,0},{16,8},{24,16},{32,24},{40,32},{48,40},{56,48},{64,56},{72,6... | collective-permute-start | bytes 12296 | tf_op jit(solution)/shard_map/ppermute | solution.py:29
where the time goes:
time: 427 us; the launch traced here: 421 us
  local copies, waits for them, and re-layouts  158 us (37%)
  blocking collectives  149 us (35%)
  other arithmetic  76.9 us (18%)
  matrix products  23.5 us (6%)
  starting transfers between devices  12.8 us (3%)
    psum x1, blocking collectives, local(): query_feat = lax.psum(term, ('frame', 'tile')).astype(jnp.bfloat16)  93 us
    gather x1, local copies, waits for them, and re-layouts, local(): picked = features[local_frame, local_pix].astype(jnp.float32)  79.7 us
    exp x8, local copies, waits for them, and re-layouts, one_block(): jnp.exp(scores - peak[:, None]).reshape(query_block.shape[0], rows_here, W)  72.5 us
    all_gather x4, blocking collectives, merged_2(): everything = jax.tree.map(lambda part: lax.all_gather(part, axis), array)  56.2 us
    reduce_sum x8, other arithmetic, one_block(): return (peak, jnp.sum(row_sum, axis=1), sum_x, sum_y)  35.3 us
    reduce_sum x8, other arithmetic, one_block(): row_sum = jnp.sum(expo, axis=2)  35.2 us
    dot_general x8, matrix products, one_block(): jnp.einsum('qc,pc->qp', query_block, frame_feat, preferred_element_type=j...  21 us
    ppermute x1, starting transfers between devices, with_halo(): after = lax.ppermute(initial, axis, down)  8.95 us
  transfers between devices with their start and end apart: 2, of which 0 were waited for; matrix products, arithmetic and copies ran while one was open for 0% of the time, Pallas kernels for 0%

commit v1 on v0

v1 whole, which is shorter than its diff:
```python
import functools
import math

import jax
import jax.numpy as jnp
from jax import lax
from jax.experimental import pallas as pl
from jax.experimental.pallas import tpu as pltpu
from jax.sharding import PartitionSpec as P

W = 480
LOG2E = math.log2(math.e)
HIGHEST = lax.Precision.HIGHEST
BOTH = ("frame", "tile")


def mesh_groups():
    plane = [[x * 8 + zh * 4 + y for x in range(4) for y in range(4)] for zh in range(2)]
    column = [
        [(x * 8 + zh * 4 + y) * 8 + zl * 2 + c for zh in range(2) for zl in range(4)]
        for x in range(4)
        for y in range(4)
        for c in range(2)
    ]
    return plane, column


def pick_kernel(rows_here, qf_ref, qr_ref, qc_ref, feat_ref, keep_ref, send_ref, vm, sm, slots, sem_m, sem):
    frame_idx, tile_idx = lax.axis_index("frame"), lax.axis_index("tile")
    core = tile_idx % 2
    pix_count = rows_here * W
    frame_count = feat_ref.shape[0] // pix_count
    half = keep_ref.shape[0]
    groups = qf_ref.shape[1]
    frame = qf_ref[...] - frame_idx * frame_count
    row = qr_ref[...] - tile_idx * rows_here
    owned = (frame >= 0) & (frame < frame_count) & (row >= 0) & (row < rows_here)
    sets = qf_ref.shape[0]
    vm[0:sets, :] = frame * pix_count + row * W + qc_ref[...]
    bit = lax.broadcasted_iota(jnp.int32, owned.shape, 0)
    word = jnp.sum(jnp.where(owned, jnp.left_shift(1, bit), 0), axis=0, keepdims=True)
    vm[sets : sets + 8, :] = jnp.broadcast_to(word, (8, groups))
    to_scalar = pltpu.make_async_copy(vm, sm, sem_m)
    to_scalar.start()
    keep_ref[...] = jnp.zeros_like(keep_ref)
    send_ref[...] = jnp.zeros_like(send_ref)
    to_scalar.wait()

    def each(visit, count):
        def group(g, count):
            def more(state):
                return state[0] != 0

            def step(state):
                left, count = state
                low = left & -left
                visit((31 - lax.clz(low)) * groups + g, sm[31 - lax.clz(low), g])
                return left & (left - 1), count + 1

            return lax.while_loop(more, step, (sm[sets, g], count))[1]

        return lax.fori_loop(0, groups, group, count)

    def copy(j, pix):
        first = pl.multiple_of((pix // 16) * 16, 16)
        return pltpu.make_async_copy(feat_ref.at[pl.ds(first, 16), :], slots.at[j], sem)

    found = each(lambda j, pix: copy(j, pix).start(), 0)

    def wait(k, carry):
        copy(0, 0).wait()
        return carry

    lax.fori_loop(0, found, wait, 0)
    sub = lax.broadcasted_iota(jnp.int32, (16, feat_ref.shape[1]), 0)

    def place(j, pix):
        block = slots[j].astype(jnp.float32)
        line = jnp.sum(jnp.where(sub == pix % 16, block, 0.0), axis=0, keepdims=True) * 0.0625
        spot = j % half
        at = pl.ds(pl.multiple_of((spot // 16) * 16, 16), 16)

        def put(ref):
            now = ref[at, :].astype(jnp.float32)
            ref[at, :] = jnp.where(sub == spot % 16, line, now).astype(ref.dtype)

        @pl.when(j // half == core)
        def _():
            put(keep_ref)

        @pl.when(j // half != core)
        def _():
            put(send_ref)

    each(place, 0)


def pick(features, query_frame, query_row, query_col, rows_here):
    flat = features.reshape(-1, features.shape[2])
    queries, chan = query_frame.shape[0], features.shape[2]
    lanes = 128
    sets = queries // lanes
    half = jax.ShapeDtypeStruct((queries // 2, chan), features.dtype)
    vmem = pl.BlockSpec(memory_space=pltpu.VMEM)
    return pl.pallas_call(
        functools.partial(pick_kernel, rows_here),
        out_shape=(half, half),
        in_specs=[vmem, vmem, vmem, pl.BlockSpec(memory_space=pl.ANY)],
        out_specs=(vmem, vmem),
        scratch_shapes=[
            pltpu.VMEM((sets + 8, lanes), jnp.int32),
            pltpu.SMEM((sets + 8, lanes), jnp.int32),
            pltpu.VMEM((queries, 16, chan), features.dtype),
            pltpu.SemaphoreType.DMA,
            pltpu.SemaphoreType.DMA,
        ],
        compiler_params=pltpu.CompilerParams(vmem_limit_bytes=40 << 20),
        name="pick",
    )(*[a.reshape(sets, lanes) for a in (query_frame, query_row, query_col)], flat)


BLOCK = 256
PARTS = 5


def score_kernel(rows_here, own_ref, other_ref, feat_ref, out_ref, fbuf, qbuf, s_ref, sems):
    tile_idx = lax.axis_index("tile")
    core = tile_idx % 2
    frames, pix_count = fbuf.shape[0], fbuf.shape[1]
    copies = [pltpu.make_async_copy(feat_ref.at[f], fbuf.at[f], sems.at[f]) for f in range(frames)]
    for c in copies:
        c.start()
    half_blocks = own_ref.shape[0] // BLOCK
    blocks = 2 * half_blocks
    for b in range(half_blocks):
        qbuf[b] = own_ref[b * BLOCK : (b + 1) * BLOCK, :]
        qbuf[half_blocks + b] = other_ref[b * BLOCK : (b + 1) * BLOCK, :]
    steps = frames * blocks
    span = pix_count // PARTS
    cols = W // PARTS
    total_rows = float(rows_here * lax.axis_size("tile"))
    sub = lax.broadcasted_iota(jnp.int32, (8, BLOCK), 0).astype(jnp.float32)
    zero = jnp.zeros((8, BLOCK), jnp.float32)
    low = jnp.full((8, BLOCK), -jnp.inf, jnp.float32)

    def matmul_part(step, part, top):
        at = pl.ds(pl.multiple_of(part * span, span), span)
        scores = lax.dot_general(
            fbuf[step // blocks, at, :],
            qbuf[step % blocks],
            (((1,), (1,)), ((), ())),
            preferred_element_type=jnp.float32,
        )
        s_ref[step % 2, at, :] = scores
        return jnp.maximum(top, jnp.max(scores.reshape(span // 8, 8, BLOCK), axis=0))

    def sum_part(step, part, peak, sums):
        total, sum_x, sum_y = sums
        for k in range(cols // 8):
            col = part * cols + k * 8
            tail, below = None, None
            for r in reversed(range(rows_here)):
                at = pl.ds(pl.multiple_of(r * W + col, 8), 8)
                expo = jnp.exp2((s_ref[step % 2, at, :] - peak) * LOG2E)
                tail = expo if tail is None else tail + expo
                if r > 0:
                    below = tail if below is None else below + tail
            total = total + tail
            sum_y = sum_y + below
            sum_x = sum_x + tail * (sub + jnp.asarray(col).astype(jnp.float32))
        return total, sum_x, sum_y

    def finish(step, peak, sums):
        total, sum_x, sum_y = [jnp.sum(a, axis=0, keepdims=True) for a in sums]
        first_row = (tile_idx * rows_here).astype(jnp.float32)
        b = step % blocks
        where_to = lax.rem(b + core * half_blocks, blocks)
        packed = jnp.concatenate(
            [peak[0:1], total, sum_x * (1.0 / W), (sum_y + first_row * total) * (1.0 / total_rows)], axis=0
        )
        out_ref[where_to, step // blocks] = packed

    def settle(top):
        return jnp.broadcast_to(jnp.max(top, axis=0, keepdims=True), top.shape)

    copies[0].wait()
    peak = settle(lax.fori_loop(0, PARTS, lambda i, t: matmul_part(0, i, t), low))

    def both(step, peak):
        @pl.when(step % blocks == 0)
        def _():
            for f in range(1, frames):
                @pl.when(step // blocks == f)
                def _():
                    copies[f].wait()

        def part(i, state):
            top, sums = state
            return matmul_part(step, i, top), sum_part(step - 1, i, peak, sums)

        top, sums = lax.fori_loop(0, PARTS, part, (low, (zero, zero, zero)))
        finish(step - 1, peak, sums)
        return settle(top)

    peak = lax.fori_loop(1, steps, both, peak)
    sums = lax.fori_loop(0, PARTS, lambda i, s: sum_part(steps - 1, i, peak, s), (zero, zero, zero))
    finish(steps - 1, peak, sums)


def score(own, other, features, rows_here):
    frames, pix_count, chan = features.shape
    blocks = 2 * own.shape[0] // BLOCK
    vmem = pl.BlockSpec(memory_space=pltpu.VMEM)
    return pl.pallas_call(
        functools.partial(score_kernel, rows_here),
        out_shape=jax.ShapeDtypeStruct((blocks, frames, 4, BLOCK), jnp.float32),
        in_specs=[vmem, vmem, pl.BlockSpec(memory_space=pl.ANY)],
        out_specs=vmem,
        scratch_shapes=[
            pltpu.VMEM((frames, pix_count, chan), features.dtype),
            pltpu.VMEM((blocks, BLOCK, chan), features.dtype),
            pltpu.VMEM((2, pix_count, BLOCK), jnp.float32),
            pltpu.SemaphoreType.DMA((frames,)),
        ],
        compiler_params=pltpu.CompilerParams(vmem_limit_bytes=40 << 20),
        name="score",
    )(own, other, features)


def merge_kernel(pixels, parts_ref, inputs_ref, first_ref, last_ref):
    tiles, frames = parts_ref.shape[0], parts_ref.shape[1]
    for f in range(frames):
        parts = [parts_ref[k, f] for k in range(tiles)]
        peak = functools.reduce(jnp.maximum, [p[0:1] for p in parts])
        sums = functools.reduce(jnp.add, [p[1:4] * jnp.exp(p[0:1] - peak) for p in parts])
        total = sums[0:1]
        log_total = jnp.log(total)
        here = jnp.concatenate(
            [sums[1:2] / total, sums[2:3] / total, -log_total, peak + log_total - math.log(pixels)], axis=0
        )
        inputs_ref[f] = here
        if f == 0:
            first_ref[...] = here
        if f == frames - 1:
            last_ref[...] = here


def merge(parts, pixels):
    tiles, frames, stats, share = parts.shape
    vmem = pl.BlockSpec(memory_space=pltpu.VMEM)
    edge = jax.ShapeDtypeStruct((stats, share), jnp.float32)
    return pl.pallas_call(
        functools.partial(merge_kernel, pixels),
        out_shape=(jax.ShapeDtypeStruct((frames, stats, share), jnp.float32), edge, edge),
        in_specs=[vmem],
        out_specs=(vmem, vmem, vmem),
        name="merge",
    )(parts)


def refine_kernel(before_ref, inputs_ref, after_ref, weight_ref, bias_ref, out_weight_ref, out_ref):
    frames, share = inputs_ref.shape[0], inputs_ref.shape[2]
    bias = jnp.transpose(jnp.broadcast_to(bias_ref[...], (share, bias_ref.shape[1])))
    line = [before_ref[...]] + [inputs_ref[f] for f in range(frames)] + [after_ref[...]]
    for f in range(frames):
        acc = bias
        for k in range(3):
            acc = acc + lax.dot_general(
                weight_ref[k],
                line[f + k],
                (((0,), (0,)), ((), ())),
                precision=HIGHEST,
                preferred_element_type=jnp.float32,
            )
        hidden = jax.nn.gelu(acc)
        delta = jnp.dot(out_weight_ref[...], hidden, precision=HIGHEST, preferred_element_type=jnp.float32)
        out_ref[f] = line[f + 1][0:3] + delta


def refine(before, inputs, after, conv_weight, conv_bias, out_weight):
    frames, _, share = inputs.shape
    return pl.pallas_call(
        refine_kernel,
        out_shape=jax.ShapeDtypeStruct((frames, 3, share), jnp.float32),
        in_specs=[pl.BlockSpec(memory_space=pltpu.VMEM)] * 6,
        out_specs=pl.BlockSpec(memory_space=pltpu.VMEM),
        name="refine",
    )(before, inputs, after, conv_weight, conv_bias[None, :], out_weight)


def local(features, query_frame, query_row, query_col, conv_weight, conv_bias, out_weight):
    frame_count, pix_count, chan = features.shape
    rows_here = pix_count // W
    tiles, groups = lax.axis_size("tile"), lax.axis_size("frame")
    plane, column = mesh_groups()
    keep, send = pick(features, query_frame, query_row, query_col, rows_here)
    swap = [(i, i ^ 1) for i in range(tiles)]
    mine = keep + lax.ppermute(send, "tile", swap)
    wide, tall = len(plane[0]), len(column[0])
    rows = mine.shape[0] // wide
    got = lax.all_to_all(mine.reshape(wide, rows, chan), "frame", 0, 0, axis_index_groups=plane)
    piece = jnp.sum(got, axis=0)
    got = lax.all_to_all(jnp.broadcast_to(piece, (tall, rows, chan)), BOTH, 0, 0, axis_index_groups=column)
    piece = jnp.sum(got, axis=0)
    got = lax.all_to_all(jnp.broadcast_to(piece, (wide, rows, chan)), "frame", 0, 0, axis_index_groups=plane)
    own = got.reshape(wide * rows, chan)
    other = lax.ppermute(own, "tile", swap)
    parts = score(own, other, features, rows_here)
    parts = lax.all_to_all(parts, "tile", 0, 0)
    inputs, first, last = merge(parts, rows_here * tiles * W)
    up = [(i, i + 1) for i in range(groups - 1)]
    before = lax.ppermute(last, "frame", up)
    after = lax.ppermute(first, "frame", [(j, i) for i, j in up])
    return refine(before, inputs, after, conv_weight, conv_bias, out_weight)


def solution(mesh):
    in_specs = (P("frame", "tile", None), P(), P(), P(), P(), P(), P())
    out_specs = P("frame", None, "tile")
    return jax.shard_map(local, mesh=mesh, in_specs=in_specs, out_specs=out_specs, check_vma=False)
```

time: 427 us -> 138 us (0.32)
  the two profiles are of different devices: /device:TPU:6 before, /device:TPU:24 now
where the time goes in v1:
time: 138 us; the launch traced here: 136 us
  blocking collectives  56.9 us (41%)
  Pallas kernels  49.3 us (36%)
  waiting for transfers between devices  13.6 us (10%)
  local copies, waits for them, and re-layouts  8.26 us (6%)
  starting transfers between devices  7.41 us (5%)
    pallas_call x1, Pallas kernels, score(): pl.pallas_call(functools.partial(score_kernel, rows_here), out_shape=jax....  37 us
    all_to_all x1, blocking collectives, local(): lax.all_to_all(mine.reshape(wide, rows, chan), 'frame', 0, 0, axis_index_...  17.4 us
    all_to_all x1, blocking collectives, local(): lax.all_to_all(jnp.broadcast_to(piece, (tall, rows, chan)), BOTH, 0, 0, a...  17.2 us
    all_to_all x1, blocking collectives, local(): lax.all_to_all(jnp.broadcast_to(piece, (wide, rows, chan)), 'frame', 0, 0...  13.3 us
    ppermute x1, waiting for transfers between devices, local(): after = lax.ppermute(first, 'frame', [(j, i) for i, j in up])  9.78 us
    all_to_all x1, blocking collectives, local(): parts = lax.all_to_all(parts, 'tile', 0, 0)  8.98 us
    unnamed x14, local copies, waits for them, and re-layouts  6.91 us
    pallas_call x1, Pallas kernels, pick(): pl.pallas_call(functools.partial(pick_kernel, rows_here), out_shape=(half...  6.11 us
  transfers between devices with their start and end apart: 4, of which 3 were waited for; matrix products, arithmetic and copies ran while one was open for 0% of the time, Pallas kernels for 0%

profile of v1, /device:TPU:24, one launch (start us, length us, event | category | flops | bytes accessed | tf_op | source)
XLA Modules:
  0.0 135.7 jit_solution(2491955897515622324)
XLA Ops:
  0.0 0.0 copy-start
  0.0 2.1 %copy-done = bf16[2,3840,256]{2,1,0:T(8,128)(2,1)S(1)} copy-done((bf16[2,3840,256]{2,1,0:T(8,128)(2,1)S(1)}, bf16[2,3840,256]{2,1,0:T(8,128)(2,1)}, u32[]{:S(2)}) %copy-start) | copy-done | bytes 3932184
  2.1 0.0 copy-start.2
  2.1 0.7 copy-done.2
  2.8 0.0 copy-start.3
  2.8 0.7 copy-done.3
  3.5 0.0 copy-start.4
  3.5 0.7 copy-done.4
  4.2 6.1 %pick.1 = (bf16[1024,256]{1,0:T(8,128)(2,1)S(1)}, bf16[1024,256]{1,0:T(8,128)(2,1)S(1)}) custom-call(s32[16,128]{1,0:T(8,128)S(1)} %bitcast.10, s32[16,128]{1,0:T(8,128)S(1)} %bitcast.11, s32[16,128]{1,0:T(8,128)S(1)} %bitcast.12, bf16[7680,256]{1,0:T(8,128)(2,1)S(1)} %bitcast.7), custom_call_target="tpu_custom_call" | custom-call | tf_op jit(solution)/shard_map/pick/pallas_call | solution.py:105
  10.3 0.1 collective-permute-start
  10.4 1.9 %collective-permute-done = bf16[1024,256]{1,0:T(8,128)(2,1)S(1)} collective-permute-done((bf16[1024,256]{1,0:T(8,128)(2,1)S(1)}, bf16[1024,256]{1,0:T(8,128)(2,1)S(1)}, u32[]{:S(2)}, u32[]{:S(2)}) %collective-permute-start) | collective-permute-done | bytes 524320 | tf_op jit(solution)/shard_map/ppermute | solution.py:298
  12.3 0.1 add.3
  12.5 17.4 %all_to_all.20 = bf16[16,64,256]{2,1,0:T(8,128)(2,1)S(1)} all-to-all(bf16[16,64,256]{2,1,0:T(8,128)(2,1)S(1)} %bitcast.13), channel_id=1, replica_groups={{0,8,16,24,64,72,80,88,128,136,144,152,192,200,208,216},{32,40,48,56,96..., dimensions={0} | all-to-all | bytes 1048576 | tf_op jit(solution)/shard_map/all_to_all | solution.py:301
  29.8 0.1 reduce_sum.24
  29.9 17.2 %all_to_all.21 = bf16[8,64,256]{2,1,0:T(8,128)(2,1)S(1)} all-to-all(bf16[8,64,256]{2,1,0:T(8,128)(2,1)S(1)} %broadcast_in_dim.9), channel_id=1, replica_groups={{0,2,4,6,32,34,36,38},{1,3,5,7,33,35,37,39},{8,10,12,14,40,42,44,46},{9..., dimensions={0} | all-to-all | bytes 524288 | tf_op jit(solution)/shard_map/all_to_all | solution.py:303
  47.2 13.3 %all_to_all.22 = bf16[16,64,256]{2,1,0:T(8,128)(2,1)S(1)} all-to-all(bf16[16,64,256]{2,1,0:T(8,128)(2,1)S(1)} %broadcast_in_dim.10), channel_id=1, replica_groups={{0,8,16,24,64,72,80,88,128,136,144,152,192,200,208,216},{32,40,48,56,96..., dimensions={0} | all-to-all | bytes 1048576 | tf_op jit(solution)/shard_map/all_to_all | solution.py:305
  60.5 0.0 collective-permute-start.1
  60.5 1.9 %collective-permute-done.1.other_ref = bf16[1024,256]{1,0:T(8,128)(2,1)S(1)} collective-permute-done((bf16[1024,256]{1,0:T(8,128)(2,1)S(1)}, bf16[1024,256]{1,0:T(8,128)(2,1)S(1)}, u32[]{:S(2)}, u32[]{:S(2)}) %collective-permute-start.1) | collective-permute-done | bytes 524320 | tf_op jit(solution)/shard_map/ppermute | solution.py:307
  62.5 0.0 copy-start.1
  62.5 2.1 %copy-done.1 = bf16[2,3840,256]{2,1,0:T(8,128)(2,1)S(1)} copy-done((bf16[2,3840,256]{2,1,0:T(8,128)(2,1)S(1)}, bf16[2,3840,256]{2,1,0:T(8,128)(2,1)}, u32[]{:S(2)}) %copy-start.1) | copy-done | bytes 3932184
  64.6 37.0 %score.1 = f32[8,2,4,256]{3,2,1,0:T(4,128)S(1)} custom-call(bf16[1024,256]{1,0:T(8,128)(2,1)S(1)} %bitcast.9, bf16[1024,256]{1,0:T(8,128)(2,1)S(1)} %collective-permute-done.1.other_ref, bf16[2,3840,256]{2,1,0:T(8,128)(2,1)S(1)} %copy-done.1), custom_call_target="tpu_custom_call" | custom-call | tf_op jit(solution)/shard_map/score/pallas_call | solution.py:214
  101.6 9.0 %all_to_all.23.parts_ref = f32[8,2,4,256]{3,2,1,0:T(4,128)} all-to-all(f32[8,2,4,256]{3,2,1,0:T(4,128)S(1)} %score.1), channel_id=1, replica_groups=mesh['frame'=32,'tile'=8] {'tile'}, dimensions={0} | all-to-all | bytes 131072 | tf_op jit(solution)/shard_map/all_to_all | solution.py:309
  110.6 1.5 %merge.1 = (f32[2,4,256]{2,1,0:T(4,128)}, f32[4,256]{1,0:T(4,128)}, f32[4,256]{1,0:T(4,128)}) custom-call(f32[8,2,4,256]{3,2,1,0:T(4,128)} %all_to_all.23.parts_ref), custom_call_target="tpu_custom_call" | custom-call | tf_op jit(solution)/shard_map/merge/pallas_call | solution.py:252
  112.1 5.4 %collective-permute-start.2 = (f32[4,256]{1,0:T(4,128)}, f32[4,256]{1,0:T(4,128)S(1)}, u32[]{:S(2)}, u32[]{:S(2)}) collective-permute-start(f32[4,256]{1,0:T(4,128)} %get-tuple-element.12), channel_id=1, source_target_pairs={{0,8},{8,16},{16,24},{24,32},{32,40},{40,48},{48,56},{56,64},{64,7... | collective-permute-start | bytes 12296 | tf_op jit(solution)/shard_map/ppermute | solution.py:312
  117.5 1.9 %collective-permute-start.3 = (f32[4,256]{1,0:T(4,128)}, f32[4,256]{1,0:T(4,128)S(1)}, u32[]{:S(2)}, u32[]{:S(2)}) collective-permute-start(f32[4,256]{1,0:T(4,128)} %get-tuple-element.14), channel_id=1, source_target_pairs={{8,0},{16,8},{24,16},{32,24},{40,32},{48,40},{56,48},{64,56},{72,6... | collective-permute-start | bytes 12296 | tf_op jit(solution)/shard_map/ppermute | solution.py:313
  119.4 0.0 collective-permute-done.2.before_ref
  119.4 0.0 copy-start.5
  119.4 9.8 %collective-permute-done.3.after_ref = f32[4,256]{1,0:T(4,128)S(1)} collective-permute-done((f32[4,256]{1,0:T(4,128)}, f32[4,256]{1,0:T(4,128)S(1)}, u32[]{:S(2)}, u32[]{:S(2)}) %collective-permute-start.3) | collective-permute-done | bytes 4128 | tf_op jit(solution)/shard_map/ppermute | solution.py:313
  129.2 0.0 copy-start.6
  129.2 0.0 copy-done.5
  129.2 0.6 copy-done.6
  129.8 4.6 %refine.1 = f32[2,3,256]{2,1,0:T(4,128)} custom-call(f32[4,256]{1,0:T(4,128)} %copy-done.5, f32[2,4,256]{2,1,0:T(4,128)} %get-tuple-element.13.inputs_ref, f32[4,256]{1,0:T(4,128)} %copy-done.6, f32[3,4,256]{2,1,0:T(4,128)} %weight_ref.1, f32[1,256]{1,0:T(1,128)} %bitcast.14, f32[3,256]{1,0:T(4,128)} %out_weight_ref.1), custom_call_target="tpu_custom_call" | custom-call | tf_op jit(solution)/shard_map/refine/pallas_call | solution.py:282
  134.4 1.3 copy.9
  (3 shorter events, 0.1 us)
Async XLA Ops:
  0.0 2.1 %copy-start = (bf16[2,3840,256]{2,1,0:T(8,128)(2,1)S(1)}, bf16[2,3840,256]{2,1,0:T(8,128)(2,1)}, u32[]{:S(2)}) copy-start(bf16[2,3840,256]{2,1,0:T(8,128)(2,1)} %feat_ref.1) | copy-start | bytes 11796484
  2.1 0.7 copy-start.2
  2.8 0.7 copy-start.3
  3.5 0.7 copy-start.4
  10.3 2.0 %collective-permute-start = (bf16[1024,256]{1,0:T(8,128)(2,1)S(1)}, bf16[1024,256]{1,0:T(8,128)(2,1)S(1)}, u32[]{:S(2)}, u32[]{:S(2)}) collective-permute-start(bf16[1024,256]{1,0:T(8,128)(2,1)S(1)} %get-tuple-element.11), channel_id=1, source_target_pairs={{0,1},{1,0},{2,3},{3,2},{4,5},{5,4},{6,7},{7,6},{8,9},{9,8},{10,11... | collective-permute-start | bytes 1572872 | tf_op jit(solution)/shard_map/ppermute | solution.py:298
  60.5 1.9 %collective-permute-start.1 = (bf16[1024,256]{1,0:T(8,128)(2,1)S(1)}, bf16[1024,256]{1,0:T(8,128)(2,1)S(1)}, u32[]{:S(2)}, u32[]{:S(2)}) collective-permute-start(bf16[1024,256]{1,0:T(8,128)(2,1)S(1)} %bitcast.8), channel_id=1, source_target_pairs={{0,1},{1,0},{2,3},{3,2},{4,5},{5,4},{6,7},{7,6},{8,9},{9,8},{10,11... | collective-permute-start | bytes 1572872 | tf_op jit(solution)/shard_map/ppermute | solution.py:307
  62.5 2.1 %copy-start.1 = (bf16[2,3840,256]{2,1,0:T(8,128)(2,1)S(1)}, bf16[2,3840,256]{2,1,0:T(8,128)(2,1)}, u32[]{:S(2)}) copy-start(bf16[2,3840,256]{2,1,0:T(8,128)(2,1)} %feat_ref.1) | copy-start | bytes 11796484
  112.1 7.3 %collective-permute-start.2 = (f32[4,256]{1,0:T(4,128)}, f32[4,256]{1,0:T(4,128)S(1)}, u32[]{:S(2)}, u32[]{:S(2)}) collective-permute-start(f32[4,256]{1,0:T(4,128)} %get-tuple-element.12), channel_id=1, source_target_pairs={{0,8},{8,16},{16,24},{24,32},{32,40},{40,48},{48,56},{56,64},{64,7... | collective-permute-start | bytes 12296 | tf_op jit(solution)/shard_map/ppermute | solution.py:312
  117.5 11.7 %collective-permute-start.3 = (f32[4,256]{1,0:T(4,128)}, f32[4,256]{1,0:T(4,128)S(1)}, u32[]{:S(2)}, u32[]{:S(2)}) collective-permute-start(f32[4,256]{1,0:T(4,128)} %get-tuple-element.14), channel_id=1, source_target_pairs={{8,0},{16,8},{24,16},{32,24},{40,32},{48,40},{56,48},{64,56},{72,6... | collective-permute-start | bytes 12296 | tf_op jit(solution)/shard_map/ppermute | solution.py:313
  119.4 9.8 %copy-start.5 = (f32[4,256]{1,0:T(4,128)}, f32[4,256]{1,0:T(4,128)S(1)}, u32[]{:S(2)}) copy-start(f32[4,256]{1,0:T(4,128)S(1)} %collective-permute-done.2.before_ref) | copy-start | bytes 12292
  129.2 0.6 copy-start.6

commit v2 on v1

v2 whole, which is shorter than its diff:
```python
import functools
import math

import jax
import jax.numpy as jnp
from jax import lax
from jax.experimental import pallas as pl
from jax.experimental.pallas import tpu as pltpu
from jax.sharding import PartitionSpec as P

W = 480
LOG2E = math.log2(math.e)
BOTH = ("frame", "tile")


def mesh_groups():
    plane = [[x * 8 + zh * 4 + y for x in range(4) for y in range(4)] for zh in range(2)]
    column = [
        [(x * 8 + zh * 4 + y) * 8 + zl * 2 + c for zh in range(2) for zl in range(4)]
        for x in range(4)
        for y in range(4)
        for c in range(2)
    ]
    return plane, column


def pick_kernel(rows_here, qf_ref, qr_ref, qc_ref, feat_ref, keep_ref, send_ref, idx, vm, sm, found_at, slots, wide, lines, sems, sem):
    frame_idx, tile_idx = lax.axis_index("frame"), lax.axis_index("tile")
    core = tile_idx % 2
    loads = [
        pltpu.make_async_copy(ref, idx.at[k], sems.at[k]) for k, ref in enumerate((qf_ref, qr_ref, qc_ref))
    ]
    for load in loads:
        load.start()
    pix_count = rows_here * W
    frame_count = feat_ref.shape[0] // pix_count
    half = keep_ref.shape[0]
    sets, groups = idx.shape[1], idx.shape[2]
    lines[...] = jnp.zeros_like(lines)
    for load in loads:
        load.wait()
    frame = idx[0] - frame_idx * frame_count
    row = idx[1] - tile_idx * rows_here
    owned = (frame >= 0) & (frame < frame_count) & (row >= 0) & (row < rows_here)
    vm[0:sets, :] = frame * pix_count + row * W + idx[2]
    bit = lax.broadcasted_iota(jnp.int32, owned.shape, 0)
    word = jnp.sum(jnp.where(owned, jnp.left_shift(1, bit), 0), axis=0, keepdims=True)
    vm[sets : sets + 8, :] = jnp.broadcast_to(word, (8, groups))
    to_scalar = pltpu.make_async_copy(vm, sm, sems.at[3])
    to_scalar.start()
    to_scalar.wait()

    def copy(k, pix):
        first = pl.multiple_of((pix // 16) * 16, 16)
        return pltpu.make_async_copy(feat_ref.at[pl.ds(first, 16), :], slots.at[k], sem)

    def group(g, count):
        def step(state):
            left, count = state
            i = 31 - lax.clz(left & -left)
            pix = sm[i, g]
            copy(count, pix).start()
            found_at[0, count] = i * groups + g
            found_at[1, count] = pix % 16
            return left & (left - 1), count + 1

        return lax.while_loop(lambda state: state[0] != 0, step, (sm[sets, g], count))[1]

    found = lax.fori_loop(0, groups, group, 0)

    def wait(k, carry):
        copy(0, 0).wait()
        return carry

    lax.fori_loop(0, found, wait, 0)

    def place(k, carry):
        wide[k % 8] = slots[k].astype(jnp.float32)
        lines[pl.ds(found_at[0, k], 1), :] = wide[k % 8, pl.ds(found_at[1, k], 1), :]
        return carry

    lax.fori_loop(0, found, place, 0)
    mine = pl.multiple_of(core * half, half)
    theirs = pl.multiple_of((1 - core) * half, half)
    keep_ref[...] = (lines[pl.ds(mine, half), :] * 0.0625).astype(keep_ref.dtype)
    send_ref[...] = (lines[pl.ds(theirs, half), :] * 0.0625).astype(send_ref.dtype)


def pick(features, query_frame, query_row, query_col, rows_here):
    flat = features.reshape(-1, features.shape[2])
    queries, chan = query_frame.shape[0], features.shape[2]
    lanes = 128
    sets = queries // lanes
    half = jax.ShapeDtypeStruct((queries // 2, chan), features.dtype)
    vmem = pl.BlockSpec(memory_space=pltpu.VMEM)
    hbm = pl.BlockSpec(memory_space=pltpu.MemorySpace.HBM)
    return pl.pallas_call(
        functools.partial(pick_kernel, rows_here),
        out_shape=(half, half),
        in_specs=[hbm, hbm, hbm, hbm],
        out_specs=(vmem, vmem),
        scratch_shapes=[
            pltpu.VMEM((3, sets, lanes), jnp.int32),
            pltpu.VMEM((sets + 8, lanes), jnp.int32),
            pltpu.SMEM((sets + 8, lanes), jnp.int32),
            pltpu.SMEM((2, queries), jnp.int32),
            pltpu.VMEM((queries, 16, chan), features.dtype),
            pltpu.VMEM((8, 16, chan), jnp.float32),
            pltpu.VMEM((queries, chan), jnp.float32),
            pltpu.SemaphoreType.DMA((4,)),
            pltpu.SemaphoreType.DMA,
        ],
        compiler_params=pltpu.CompilerParams(vmem_limit_bytes=28 << 20),
        name="pick",
    )(*[a.reshape(sets, lanes) for a in (query_frame, query_row, query_col)], flat)


BLOCK = 256
PARTS = 5
UNITS = 2


def score_kernel(own_ref, other_ref, feat_ref, out_ref, fbuf, even, odd, sems):
    tile_idx = lax.axis_index("tile")
    core = tile_idx % 2
    frames, rows_here = fbuf.shape[0], fbuf.shape[1]
    cols = W // PARTS
    loads = [
        [
            pltpu.make_async_copy(
                feat_ref.at[f, :, pl.ds(i * cols, cols), :], fbuf.at[f, :, pl.ds(i * cols, cols), :], sems.at[f, i]
            )
            for i in range(PARTS)
        ]
        for f in range(frames)
    ]
    for load in loads[0] + loads[1]:
        load.start()
    half_blocks = own_ref.shape[0] // BLOCK
    blocks = 2 * half_blocks
    pairs = blocks // UNITS
    steps = frames * pairs
    total_rows = float(rows_here * lax.axis_size("tile"))
    first_row = (tile_idx * rows_here).astype(jnp.float32)
    sub = lax.broadcasted_iota(jnp.int32, (8, BLOCK), 0).astype(jnp.float32)
    zero = jnp.zeros((8, BLOCK), jnp.float32)
    low = jnp.full((8, BLOCK), -jnp.inf, jnp.float32)

    def stage(pair):
        for m in range(UNITS):
            ref, k = (own_ref, pair * UNITS + m) if pair * UNITS < half_blocks else (other_ref, pair * UNITS + m - half_blocks)
            pltpu.matmul_push_rhs(ref[k * BLOCK : (k + 1) * BLOCK, :], 0, m, transpose=True)

    def run(*accs):
        def feed(f, part, staged):
            for r in range(rows_here):
                lhs = fbuf[f, r, pl.ds(pl.multiple_of(part * cols, 16), cols), :]
                for m in range(UNITS):
                    pltpu.matmul_acc_lhs(accs[m * rows_here + r], lhs, load_staged_rhs=staged if r == 0 else None)

        def drain(kept, part, tops):
            tops = list(tops)
            for r in range(rows_here):
                for m in range(UNITS):
                    scores = pltpu.matmul_pop(accs[m * rows_here + r])
                    kept[part, m, r * cols : (r + 1) * cols, :] = scores
                    tops[m] = jnp.maximum(tops[m], jnp.max(scores.reshape(cols // 8, 8, BLOCK), axis=0))
            return tuple(tops)

        def weigh(kept, part, peaks, sums):
            out = []
            start = jnp.asarray(part * cols).astype(jnp.float32)
            for m in range(UNITS):
                total, sum_x, sum_y = sums[m]
                here, across = None, None
                for k in range(cols // 8):
                    tail, below = None, None
                    for r in reversed(range(rows_here)):
                        at = r * cols + k * 8
                        expo = jnp.exp2((kept[part, m, at : at + 8, :] - peaks[m]) * LOG2E)
                        tail = expo if tail is None else tail + expo
                        if r > 0:
                            below = tail if below is None else below + tail
                    sum_y = sum_y + below
                    here = tail if here is None else here + tail
                    if k > 0:
                        shifted = tail * float(k * 8)
                        across = shifted if across is None else across + shifted
                out.append((total + here, sum_x + (across + here * (sub + start)), sum_y))
            return tuple(out)

        def settle(tops):
            return tuple(jnp.broadcast_to(jnp.max(t, axis=0, keepdims=True), t.shape) for t in tops)

        def finish(step, peaks, sums):
            f, pair = divmod(step, pairs)
            for m in range(UNITS):
                total, sum_x, sum_y = [jnp.sum(a, axis=0, keepdims=True) for a in sums[m]]
                where_to = lax.rem(pair * UNITS + m + core * half_blocks, blocks)
                out_ref[where_to, f] = jnp.concatenate(
                    [peaks[m][0:1], total, sum_x * (1.0 / W), (sum_y + first_row * total) * (1.0 / total_rows)], axis=0
                )

        stage(0)
        peaks = None
        for step in range(steps + 1):
            f = step // pairs
            new, old = (even, odd) if step % 2 == 0 else (odd, even)

            def part_of(i, state, staged=None):
                tops, sums = state
                if step < steps:
                    if step == 0:
                        pltpu.make_async_copy(
                            feat_ref.at[0, :, pl.ds(0, cols), :], fbuf.at[0, :, pl.ds(0, cols), :], sems.at[0, i]
                        ).wait()
                    feed(f, i, staged)
                if step > 0:
                    sums = weigh(old, i, peaks, sums)
                if step < steps:
                    tops = drain(new, i, tops)
                return tops, sums

            if step == pairs:
                for load in loads[1]:
                    load.wait()
            state = ((low,) * UNITS, ((zero, zero, zero),) * UNITS)
            state = part_of(0, state, 0)
            if step + 1 < steps:
                stage((step + 1) % pairs)
            tops, sums = lax.fori_loop(1, PARTS, part_of, state)
            if step > 0:
                finish(step - 1, peaks, sums)
            if step < steps:
                peaks = settle(tops)

    pl.run_scoped(
        run, *[pltpu.ACC(m)((cols, BLOCK), jnp.float32) for m in range(UNITS) for _ in range(rows_here)]
    )


def score(own, other, features, rows_here):
    frames, pix_count, chan = features.shape
    blocks = 2 * own.shape[0] // BLOCK
    vmem = pl.BlockSpec(memory_space=pltpu.VMEM)
    kept = pltpu.VMEM((PARTS, UNITS, pix_count // PARTS, BLOCK), jnp.float32)
    return pl.pallas_call(
        score_kernel,
        out_shape=jax.ShapeDtypeStruct((blocks, frames, 4, BLOCK), jnp.float32),
        in_specs=[vmem, vmem, pl.BlockSpec(memory_space=pltpu.MemorySpace.HBM)],
        out_specs=vmem,
        scratch_shapes=[
            pltpu.VMEM((frames, rows_here, W, chan), features.dtype),
            kept,
            kept,
            pltpu.SemaphoreType.DMA((frames, PARTS)),
        ],
        compiler_params=pltpu.CompilerParams(vmem_limit_bytes=28 << 20),
        name="score",
    )(own, other, features.reshape(frames, rows_here, W, chan))


def merge_kernel(pixels, parts_ref, inputs_ref, first_ref, last_ref):
    tiles, frames = parts_ref.shape[0], parts_ref.shape[1]
    for f in range(frames):
        parts = [parts_ref[k, f] for k in range(tiles)]
        peak = functools.reduce(jnp.maximum, [p[0:1] for p in parts])
        sums = functools.reduce(jnp.add, [p[1:4] * jnp.exp(p[0:1] - peak) for p in parts])
        total = sums[0:1]
        log_total = jnp.log(total)
        here = jnp.concatenate(
            [sums[1:2] / total, sums[2:3] / total, -log_total, peak + log_total - math.log(pixels)], axis=0
        )
        inputs_ref[f] = here
        if f == 0:
            first_ref[...] = here
        if f == frames - 1:
            last_ref[...] = here


def merge(parts, pixels):
    tiles, frames, stats, share = parts.shape
    vmem = pl.BlockSpec(memory_space=pltpu.VMEM)
    edge = jax.ShapeDtypeStruct((stats, share), jnp.float32)
    return pl.pallas_call(
        functools.partial(merge_kernel, pixels),
        out_shape=(jax.ShapeDtypeStruct((frames, stats, share), jnp.float32), edge, edge),
        in_specs=[vmem],
        out_specs=(vmem, vmem, vmem),
        name="merge",
    )(parts)


def split(array, count):
    parts = []
    for _ in range(count):
        parts.append(array.astype(jnp.bfloat16))
        array = array - parts[-1].astype(jnp.float32)
    return parts


MEET = ((0, 0), (0, 1), (1, 0), (1, 1), (0, 2), (2, 0))
DEPTH = 128


def prepare_kernel(weight_ref, bias_ref, out_weight_ref, taps_ref, last_ref):
    taps, stats, hidden = weight_ref.shape
    rows = jnp.concatenate([weight_ref[k] for k in range(taps)] + [jnp.broadcast_to(bias_ref[...], (4, hidden))], axis=0)
    thirds = [p.astype(jnp.float32) for p in split(rows, 3)]
    stacked = jnp.concatenate([thirds[i] for i, _ in MEET], axis=0)
    filler = jnp.zeros((DEPTH - stacked.shape[0], hidden), jnp.float32)
    taps_ref[...] = jnp.transpose(jnp.concatenate([stacked, filler], axis=0)).astype(jnp.bfloat16)
    thirds = [p.astype(jnp.float32) for p in split(out_weight_ref[...], 2)]
    filler = jnp.zeros((8 - out_weight_ref.shape[0], hidden), jnp.float32)
    last_ref[...] = jnp.concatenate([thirds[0], filler, thirds[1], filler], axis=0).astype(jnp.bfloat16)


def prepare(conv_weight, conv_bias, out_weight):
    hidden = conv_bias.shape[0]
    vmem = pl.BlockSpec(memory_space=pltpu.VMEM)
    return pl.pallas_call(
        prepare_kernel,
        out_shape=(
            jax.ShapeDtypeStruct((hidden, DEPTH), jnp.bfloat16),
            jax.ShapeDtypeStruct((16, hidden), jnp.bfloat16),
        ),
        in_specs=[vmem] * 3,
        out_specs=(vmem, vmem),
        cost_estimate=pl.CostEstimate(flops=200000, bytes_accessed=200000, transcendentals=0),
        name="prepare",
    )(conv_weight, conv_bias[None, :], out_weight)


def refine_kernel(before_ref, inputs_ref, after_ref, taps_ref, last_ref, out_ref, held, sem):
    frames, share = inputs_ref.shape[0], inputs_ref.shape[2]
    line = [before_ref[...]] + [inputs_ref[f] for f in range(frames)] + [after_ref[...]]
    unit = jnp.where(lax.broadcasted_iota(jnp.int32, (4, share), 0) == 0, 1.0, 0.0)
    right = []
    for f in range(frames):
        rows = jnp.concatenate([line[f + k] for k in range(3)] + [unit], axis=0)
        thirds = [p.astype(jnp.float32) for p in split(rows, 3)]
        stacked = jnp.concatenate([thirds[j] for _, j in MEET], axis=0)
        filler = jnp.zeros((DEPTH - stacked.shape[0], share), jnp.float32)
        right.append(jnp.concatenate([stacked, filler], axis=0).astype(jnp.bfloat16))
    for f in range(frames):
        acc = jnp.dot(taps_ref[...], right[f], preferred_element_type=jnp.float32)
        hidden = jax.nn.gelu(acc)
        high, rest = split(hidden, 2)
        first = jnp.dot(last_ref[...], high, preferred_element_type=jnp.float32)
        second = jnp.dot(last_ref[...], rest, preferred_element_type=jnp.float32)
        delta = first[0:3] + (first[8:11] + second[0:3])
        held[f] = line[f + 1][0:3] + delta
    store = pltpu.make_async_copy(held, out_ref, sem)
    store.start()
    store.wait()


def refine(before, inputs, after, taps, last):
    frames, _, share = inputs.shape
    return pl.pallas_call(
        refine_kernel,
        out_shape=jax.ShapeDtypeStruct((frames, 3, share), jnp.float32),
        in_specs=[pl.BlockSpec(memory_space=pltpu.VMEM)] * 5,
        out_specs=pl.BlockSpec(memory_space=pltpu.MemorySpace.HBM),
        scratch_shapes=[pltpu.VMEM((frames, 3, share), jnp.float32), pltpu.SemaphoreType.DMA],
        name="refine",
    )(before, inputs, after, taps, last)


def local(features, query_frame, query_row, query_col, conv_weight, conv_bias, out_weight):
    frame_count, pix_count, chan = features.shape
    rows_here = pix_count // W
    tiles, groups = lax.axis_size("tile"), lax.axis_size("frame")
    plane, column = mesh_groups()
    keep, send = pick(features, query_frame, query_row, query_col, rows_here)
    swap = [(i, i ^ 1) for i in range(tiles)]
    mine = keep + lax.ppermute(send, "tile", swap)
    wide, tall = len(plane[0]), len(column[0])
    rows = mine.shape[0] // wide
    got = lax.all_to_all(mine.reshape(wide, rows, chan), "frame", 0, 0, axis_index_groups=plane)
    piece = jnp.sum(got, axis=0)
    got = lax.all_to_all(jnp.broadcast_to(piece, (tall, rows, chan)), BOTH, 0, 0, axis_index_groups=column)
    piece = jnp.sum(got, axis=0)
    got = lax.all_to_all(jnp.broadcast_to(piece, (wide, rows, chan)), "frame", 0, 0, axis_index_groups=plane)
    own = got.reshape(wide * rows, chan)
    other = lax.ppermute(own, "tile", swap)
    parts = score(own, other, features, rows_here)
    parts = lax.all_to_all(parts, "tile", 0, 0)
    inputs, first, last = merge(parts, rows_here * tiles * W)
    up = [(i, i + 1) for i in range(groups - 1)]
    before = lax.ppermute(last, "frame", up)
    after = lax.ppermute(first, "frame", [(j, i) for i, j in up])
    taps, last_weight = prepare(conv_weight, conv_bias, out_weight)
    return refine(before, inputs, after, taps, last_weight)


def solution(mesh):
    in_specs = (P("frame", "tile", None), P(), P(), P(), P(), P(), P())
    out_specs = P("frame", None, "tile")
    return jax.shard_map(local, mesh=mesh, in_specs=in_specs, out_specs=out_specs, check_vma=False)
```

time: 138 us -> 116 us (0.84); the launches traced: 136 us -> 116 us
  Pallas kernels: 49.3 us -> 28.1 us
  blocking collectives: 56.9 us -> 59.3 us
  waiting for transfers between devices: 13.6 us -> 12.1 us
    pallas_call x1 -> x2, Pallas kernels: 37 us -> 21.5 us  [the longest x1 20 us: score(): pl.pallas_call(score_kernel, out_shape=jax.ShapeDtypeStruct((blocks, fram...]
    all_to_all x1, blocking collectives: 17.2 us -> 20.2 us  [local(): lax.all_to_all(jnp.broadcast_to(piece, (tall, rows, chan)), BOTH, 0, 0, a...]
    pallas_call x1, Pallas kernels: 6.11 us -> 3.17 us  [pick(): pl.pallas_call(functools.partial(pick_kernel, rows_here), out_shape=(half...]
    pallas_call x1, Pallas kernels: 4.65 us -> 1.94 us  [refine(): pl.pallas_call(refine_kernel, out_shape=jax.ShapeDtypeStruct((frames, 3,...]
    ppermute x1, waiting for transfers between devices: 9.78 us -> 8.33 us  [local(): after = lax.ppermute(first, 'frame', [(j, i) for i, j in up])]
  transfers between devices with their start and end apart: 4 -> 4, of which waited for: 3 -> 3; matrix products, arithmetic and copies ran while one was open for 0% -> 0% of each run, Pallas kernels for 0% -> 1%
where the time goes in v2:
time: 116 us
  blocking collectives  59.3 us (51%)
  Pallas kernels  28.1 us (24%)
  waiting for transfers between devices  12.1 us (10%)
  local copies, waits for them, and re-layouts  8.26 us (7%)
  starting transfers between devices  7.43 us (6%)
    all_to_all x1, blocking collectives, local(): lax.all_to_all(jnp.broadcast_to(piece, (tall, rows, chan)), BOTH, 0, 0, a...  20.2 us
    pallas_call x1, Pallas kernels, score(): pl.pallas_call(score_kernel, out_shape=jax.ShapeDtypeStruct((blocks, fram...  20 us
    all_to_all x1, blocking collectives, local(): lax.all_to_all(mine.reshape(wide, rows, chan), 'frame', 0, 0, axis_index_...  16.8 us
    all_to_all x1, blocking collectives, local(): lax.all_to_all(jnp.broadcast_to(piece, (wide, rows, chan)), 'frame', 0, 0...  13.3 us
    all_to_all x1, blocking collectives, local(): parts = lax.all_to_all(parts, 'tile', 0, 0)  8.98 us
    ppermute x1, waiting for transfers between devices, local(): after = lax.ppermute(first, 'frame', [(j, i) for i, j in up])  8.33 us
    unnamed x14, local copies, waits for them, and re-layouts  6.91 us
    ppermute x1, starting transfers between devices, local(): before = lax.ppermute(last, 'frame', up)  5.42 us
  transfers between devices with their start and end apart: 4, of which 3 were waited for; matrix products, arithmetic and copies ran while one was open for 0% of the time, Pallas kernels for 1%

profile of v2, /device:TPU:24, one launch (start us, length us, event | category | flops | bytes accessed | tf_op | source)
XLA Modules:
  0.0 115.5 jit_solution(5165356967960511462)
XLA Ops:
  0.0 0.0 copy-start
  0.0 2.1 %copy-done = bf16[2,3840,256]{2,1,0:T(8,128)(2,1)S(1)} copy-done((bf16[2,3840,256]{2,1,0:T(8,128)(2,1)S(1)}, bf16[2,3840,256]{2,1,0:T(8,128)(2,1)}, u32[]{:S(2)}) %copy-start) | copy-done | bytes 3932184
  2.1 0.0 copy-start.2
  2.1 0.7 copy-done.2
  2.8 0.0 copy-start.3
  2.8 0.7 copy-done.3
  3.5 0.0 copy-start.4
  3.5 0.7 copy-done.4
  4.2 3.2 %pick.1 = (bf16[1024,256]{1,0:T(8,128)(2,1)S(1)}, bf16[1024,256]{1,0:T(8,128)(2,1)S(1)}) custom-call(s32[16,128]{1,0:T(8,128)S(1)} %bitcast.12, s32[16,128]{1,0:T(8,128)S(1)} %bitcast.13, s32[16,128]{1,0:T(8,128)S(1)} %bitcast.14, bf16[7680,256]{1,0:T(8,128)(2,1)S(1)} %bitcast.8), custom_call_target="tpu_custom_call" | custom-call | tf_op jit(solution)/shard_map/pick/pallas_call | solution.py:97
  7.4 0.1 collective-permute-start
  7.5 1.9 %collective-permute-done = bf16[1024,256]{1,0:T(8,128)(2,1)S(1)} collective-permute-done((bf16[1024,256]{1,0:T(8,128)(2,1)S(1)}, bf16[1024,256]{1,0:T(8,128)(2,1)S(1)}, u32[]{:S(2)}, u32[]{:S(2)}) %collective-permute-start) | collective-permute-done | bytes 524320 | tf_op jit(solution)/shard_map/ppermute | solution.py:377
  9.4 0.1 add.3
  9.5 16.8 %all_to_all.20 = bf16[16,64,256]{2,1,0:T(8,128)(2,1)S(1)} all-to-all(bf16[16,64,256]{2,1,0:T(8,128)(2,1)S(1)} %bitcast.15), channel_id=1, replica_groups={{0,8,16,24,64,72,80,88,128,136,144,152,192,200,208,216},{32,40,48,56,96..., dimensions={0} | all-to-all | bytes 1048576 | tf_op jit(solution)/shard_map/all_to_all | solution.py:380
  26.3 0.1 reduce_sum.24
  26.4 20.2 %all_to_all.21 = bf16[8,64,256]{2,1,0:T(8,128)(2,1)S(1)} all-to-all(bf16[8,64,256]{2,1,0:T(8,128)(2,1)S(1)} %broadcast_in_dim.9), channel_id=1, replica_groups={{0,2,4,6,32,34,36,38},{1,3,5,7,33,35,37,39},{8,10,12,14,40,42,44,46},{9..., dimensions={0} | all-to-all | bytes 524288 | tf_op jit(solution)/shard_map/all_to_all | solution.py:382
  46.7 13.3 %all_to_all.22 = bf16[16,64,256]{2,1,0:T(8,128)(2,1)S(1)} all-to-all(bf16[16,64,256]{2,1,0:T(8,128)(2,1)S(1)} %broadcast_in_dim.10), channel_id=1, replica_groups={{0,8,16,24,64,72,80,88,128,136,144,152,192,200,208,216},{32,40,48,56,96..., dimensions={0} | all-to-all | bytes 1048576 | tf_op jit(solution)/shard_map/all_to_all | solution.py:384
  60.0 0.0 collective-permute-start.1
  60.0 1.9 %collective-permute-done.1.other_ref = bf16[1024,256]{1,0:T(8,128)(2,1)S(1)} collective-permute-done((bf16[1024,256]{1,0:T(8,128)(2,1)S(1)}, bf16[1024,256]{1,0:T(8,128)(2,1)S(1)}, u32[]{:S(2)}, u32[]{:S(2)}) %collective-permute-start.1) | collective-permute-done | bytes 524320 | tf_op jit(solution)/shard_map/ppermute | solution.py:386
  61.9 0.0 copy-start.1
  61.9 2.1 %copy-done.1 = bf16[2,3840,256]{2,1,0:T(8,128)(2,1)S(1)} copy-done((bf16[2,3840,256]{2,1,0:T(8,128)(2,1)S(1)}, bf16[2,3840,256]{2,1,0:T(8,128)(2,1)}, u32[]{:S(2)}) %copy-start.1) | copy-done | bytes 3932184
  64.0 20.0 %score.1 = f32[8,2,4,256]{3,2,1,0:T(4,128)S(1)} custom-call(bf16[1024,256]{1,0:T(8,128)(2,1)S(1)} %bitcast.11, bf16[1024,256]{1,0:T(8,128)(2,1)S(1)} %collective-permute-done.1.other_ref, bf16[2,8,480,256]{3,2,1,0:T(8,128)(2,1)S(1)} %bitcast.9), custom_call_target="tpu_custom_call" | custom-call | tf_op jit(solution)/shard_map/score/pallas_call | solution.py:247
  84.1 9.0 %all_to_all.23.parts_ref = f32[8,2,4,256]{3,2,1,0:T(4,128)} all-to-all(f32[8,2,4,256]{3,2,1,0:T(4,128)S(1)} %score.1), channel_id=1, replica_groups=mesh['frame'=32,'tile'=8] {'tile'}, dimensions={0} | all-to-all | bytes 131072 | tf_op jit(solution)/shard_map/all_to_all | solution.py:388
  93.1 1.5 %merge.1 = (f32[2,4,256]{2,1,0:T(4,128)}, f32[4,256]{1,0:T(4,128)}, f32[4,256]{1,0:T(4,128)}) custom-call(f32[8,2,4,256]{3,2,1,0:T(4,128)} %all_to_all.23.parts_ref), custom_call_target="tpu_custom_call" | custom-call | tf_op jit(solution)/shard_map/merge/pallas_call | solution.py:285
  94.5 5.4 %collective-permute-start.2 = (f32[4,256]{1,0:T(4,128)}, f32[4,256]{1,0:T(4,128)S(1)}, u32[]{:S(2)}, u32[]{:S(2)}) collective-permute-start(f32[4,256]{1,0:T(4,128)} %get-tuple-element.14), channel_id=1, source_target_pairs={{0,8},{8,16},{16,24},{24,32},{32,40},{40,48},{48,56},{56,64},{64,7... | collective-permute-start | bytes 12296 | tf_op jit(solution)/shard_map/ppermute | solution.py:391
  100.0 1.9 %collective-permute-start.3 = (f32[4,256]{1,0:T(4,128)}, f32[4,256]{1,0:T(4,128)S(1)}, u32[]{:S(2)}, u32[]{:S(2)}) collective-permute-start(f32[4,256]{1,0:T(4,128)} %get-tuple-element.16), channel_id=1, source_target_pairs={{8,0},{16,8},{24,16},{32,24},{40,32},{48,40},{56,48},{64,56},{72,6... | collective-permute-start | bytes 12296 | tf_op jit(solution)/shard_map/ppermute | solution.py:392
  101.9 1.5 %prepare.1 = (bf16[256,128]{1,0:T(8,128)(2,1)}, bf16[16,256]{1,0:T(8,128)(2,1)}) custom-call(f32[3,4,256]{2,1,0:T(4,128)} %weight_ref.1, f32[1,256]{1,0:T(1,128)} %bitcast.16, f32[3,256]{1,0:T(4,128)} %out_weight_ref.1), custom_call_target="tpu_custom_call" | custom-call | flops 200000 | bytes 200000 | tf_op jit(solution)/shard_map/prepare/pallas_call | solution.py:321
  103.4 0.0 collective-permute-done.2.before_ref
  103.4 0.0 copy-start.5
  103.4 8.3 %collective-permute-done.3.after_ref = f32[4,256]{1,0:T(4,128)S(1)} collective-permute-done((f32[4,256]{1,0:T(4,128)}, f32[4,256]{1,0:T(4,128)S(1)}, u32[]{:S(2)}, u32[]{:S(2)}) %collective-permute-start.3) | collective-permute-done | bytes 4128 | tf_op jit(solution)/shard_map/ppermute | solution.py:392
  111.7 0.0 copy-start.6
  111.7 0.0 copy-done.5
  111.7 0.6 copy-done.6
  112.3 1.9 %refine.1 = f32[2,3,256]{2,1,0:T(4,128)} custom-call(f32[4,256]{1,0:T(4,128)} %copy-done.5, f32[2,4,256]{2,1,0:T(4,128)} %get-tuple-element.15.inputs_ref, f32[4,256]{1,0:T(4,128)} %copy-done.6, bf16[256,128]{1,0:T(8,128)(2,1)} %get-tuple-element.17.taps_ref, bf16[16,256]{1,0:T(8,128)(2,1)} %get-tuple-element.18.last_ref), custom_call_target="tpu_custom_call" | custom-call | tf_op jit(solution)/shard_map/refine/pallas_call | solution.py:360
  114.2 1.3 %copy.9 = f32[2,3,256]{2,0,1:T(2,128)} copy(f32[2,3,256]{2,1,0:T(4,128)} %refine.1) | data formatting | bytes 12288 | tf_op jit(solution)/shard_map/refine/pallas_call | solution.py:360
  (3 shorter events, 0.1 us)
Async XLA Ops:
  0.0 2.1 %copy-start = (bf16[2,3840,256]{2,1,0:T(8,128)(2,1)S(1)}, bf16[2,3840,256]{2,1,0:T(8,128)(2,1)}, u32[]{:S(2)}) copy-start(bf16[2,3840,256]{2,1,0:T(8,128)(2,1)} %param.7) | copy-start | bytes 11796484
  2.1 0.7 copy-start.2
  2.8 0.7 copy-start.3
  3.5 0.7 copy-start.4
  7.4 2.0 %collective-permute-start = (bf16[1024,256]{1,0:T(8,128)(2,1)S(1)}, bf16[1024,256]{1,0:T(8,128)(2,1)S(1)}, u32[]{:S(2)}, u32[]{:S(2)}) collective-permute-start(bf16[1024,256]{1,0:T(8,128)(2,1)S(1)} %get-tuple-element.13), channel_id=1, source_target_pairs={{0,1},{1,0},{2,3},{3,2},{4,5},{5,4},{6,7},{7,6},{8,9},{9,8},{10,11... | collective-permute-start | bytes 1572872 | tf_op jit(solution)/shard_map/ppermute | solution.py:377
  60.0 1.9 %collective-permute-start.1 = (bf16[1024,256]{1,0:T(8,128)(2,1)S(1)}, bf16[1024,256]{1,0:T(8,128)(2,1)S(1)}, u32[]{:S(2)}, u32[]{:S(2)}) collective-permute-start(bf16[1024,256]{1,0:T(8,128)(2,1)S(1)} %bitcast.10), channel_id=1, source_target_pairs={{0,1},{1,0},{2,3},{3,2},{4,5},{5,4},{6,7},{7,6},{8,9},{9,8},{10,11... | collective-permute-start | bytes 1572872 | tf_op jit(solution)/shard_map/ppermute | solution.py:386
  61.9 2.1 %copy-start.1 = (bf16[2,3840,256]{2,1,0:T(8,128)(2,1)S(1)}, bf16[2,3840,256]{2,1,0:T(8,128)(2,1)}, u32[]{:S(2)}) copy-start(bf16[2,3840,256]{2,1,0:T(8,128)(2,1)} %param.7) | copy-start | bytes 11796484
  94.5 8.8 %collective-permute-start.2 = (f32[4,256]{1,0:T(4,128)}, f32[4,256]{1,0:T(4,128)S(1)}, u32[]{:S(2)}, u32[]{:S(2)}) collective-permute-start(f32[4,256]{1,0:T(4,128)} %get-tuple-element.14), channel_id=1, source_target_pairs={{0,8},{8,16},{16,24},{24,32},{32,40},{40,48},{48,56},{56,64},{64,7... | collective-permute-start | bytes 12296 | tf_op jit(solution)/shard_map/ppermute | solution.py:391
  100.0 11.7 %collective-permute-start.3 = (f32[4,256]{1,0:T(4,128)}, f32[4,256]{1,0:T(4,128)S(1)}, u32[]{:S(2)}, u32[]{:S(2)}) collective-permute-start(f32[4,256]{1,0:T(4,128)} %get-tuple-element.16), channel_id=1, source_target_pairs={{8,0},{16,8},{24,16},{32,24},{40,32},{48,40},{56,48},{64,56},{72,6... | collective-permute-start | bytes 12296 | tf_op jit(solution)/shard_map/ppermute | solution.py:392
  103.4 8.3 %copy-start.5 = (f32[4,256]{1,0:T(4,128)}, f32[4,256]{1,0:T(4,128)S(1)}, u32[]{:S(2)}) copy-start(f32[4,256]{1,0:T(4,128)S(1)} %collective-permute-done.2.before_ref) | copy-start | bytes 12292
  111.7 0.6 copy-start.6

commit v3 on v2

--- a/solution.py
+++ b/solution.py
@@ -22,6 +22,9 @@
         for c in range(2)
     ]
     return plane, column
+
+
+BATCH = 4
 
 
 def pick_kernel(rows_here, qf_ref, qr_ref, qc_ref, feat_ref, keep_ref, send_ref, idx, vm, sm, found_at, slots, wide, lines, sems, sem):
@@ -45,6 +48,7 @@
     vm[0:sets, :] = frame * pix_count + row * W + idx[2]
     bit = lax.broadcasted_iota(jnp.int32, owned.shape, 0)
     word = jnp.sum(jnp.where(owned, jnp.left_shift(1, bit), 0), axis=0, keepdims=True)
+    word = word | jnp.left_shift(pltpu.roll(word, groups // 2, axis=1), sets)
     vm[sets : sets + 8, :] = jnp.broadcast_to(word, (8, groups))
     to_scalar = pltpu.make_async_copy(vm, sm, sems.at[3])
     to_scalar.start()
@@ -58,15 +62,19 @@
         def step(state):
             left, count = state
             i = 31 - lax.clz(left & -left)
-            pix = sm[i, g]
+            at, lane = i % sets, g + (i // sets) * (groups // 2)
+            pix = sm[at, lane]
             copy(count, pix).start()
-            found_at[0, count] = i * groups + g
+            found_at[0, count] = at * groups + lane
             found_at[1, count] = pix % 16
             return left & (left - 1), count + 1
 
         return lax.while_loop(lambda state: state[0] != 0, step, (sm[sets, g], count))[1]
 
-    found = lax.fori_loop(0, groups, group, 0)
+    found = lax.fori_loop(0, groups // 2, group, 0)
+    for k in range(BATCH - 1):
+        found_at[0, found + k] = lines.shape[0] - 8
+        found_at[1, found + k] = 0
 
     def wait(k, carry):
         copy(0, 0).wait()
@@ -74,12 +82,15 @@
 
     lax.fori_loop(0, found, wait, 0)
 
-    def place(k, carry):
-        wide[k % 8] = slots[k].astype(jnp.float32)
-        lines[pl.ds(found_at[0, k], 1), :] = wide[k % 8, pl.ds(found_at[1, k], 1), :]
+    def place(batch, carry):
+        for k in range(BATCH):
+            wide[k] = slots[batch * BATCH + k].astype(jnp.float32)
+        picked = [wide[k, pl.ds(found_at[1, batch * BATCH + k], 1), :] for k in range(BATCH)]
+        for k in range(BATCH):
+            lines[pl.ds(found_at[0, batch * BATCH + k], 1), :] = picked[k]
         return carry
 
-    lax.fori_loop(0, found, place, 0)
+    lax.fori_loop(0, (found + BATCH - 1) // BATCH, place, 0)
     mine = pl.multiple_of(core * half, half)
     theirs = pl.multiple_of((1 - core) * half, half)
     keep_ref[...] = (lines[pl.ds(mine, half), :] * 0.0625).astype(keep_ref.dtype)
@@ -103,14 +114,14 @@
             pltpu.VMEM((3, sets, lanes), jnp.int32),
             pltpu.VMEM((sets + 8, lanes), jnp.int32),
             pltpu.SMEM((sets + 8, lanes), jnp.int32),
-            pltpu.SMEM((2, queries), jnp.int32),
-            pltpu.VMEM((queries, 16, chan), features.dtype),
-            pltpu.VMEM((8, 16, chan), jnp.float32),
-            pltpu.VMEM((queries, chan), jnp.float32),
+            pltpu.SMEM((2, queries + BATCH), jnp.int32),
+            pltpu.VMEM((queries + BATCH, 16, chan), features.dtype),
+            pltpu.VMEM((BATCH, 16, chan), jnp.float32),
+            pltpu.VMEM((queries + 8, chan), jnp.float32),
             pltpu.SemaphoreType.DMA((4,)),
             pltpu.SemaphoreType.DMA,
         ],
-        compiler_params=pltpu.CompilerParams(vmem_limit_bytes=28 << 20),
+        compiler_params=pltpu.CompilerParams(vmem_limit_bytes=56 << 20),
         name="pick",
     )(*[a.reshape(sets, lanes) for a in (query_frame, query_row, query_col)], flat)
 
@@ -255,12 +266,12 @@
             kept,
             pltpu.SemaphoreType.DMA((frames, PARTS)),
         ],
-        compiler_params=pltpu.CompilerParams(vmem_limit_bytes=28 << 20),
+        compiler_params=pltpu.CompilerParams(vmem_limit_bytes=51 << 20),
         name="score",
     )(own, other, features.reshape(frames, rows_here, W, chan))
 
 
-def merge_kernel(pixels, parts_ref, inputs_ref, first_ref, last_ref):
+def merge_kernel(pixels, parts_ref, inputs_ref, far_ref, near_ref):
     tiles, frames = parts_ref.shape[0], parts_ref.shape[1]
     for f in range(frames):
         parts = [parts_ref[k, f] for k in range(tiles)]
@@ -273,9 +284,12 @@
         )
         inputs_ref[f] = here
         if f == 0:
-            first_ref[...] = here
+            first = here
         if f == frames - 1:
-            last_ref[...] = here
+            last = here
+    odd = lax.axis_index("frame") % 2 == 1
+    far_ref[...] = jnp.where(odd, last, first)
+    near_ref[...] = jnp.where(odd, first, last)
 
 
 def merge(parts, pixels):
@@ -287,6 +301,7 @@
         out_shape=(jax.ShapeDtypeStruct((frames, stats, share), jnp.float32), edge, edge),
         in_specs=[vmem],
         out_specs=(vmem, vmem, vmem),
+        compiler_params=pltpu.CompilerParams(vmem_limit_bytes=4 << 20),
         name="merge",
     )(parts)
 
@@ -327,13 +342,17 @@
         in_specs=[vmem] * 3,
         out_specs=(vmem, vmem),
         cost_estimate=pl.CostEstimate(flops=200000, bytes_accessed=200000, transcendentals=0),
+        compiler_params=pltpu.CompilerParams(vmem_limit_bytes=8 << 20),
         name="prepare",
     )(conv_weight, conv_bias[None, :], out_weight)
 
 
-def refine_kernel(before_ref, inputs_ref, after_ref, taps_ref, last_ref, out_ref, held, sem):
+def refine_kernel(far_ref, inputs_ref, near_ref, taps_ref, last_ref, out_ref, held, sem):
     frames, share = inputs_ref.shape[0], inputs_ref.shape[2]
-    line = [before_ref[...]] + [inputs_ref[f] for f in range(frames)] + [after_ref[...]]
+    odd = lax.axis_index("frame") % 2 == 1
+    far, near = far_ref[...], near_ref[...]
+    before, after = jnp.where(odd, near, far), jnp.where(odd, far, near)
+    line = [before] + [inputs_ref[f] for f in range(frames)] + [after]
     unit = jnp.where(lax.broadcasted_iota(jnp.int32, (4, share), 0) == 0, 1.0, 0.0)
     right = []
     for f in range(frames):
@@ -349,22 +368,26 @@
         first = jnp.dot(last_ref[...], high, preferred_element_type=jnp.float32)
         second = jnp.dot(last_ref[...], rest, preferred_element_type=jnp.float32)
         delta = first[0:3] + (first[8:11] + second[0:3])
-        held[f] = line[f + 1][0:3] + delta
+        moved = line[f + 1][0:3] + delta
+        for o in range(3):
+            held[o, f : f + 1] = moved[o : o + 1]
     store = pltpu.make_async_copy(held, out_ref, sem)
     store.start()
     store.wait()
 
 
-def refine(before, inputs, after, taps, last):
+def refine(far, inputs, near, taps, last):
     frames, _, share = inputs.shape
-    return pl.pallas_call(
+    moved = pl.pallas_call(
         refine_kernel,
-        out_shape=jax.ShapeDtypeStruct((frames, 3, share), jnp.float32),
+        out_shape=jax.ShapeDtypeStruct((3, frames, share), jnp.float32),
         in_specs=[pl.BlockSpec(memory_space=pltpu.VMEM)] * 5,
         out_specs=pl.BlockSpec(memory_space=pltpu.MemorySpace.HBM),
-        scratch_shapes=[pltpu.VMEM((frames, 3, share), jnp.float32), pltpu.SemaphoreType.DMA],
+        scratch_shapes=[pltpu.VMEM((3, frames, share), jnp.float32), pltpu.SemaphoreType.DMA],
+        compiler_params=pltpu.CompilerParams(vmem_limit_bytes=8 << 20),
         name="refine",
-    )(before, inputs, after, taps, last)
+    )(far, inputs, near, taps, last)
+    return jnp.transpose(moved, (1, 0, 2))
 
 
 def local(features, query_frame, query_row, query_col, conv_weight, conv_bias, out_weight):
@@ -386,12 +409,11 @@
     other = lax.ppermute(own, "tile", swap)
     parts = score(own, other, features, rows_here)
     parts = lax.all_to_all(parts, "tile", 0, 0)
-    inputs, first, last = merge(parts, rows_here * tiles * W)
-    up = [(i, i + 1) for i in range(groups - 1)]
-    before = lax.ppermute(last, "frame", up)
-    after = lax.ppermute(first, "frame", [(j, i) for i, j in up])
+    inputs, far, near = merge(parts, rows_here * tiles * W)
+    far = lax.ppermute(far, "frame", [p for i in range(1, groups - 1, 2) for p in ((i, i + 1), (i + 1, i))])
+    near = lax.ppermute(near, "frame", [(i, i ^ 1) for i in range(groups)])
     taps, last_weight = prepare(conv_weight, conv_bias, out_weight)
-    return refine(before, inputs, after, taps, last_weight)
+    return refine(far, inputs, near, taps, last_weight)
 
 
 def solution(mesh):

time: 116 us -> 103 us (0.89)
  the two profiles are of different devices: /device:TPU:24 before, /device:TPU:6 now
where the time goes in v3:
time: 103 us; the launch traced here: 102 us
  blocking collectives  58.1 us (56%)
  Pallas kernels  26.3 us (26%)
  waiting for transfers between devices  11.9 us (12%)
  starting transfers between devices  4.51 us (4%)
  other arithmetic  1.29 us (1%)
    pallas_call x1, Pallas kernels, score(): pl.pallas_call(score_kernel, out_shape=jax.ShapeDtypeStruct((blocks, fram...  20.6 us
    all_to_all x1, blocking collectives, local(): lax.all_to_all(jnp.broadcast_to(piece, (tall, rows, chan)), BOTH, 0, 0, a...  18.6 us
    all_to_all x1, blocking collectives, local(): lax.all_to_all(mine.reshape(wide, rows, chan), 'frame', 0, 0, axis_index_...  17.6 us
    all_to_all x1, blocking collectives, local(): lax.all_to_all(jnp.broadcast_to(piece, (wide, rows, chan)), 'frame', 0, 0...  13.6 us
    all_to_all x1, blocking collectives, local(): parts = lax.all_to_all(parts, 'tile', 0, 0)  8.3 us
    ppermute x1, waiting for transfers between devices, local(): lax.ppermute(far, 'frame', [p for i in range(1, groups - 1, 2) for p in (...  7.85 us
    pallas_call x1, Pallas kernels, pick(): pl.pallas_call(functools.partial(pick_kernel, rows_here), out_shape=(half...  4.4 us
    ppermute x1, starting transfers between devices, local(): lax.ppermute(far, 'frame', [p for i in range(1, groups - 1, 2) for p in (...  4.32 us
  transfers between devices with their start and end apart: 4, of which 3 were waited for; matrix products, arithmetic and copies ran while one was open for 0% of the time, Pallas kernels for 0%

profile of v3, /device:TPU:6, one launch (start us, length us, event | category | flops | bytes accessed | tf_op | source)
XLA Modules:
  0.0 102.3 jit_solution(11254732848210330811)
XLA Ops:
  0.0 4.4 %pick.1 = (bf16[1024,256]{1,0:T(8,128)(2,1)}, bf16[1024,256]{1,0:T(8,128)(2,1)}) custom-call(s32[16,128]{1,0:T(8,128)} %bitcast.15, s32[16,128]{1,0:T(8,128)} %bitcast.16, s32[16,128]{1,0:T(8,128)} %bitcast.17, bf16[7680,256]{1,0:T(8,128)(2,1)} %bitcast.12), custom_call_target="tpu_custom_call" | custom-call | tf_op jit(solution)/shard_map/pick/pallas_call | solution.py:108
  4.4 0.1 collective-permute-start
  4.5 2.1 %collective-permute-done = bf16[1024,256]{1,0:T(8,128)(2,1)S(1)} collective-permute-done((bf16[1024,256]{1,0:T(8,128)(2,1)}, bf16[1024,256]{1,0:T(8,128)(2,1)S(1)}, u32[]{:S(2)}, u32[]{:S(2)}) %collective-permute-start) | collective-permute-done | bytes 524320 | tf_op jit(solution)/shard_map/ppermute | solution.py:400
  6.6 1.2 %add.3 = bf16[1024,256]{1,0:T(8,128)(2,1)S(1)} add(bf16[1024,256]{1,0:T(8,128)(2,1)} %get-tuple-element.12, bf16[1024,256]{1,0:T(8,128)(2,1)S(1)} %collective-permute-done) | non-fusion elementwise | flops 262144 | bytes 1572864 | tf_op jit(solution)/shard_map/add | solution.py:400
  7.8 17.6 %all_to_all.20 = bf16[16,64,256]{2,1,0:T(8,128)(2,1)S(1)} all-to-all(bf16[16,64,256]{2,1,0:T(8,128)(2,1)S(1)} %bitcast.14), channel_id=1, replica_groups={{0,8,16,24,64,72,80,88,128,136,144,152,192,200,208,216},{32,40,48,56,96..., dimensions={0} | all-to-all | bytes 1048576 | tf_op jit(solution)/shard_map/all_to_all | solution.py:403
  25.4 0.1 reduce_sum.24
  25.5 0.0 copy-start
  25.5 0.0 copy-start.1
  25.5 0.0 copy-start.2
  25.5 18.6 %all_to_all.21 = bf16[8,64,256]{2,1,0:T(8,128)(2,1)S(1)} all-to-all(bf16[8,64,256]{2,1,0:T(8,128)(2,1)S(1)} %broadcast_in_dim.9), channel_id=1, replica_groups={{0,2,4,6,32,34,36,38},{1,3,5,7,33,35,37,39},{8,10,12,14,40,42,44,46},{9..., dimensions={0} | all-to-all | bytes 524288 | tf_op jit(solution)/shard_map/all_to_all | solution.py:405
  44.3 13.6 %all_to_all.22 = bf16[16,64,256]{2,1,0:T(8,128)(2,1)S(1)} all-to-all(bf16[16,64,256]{2,1,0:T(8,128)(2,1)S(1)} %broadcast_in_dim.10), channel_id=1, replica_groups={{0,8,16,24,64,72,80,88,128,136,144,152,192,200,208,216},{32,40,48,56,96..., dimensions={0} | all-to-all | bytes 1048576 | tf_op jit(solution)/shard_map/all_to_all | solution.py:407
  57.8 0.0 collective-permute-start.1
  57.8 1.9 %collective-permute-done.1.other_ref = bf16[1024,256]{1,0:T(8,128)(2,1)S(1)} collective-permute-done((bf16[1024,256]{1,0:T(8,128)(2,1)S(1)}, bf16[1024,256]{1,0:T(8,128)(2,1)S(1)}, u32[]{:S(2)}, u32[]{:S(2)}) %collective-permute-start.1) | collective-permute-done | bytes 524320 | tf_op jit(solution)/shard_map/ppermute | solution.py:409
  59.8 20.6 %score.1 = f32[8,2,4,256]{3,2,1,0:T(4,128)S(1)} custom-call(bf16[1024,256]{1,0:T(8,128)(2,1)S(1)} %bitcast.10, bf16[1024,256]{1,0:T(8,128)(2,1)S(1)} %collective-permute-done.1.other_ref, bf16[2,8,480,256]{3,2,1,0:T(8,128)(2,1)} %bitcast.13), custom_call_target="tpu_custom_call" | custom-call | tf_op jit(solution)/shard_map/score/pallas_call | solution.py:258
  80.4 8.3 %all_to_all.23.parts_ref = f32[8,2,4,256]{3,2,1,0:T(4,128)S(1)} all-to-all(f32[8,2,4,256]{3,2,1,0:T(4,128)S(1)} %score.1), channel_id=1, replica_groups=mesh['frame'=32,'tile'=8] {'tile'}, dimensions={0} | all-to-all | bytes 131072 | tf_op jit(solution)/shard_map/all_to_all | solution.py:411
  88.7 0.1 merge.1
  88.7 4.3 %collective-permute-start.2 = (f32[4,256]{1,0:T(4,128)S(1)}, f32[4,256]{1,0:T(4,128)S(1)}, u32[]{:S(2)}, u32[]{:S(2)}) collective-permute-start(f32[4,256]{1,0:T(4,128)S(1)} %get-tuple-element.14), channel_id=1, source_target_pairs={{8,16},{16,8},{24,32},{32,24},{40,48},{48,40},{56,64},{64,56},{72,... | collective-permute-start | bytes 12296 | tf_op jit(solution)/shard_map/ppermute | solution.py:413
  93.1 0.1 collective-permute-start.3
  93.2 0.0 copy-done
  93.2 0.0 copy-done.1
  93.2 0.0 copy-done.2
  93.2 0.1 prepare.1
  93.3 7.9 %collective-permute-done.2.far_ref = f32[4,256]{1,0:T(4,128)S(1)} collective-permute-done((f32[4,256]{1,0:T(4,128)S(1)}, f32[4,256]{1,0:T(4,128)S(1)}, u32[]{:S(2)}, u32[]{:S(2)}) %collective-permute-start.2) | collective-permute-done | bytes 4128 | tf_op jit(solution)/shard_map/ppermute | solution.py:413
  101.1 0.0 collective-permute-done.3.near_ref
  101.1 1.1 %refine.1 = f32[3,2,256]{2,1,0:T(2,128)} custom-call(f32[4,256]{1,0:T(4,128)S(1)} %collective-permute-done.2.far_ref, f32[2,4,256]{2,1,0:T(4,128)S(1)} %get-tuple-element.15.inputs_ref, f32[4,256]{1,0:T(4,128)S(1)} %collective-permute-done.3.near_ref, bf16[256,128]{1,0:T(8,128)(2,1)S(1)} %get-tuple-element.17.taps_ref, ...), custom_call_target="tpu_custom_call" | custom-call | tf_op jit(solution)/shard_map/refine/pallas_call | solution.py:381
  (3 shorter events, 0.1 us)
Async XLA Ops:
  4.4 2.2 %collective-permute-start = (bf16[1024,256]{1,0:T(8,128)(2,1)}, bf16[1024,256]{1,0:T(8,128)(2,1)S(1)}, u32[]{:S(2)}, u32[]{:S(2)}) collective-permute-start(bf16[1024,256]{1,0:T(8,128)(2,1)} %get-tuple-element.13), channel_id=1, source_target_pairs={{0,1},{1,0},{2,3},{3,2},{4,5},{5,4},{6,7},{7,6},{8,9},{9,8},{10,11... | collective-permute-start | bytes 1572872 | tf_op jit(solution)/shard_map/ppermute | solution.py:400
  25.5 67.7 %copy-start = (f32[3,4,256]{2,1,0:T(4,128)S(1)}, f32[3,4,256]{2,1,0:T(4,128)}, u32[]{:S(2)}) copy-start(f32[3,4,256]{2,1,0:T(4,128)} %weight_ref.1) | copy-start | bytes 36868
  25.5 67.7 %copy-start.1 = (f32[3,256]{1,0:T(4,128)S(1)}, f32[3,256]{1,0:T(4,128)}, u32[]{:S(2)}) copy-start(f32[3,256]{1,0:T(4,128)} %out_weight_ref.1) | copy-start | bytes 9220
  25.5 67.7 %copy-start.2 = (f32[256]{0:T(256)S(1)}, f32[256]{0:T(256)}, u32[]{:S(2)}) copy-start(f32[256]{0:T(256)} %param.12) | copy-start | bytes 3076
  57.8 1.9 %collective-permute-start.1 = (bf16[1024,256]{1,0:T(8,128)(2,1)S(1)}, bf16[1024,256]{1,0:T(8,128)(2,1)S(1)}, u32[]{:S(2)}, u32[]{:S(2)}) collective-permute-start(bf16[1024,256]{1,0:T(8,128)(2,1)S(1)} %bitcast.9), channel_id=1, source_target_pairs={{0,1},{1,0},{2,3},{3,2},{4,5},{5,4},{6,7},{7,6},{8,9},{9,8},{10,11... | collective-permute-start | bytes 1572872 | tf_op jit(solution)/shard_map/ppermute | solution.py:409
  88.7 12.4 %collective-permute-start.2 = (f32[4,256]{1,0:T(4,128)S(1)}, f32[4,256]{1,0:T(4,128)S(1)}, u32[]{:S(2)}, u32[]{:S(2)}) collective-permute-start(f32[4,256]{1,0:T(4,128)S(1)} %get-tuple-element.14), channel_id=1, source_target_pairs={{8,16},{16,8},{24,32},{32,24},{40,48},{48,40},{56,64},{64,56},{72,... | collective-permute-start | bytes 12296 | tf_op jit(solution)/shard_map/ppermute | solution.py:413
  93.1 8.1 %collective-permute-start.3 = (f32[4,256]{1,0:T(4,128)S(1)}, f32[4,256]{1,0:T(4,128)S(1)}, u32[]{:S(2)}, u32[]{:S(2)}) collective-permute-start(f32[4,256]{1,0:T(4,128)S(1)} %get-tuple-element.16), channel_id=1, source_target_pairs={{0,8},{8,0},{16,24},{24,16},{32,40},{40,32},{48,56},{56,48},{64,72... | collective-permute-start | bytes 12296 | tf_op jit(solution)/shard_map/ppermute | solution.py:414

commit v4 on v3

--- a/solution.py
+++ b/solution.py
@@ -27,46 +27,41 @@
 BATCH = 4
 
 
-def pick_kernel(rows_here, qf_ref, qr_ref, qc_ref, feat_ref, keep_ref, send_ref, idx, vm, sm, found_at, slots, wide, lines, sems, sem):
+def pick_kernel(rows_here, idx_ref, feat_ref, keep_ref, send_ref, vm, sm, found_at, slots, wide, lines, sems, sem):
     frame_idx, tile_idx = lax.axis_index("frame"), lax.axis_index("tile")
     core = tile_idx % 2
-    loads = [
-        pltpu.make_async_copy(ref, idx.at[k], sems.at[k]) for k, ref in enumerate((qf_ref, qr_ref, qc_ref))
-    ]
-    for load in loads:
-        load.start()
     pix_count = rows_here * W
     frame_count = feat_ref.shape[0] // pix_count
     half = keep_ref.shape[0]
-    sets, groups = idx.shape[1], idx.shape[2]
+    sets, groups = idx_ref.shape
     lines[...] = jnp.zeros_like(lines)
-    for load in loads:
-        load.wait()
-    frame = idx[0] - frame_idx * frame_count
-    row = idx[1] - tile_idx * rows_here
+    frame = jnp.right_shift(idx_ref[...], 18) - frame_idx * frame_count
+    row = (jnp.right_shift(idx_ref[...], 9) & 511) - tile_idx * rows_here
     owned = (frame >= 0) & (frame < frame_count) & (row >= 0) & (row < rows_here)
-    vm[0:sets, :] = frame * pix_count + row * W + idx[2]
+    vm[0:sets, :] = frame * pix_count + row * W + (idx_ref[...] & 511)
     bit = lax.broadcasted_iota(jnp.int32, owned.shape, 0)
     word = jnp.sum(jnp.where(owned, jnp.left_shift(1, bit), 0), axis=0, keepdims=True)
     word = word | jnp.left_shift(pltpu.roll(word, groups // 2, axis=1), sets)
     vm[sets : sets + 8, :] = jnp.broadcast_to(word, (8, groups))
-    to_scalar = pltpu.make_async_copy(vm, sm, sems.at[3])
+    to_scalar = pltpu.make_async_copy(vm, sm, sems)
     to_scalar.start()
     to_scalar.wait()
 
     def copy(k, pix):
-        first = pl.multiple_of((pix // 16) * 16, 16)
-        return pltpu.make_async_copy(feat_ref.at[pl.ds(first, 16), :], slots.at[k], sem)
+        first = pl.multiple_of(pix & ~15, 16)
+        return pltpu.make_async_copy(
+            feat_ref.at[pl.ds(first, 16), :], slots.at[pl.ds(pl.multiple_of(k * 16, 16), 16), :], sem
+        )
 
     def group(g, count):
         def step(state):
             left, count = state
             i = 31 - lax.clz(left & -left)
-            at, lane = i % sets, g + (i // sets) * (groups // 2)
+            at, lane = i & (sets - 1), g + lax.shift_right_logical(i, sets.bit_length() - 1) * (groups // 2)
             pix = sm[at, lane]
             copy(count, pix).start()
             found_at[0, count] = at * groups + lane
-            found_at[1, count] = pix % 16
+            found_at[1, count] = pix & 15
             return left & (left - 1), count + 1
 
         return lax.while_loop(lambda state: state[0] != 0, step, (sm[sets, g], count))[1]
@@ -76,21 +71,26 @@
         found_at[0, found + k] = lines.shape[0] - 8
         found_at[1, found + k] = 0
 
-    def wait(k, carry):
-        copy(0, 0).wait()
-        return carry
-
-    lax.fori_loop(0, found, wait, 0)
+    def wait(rows):
+        def step(k, carry):
+            pltpu.make_async_copy(feat_ref.at[pl.ds(0, rows), :], slots.at[pl.ds(0, rows), :], sem).wait()
+            return carry
+
+        return step
+
+    lax.fori_loop(0, lax.shift_right_logical(found, 3), wait(128), 0)
+    lax.fori_loop(0, found & 7, wait(16), 0)
 
     def place(batch, carry):
         for k in range(BATCH):
-            wide[k] = slots[batch * BATCH + k].astype(jnp.float32)
+            at = pl.multiple_of((batch * BATCH + k) * 16, 16)
+            wide[k] = slots[pl.ds(at, 16), :].astype(jnp.float32)
         picked = [wide[k, pl.ds(found_at[1, batch * BATCH + k], 1), :] for k in range(BATCH)]
         for k in range(BATCH):
             lines[pl.ds(found_at[0, batch * BATCH + k], 1), :] = picked[k]
         return carry
 
-    lax.fori_loop(0, (found + BATCH - 1) // BATCH, place, 0)
+    lax.fori_loop(0, lax.div(found + BATCH - 1, BATCH), place, 0)
     mine = pl.multiple_of(core * half, half)
     theirs = pl.multiple_of((1 - core) * half, half)
     keep_ref[...] = (lines[pl.ds(mine, half), :] * 0.0625).astype(keep_ref.dtype)
@@ -108,22 +108,21 @@
     return pl.pallas_call(
         functools.partial(pick_kernel, rows_here),
         out_shape=(half, half),
-        in_specs=[hbm, hbm, hbm, hbm],
+        in_specs=[vmem, hbm],
         out_specs=(vmem, vmem),
         scratch_shapes=[
-            pltpu.VMEM((3, sets, lanes), jnp.int32),
             pltpu.VMEM((sets + 8, lanes), jnp.int32),
             pltpu.SMEM((sets + 8, lanes), jnp.int32),
             pltpu.SMEM((2, queries + BATCH), jnp.int32),
-            pltpu.VMEM((queries + BATCH, 16, chan), features.dtype),
+            pltpu.VMEM(((queries + BATCH) * 16, chan), features.dtype),
             pltpu.VMEM((BATCH, 16, chan), jnp.float32),
             pltpu.VMEM((queries + 8, chan), jnp.float32),
-            pltpu.SemaphoreType.DMA((4,)),
+            pltpu.SemaphoreType.DMA,
             pltpu.SemaphoreType.DMA,
         ],
-        compiler_params=pltpu.CompilerParams(vmem_limit_bytes=56 << 20),
+        compiler_params=pltpu.CompilerParams(vmem_limit_bytes=51 << 20),
         name="pick",
-    )(*[a.reshape(sets, lanes) for a in (query_frame, query_row, query_col)], flat)
+    )((query_frame * 2**18 + query_row * 2**9 + query_col).reshape(sets, lanes), flat)
 
 
 BLOCK = 256
@@ -163,28 +162,26 @@
             pltpu.matmul_push_rhs(ref[k * BLOCK : (k + 1) * BLOCK, :], 0, m, transpose=True)
 
     def run(*accs):
-        def feed(f, part, staged):
+        def moves(f, part, staged, kept, was, tops):
             for r in range(rows_here):
-                lhs = fbuf[f, r, pl.ds(pl.multiple_of(part * cols, 16), cols), :]
+                seen = None if tops is None else []
+                if tops is not None:
+                    for m in range(UNITS):
+                        scores = pltpu.matmul_pop(accs[m * rows_here + r])
+                        kept[was, m, r * cols : (r + 1) * cols, :] = scores
+                        tops[m] = jnp.maximum(tops[m], jnp.max(scores.reshape(cols // 8, 8, BLOCK), axis=0))
+                        seen.append(scores[cols - 8 : cols, :])
+                if f is not None:
+                    lhs = fbuf[f, r, pl.ds(pl.multiple_of(part * cols, 16), cols), :]
+                    for m in range(UNITS):
+                        pltpu.matmul_acc_lhs(accs[m * rows_here + r], lhs, load_staged_rhs=staged if r == 0 else None)
+                yield seen
+
+        def weighs(kept, part, peaks, sums):
+            start = jnp.asarray(part * cols).astype(jnp.float32)
+            here, across = [None] * UNITS, [None] * UNITS
+            for k in range(cols // 8):
                 for m in range(UNITS):
-                    pltpu.matmul_acc_lhs(accs[m * rows_here + r], lhs, load_staged_rhs=staged if r == 0 else None)
-
-        def drain(kept, part, tops):
-            tops = list(tops)
-            for r in range(rows_here):
-                for m in range(UNITS):
-                    scores = pltpu.matmul_pop(accs[m * rows_here + r])
-                    kept[part, m, r * cols : (r + 1) * cols, :] = scores
-                    tops[m] = jnp.maximum(tops[m], jnp.max(scores.reshape(cols // 8, 8, BLOCK), axis=0))
-            return tuple(tops)
-
-        def weigh(kept, part, peaks, sums):
-            out = []
-            start = jnp.asarray(part * cols).astype(jnp.float32)
-            for m in range(UNITS):
-                total, sum_x, sum_y = sums[m]
-                here, across = None, None
-                for k in range(cols // 8):
                     tail, below = None, None
                     for r in reversed(range(rows_here)):
                         at = r * cols + k * 8
@@ -192,13 +189,33 @@
                         tail = expo if tail is None else tail + expo
                         if r > 0:
                             below = tail if below is None else below + tail
-                    sum_y = sum_y + below
-                    here = tail if here is None else here + tail
+                    sums[m][2] = sums[m][2] + below
+                    here[m] = tail if here[m] is None else here[m] + tail
                     if k > 0:
                         shifted = tail * float(k * 8)
-                        across = shifted if across is None else across + shifted
-                out.append((total + here, sum_x + (across + here * (sub + start)), sum_y))
-            return tuple(out)
+                        across[m] = shifted if across[m] is None else across[m] + shifted
+                    yield
+            for m in range(UNITS):
+                sums[m][0] = sums[m][0] + here[m]
+                sums[m][1] = sums[m][1] + (across[m] + here[m] * (sub + start))
+
+        def weave(moving, weighing, peaks):
+            per = (cols // 8) * UNITS // rows_here
+            if moving is None:
+                moving = iter(())
+            if weighing is None:
+                weighing = iter(())
+            for _ in range(rows_here):
+                seen = next(moving, None)
+                if seen is not None and peaks is not None:
+                    for m in range(UNITS):
+                        peaks[m] = jnp.minimum(peaks[m], jnp.maximum(peaks[m], seen[m]))
+                for _ in range(per):
+                    next(weighing, None)
+            for _ in moving:
+                pass
+            for _ in weighing:
+                pass
 
         def settle(tops):
             return tuple(jnp.broadcast_to(jnp.max(t, axis=0, keepdims=True), t.shape) for t in tops)
@@ -212,38 +229,51 @@
                     [peaks[m][0:1], total, sum_x * (1.0 / W), (sum_y + first_row * total) * (1.0 / total_rows)], axis=0
                 )
 
+        none, fresh = (low,) * UNITS, ((zero, zero, zero),) * UNITS
         stage(0)
-        peaks = None
-        for step in range(steps + 1):
-            f = step // pairs
+        loads[0][0].wait()
+        tops, peaks, sums = None, None, None
+        for step in range(steps + 2):
+            f = step // pairs if step < steps else None
             new, old = (even, odd) if step % 2 == 0 else (odd, even)
-
-            def part_of(i, state, staged=None):
-                tops, sums = state
-                if step < steps:
-                    if step == 0:
-                        pltpu.make_async_copy(
-                            feat_ref.at[0, :, pl.ds(0, cols), :], fbuf.at[0, :, pl.ds(0, cols), :], sems.at[0, i]
-                        ).wait()
-                    feed(f, i, staged)
-                if step > 0:
-                    sums = weigh(old, i, peaks, sums)
-                if step < steps:
-                    tops = drain(new, i, tops)
-                return tops, sums
-
             if step == pairs:
                 for load in loads[1]:
                     load.wait()
-            state = ((low,) * UNITS, ((zero, zero, zero),) * UNITS)
-            state = part_of(0, state, 0)
+            last_peaks = peaks
+            tops = None if tops is None else list(tops)
+            sums = None if sums is None else [list(x) for x in sums]
+            bound = None if last_peaks is None else list(last_peaks)
+            weave(
+                moves(f, 0, 0, old, PARTS - 1, tops) if step <= steps else None,
+                weighs(new, PARTS - 1, bound, sums) if step > 1 else None,
+                bound,
+            )
+            if step <= steps:
+                peaks = None if tops is None else settle(tops)
             if step + 1 < steps:
                 stage((step + 1) % pairs)
-            tops, sums = lax.fori_loop(1, PARTS, part_of, state)
-            if step > 0:
-                finish(step - 1, peaks, sums)
-            if step < steps:
-                peaks = settle(tops)
+            if step > 1:
+                finish(step - 2, last_peaks, sums)
+            if step > steps:
+                break
+
+            def part_of(i, state):
+                tops, sums = state
+                if step == 0:
+                    pltpu.make_async_copy(
+                        feat_ref.at[0, :, pl.ds(0, cols), :], fbuf.at[0, :, pl.ds(0, cols), :], sems.at[0, i]
+                    ).wait()
+                tops, sums = list(tops), [list(x) for x in sums]
+                bound = None if peaks is None else list(peaks)
+                weave(
+                    moves(f, i, None, new, i - 1, tops) if step < steps else None,
+                    weighs(old, i - 1, bound, sums) if step > 0 else None,
+                    bound,
+                )
+                tops, sums = tuple(tops), tuple(tuple(x) for x in sums)
+                return tops, sums
+
+            tops, sums = lax.fori_loop(1, PARTS, part_of, (none, fresh))
 
     pl.run_scoped(
         run, *[pltpu.ACC(m)((cols, BLOCK), jnp.float32) for m in range(UNITS) for _ in range(rows_here)]

time: 103 us -> 98.3 us (0.954)
  Pallas kernels: 26.3 us -> 23 us
    pallas_call x1, Pallas kernels: 20.6 us -> 18.8 us  [score(): pl.pallas_call(score_kernel, out_shape=jax.ShapeDtypeStruct((blocks, fram...]
    pallas_call x1, Pallas kernels: 4.4 us -> 3.02 us  [pick(): pl.pallas_call(functools.partial(pick_kernel, rows_here), out_shape=(half...]
where the time goes in v4:
time: 98.3 us; the launch traced here: 97.9 us
  blocking collectives  57.5 us (58%)
  Pallas kernels  23 us (23%)
  waiting for transfers between devices  11.6 us (12%)
  starting transfers between devices  4.53 us (5%)
  other arithmetic  1 us (1%)
    pallas_call x1, Pallas kernels, score(): pl.pallas_call(score_kernel, out_shape=jax.ShapeDtypeStruct((blocks, fram...  18.8 us
    all_to_all x1, blocking collectives, local(): lax.all_to_all(jnp.broadcast_to(piece, (tall, rows, chan)), BOTH, 0, 0, a...  18.6 us
    all_to_all x1, blocking collectives, local(): lax.all_to_all(mine.reshape(wide, rows, chan), 'frame', 0, 0, axis_index_...  17 us
    all_to_all x1, blocking collectives, local(): lax.all_to_all(jnp.broadcast_to(piece, (wide, rows, chan)), 'frame', 0, 0...  13.6 us
    all_to_all x1, blocking collectives, local(): parts = lax.all_to_all(parts, 'tile', 0, 0)  8.3 us
    ppermute x1, waiting for transfers between devices, local(): lax.ppermute(far, 'frame', [p for i in range(1, groups - 1, 2) for p in (...  7.83 us
    ppermute x1, starting transfers between devices, local(): lax.ppermute(far, 'frame', [p for i in range(1, groups - 1, 2) for p in (...  4.34 us
    pallas_call x1, Pallas kernels, pick(): pl.pallas_call(functools.partial(pick_kernel, rows_here), out_shape=(half...  3.02 us
  transfers between devices with their start and end apart: 4, of which 3 were waited for; matrix products, arithmetic and copies ran while one was open for 0% of the time, Pallas kernels for 0%

profile of v4, /device:TPU:6, one launch (start us, length us, event | category | flops | bytes accessed | tf_op | source)
XLA Modules:
  0.0 97.9 jit_solution(15188157827141848605)
XLA Ops:
  0.0 0.7 add_bitcast_fusion.idx_ref
  0.7 3.0 %pick.1 = (bf16[1024,256]{1,0:T(8,128)(2,1)S(1)}, bf16[1024,256]{1,0:T(8,128)(2,1)S(1)}) custom-call(s32[16,128]{1,0:T(8,128)S(1)} %add_bitcast_fusion.idx_ref, bf16[7680,256]{1,0:T(8,128)(2,1)} %bitcast.11), custom_call_target="tpu_custom_call" | custom-call | tf_op jit(solution)/shard_map/pick/pallas_call | solution.py:108
  3.8 0.1 collective-permute-start
  3.9 1.9 %collective-permute-done = bf16[1024,256]{1,0:T(8,128)(2,1)S(1)} collective-permute-done((bf16[1024,256]{1,0:T(8,128)(2,1)S(1)}, bf16[1024,256]{1,0:T(8,128)(2,1)S(1)}, u32[]{:S(2)}, u32[]{:S(2)}) %collective-permute-start) | collective-permute-done | bytes 524320 | tf_op jit(solution)/shard_map/ppermute | solution.py:430
  5.8 0.1 add.11
  5.9 17.0 %all_to_all.20 = bf16[16,64,256]{2,1,0:T(8,128)(2,1)S(1)} all-to-all(bf16[16,64,256]{2,1,0:T(8,128)(2,1)S(1)} %bitcast.13), channel_id=1, replica_groups={{0,8,16,24,64,72,80,88,128,136,144,152,192,200,208,216},{32,40,48,56,96..., dimensions={0} | all-to-all | bytes 1048576 | tf_op jit(solution)/shard_map/all_to_all | solution.py:433
  22.9 0.1 reduce_sum.24
  23.0 0.0 copy-start
  23.0 0.0 copy-start.1
  23.0 0.0 copy-start.2
  23.0 18.6 %all_to_all.21 = bf16[8,64,256]{2,1,0:T(8,128)(2,1)S(1)} all-to-all(bf16[8,64,256]{2,1,0:T(8,128)(2,1)S(1)} %broadcast_in_dim.9), channel_id=1, replica_groups={{0,2,4,6,32,34,36,38},{1,3,5,7,33,35,37,39},{8,10,12,14,40,42,44,46},{9..., dimensions={0} | all-to-all | bytes 524288 | tf_op jit(solution)/shard_map/all_to_all | solution.py:435
  41.8 13.6 %all_to_all.22 = bf16[16,64,256]{2,1,0:T(8,128)(2,1)S(1)} all-to-all(bf16[16,64,256]{2,1,0:T(8,128)(2,1)S(1)} %broadcast_in_dim.10), channel_id=1, replica_groups={{0,8,16,24,64,72,80,88,128,136,144,152,192,200,208,216},{32,40,48,56,96..., dimensions={0} | all-to-all | bytes 1048576 | tf_op jit(solution)/shard_map/all_to_all | solution.py:437
  55.3 0.0 collective-permute-start.1
  55.4 1.9 %collective-permute-done.1.other_ref = bf16[1024,256]{1,0:T(8,128)(2,1)S(1)} collective-permute-done((bf16[1024,256]{1,0:T(8,128)(2,1)S(1)}, bf16[1024,256]{1,0:T(8,128)(2,1)S(1)}, u32[]{:S(2)}, u32[]{:S(2)}) %collective-permute-start.1) | collective-permute-done | bytes 524320 | tf_op jit(solution)/shard_map/ppermute | solution.py:439
  57.3 18.8 %score.1 = f32[8,2,4,256]{3,2,1,0:T(4,128)S(1)} custom-call(bf16[1024,256]{1,0:T(8,128)(2,1)S(1)} %bitcast.9, bf16[1024,256]{1,0:T(8,128)(2,1)S(1)} %collective-permute-done.1.other_ref, bf16[2,8,480,256]{3,2,1,0:T(8,128)(2,1)} %bitcast.12), custom_call_target="tpu_custom_call" | custom-call | tf_op jit(solution)/shard_map/score/pallas_call | solution.py:288
  76.0 8.3 %all_to_all.23.parts_ref = f32[8,2,4,256]{3,2,1,0:T(4,128)S(1)} all-to-all(f32[8,2,4,256]{3,2,1,0:T(4,128)S(1)} %score.1), channel_id=1, replica_groups=mesh['frame'=32,'tile'=8] {'tile'}, dimensions={0} | all-to-all | bytes 131072 | tf_op jit(solution)/shard_map/all_to_all | solution.py:441
  84.3 0.1 merge.1
  84.4 4.3 %collective-permute-start.2 = (f32[4,256]{1,0:T(4,128)S(1)}, f32[4,256]{1,0:T(4,128)S(1)}, u32[]{:S(2)}, u32[]{:S(2)}) collective-permute-start(f32[4,256]{1,0:T(4,128)S(1)} %get-tuple-element.14), channel_id=1, source_target_pairs={{8,16},{16,8},{24,32},{32,24},{40,48},{48,40},{56,64},{64,56},{72,... | collective-permute-start | bytes 12296 | tf_op jit(solution)/shard_map/ppermute | solution.py:443
  88.7 0.1 collective-permute-start.3
  88.8 0.0 copy-done
  88.8 0.0 copy-done.1
  88.8 0.0 copy-done.2
  88.8 0.1 prepare.1
  89.0 7.8 %collective-permute-done.2.far_ref = f32[4,256]{1,0:T(4,128)S(1)} collective-permute-done((f32[4,256]{1,0:T(4,128)S(1)}, f32[4,256]{1,0:T(4,128)S(1)}, u32[]{:S(2)}, u32[]{:S(2)}) %collective-permute-start.2) | collective-permute-done | bytes 4128 | tf_op jit(solution)/shard_map/ppermute | solution.py:443
  96.8 0.0 collective-permute-done.3.near_ref
  96.8 1.1 %refine.1 = f32[3,2,256]{2,1,0:T(2,128)} custom-call(f32[4,256]{1,0:T(4,128)S(1)} %collective-permute-done.2.far_ref, f32[2,4,256]{2,1,0:T(4,128)S(1)} %get-tuple-element.15.inputs_ref, f32[4,256]{1,0:T(4,128)S(1)} %collective-permute-done.3.near_ref, bf16[256,128]{1,0:T(8,128)(2,1)S(1)} %get-tuple-element.17.taps_ref, ...), custom_call_target="tpu_custom_call" | custom-call | tf_op jit(solution)/shard_map/refine/pallas_call | solution.py:411
  (3 shorter events, 0.1 us)
Async XLA Ops:
  3.8 2.0 %collective-permute-start = (bf16[1024,256]{1,0:T(8,128)(2,1)S(1)}, bf16[1024,256]{1,0:T(8,128)(2,1)S(1)}, u32[]{:S(2)}, u32[]{:S(2)}) collective-permute-start(bf16[1024,256]{1,0:T(8,128)(2,1)S(1)} %get-tuple-element.13), channel_id=1, source_target_pairs={{0,1},{1,0},{2,3},{3,2},{4,5},{5,4},{6,7},{7,6},{8,9},{9,8},{10,11... | collective-permute-start | bytes 1572872 | tf_op jit(solution)/shard_map/ppermute | solution.py:430
  23.0 65.9 %copy-start = (f32[3,4,256]{2,1,0:T(4,128)S(1)}, f32[3,4,256]{2,1,0:T(4,128)}, u32[]{:S(2)}) copy-start(f32[3,4,256]{2,1,0:T(4,128)} %weight_ref.1) | copy-start | bytes 36868
  23.0 65.9 %copy-start.1 = (f32[3,256]{1,0:T(4,128)S(1)}, f32[3,256]{1,0:T(4,128)}, u32[]{:S(2)}) copy-start(f32[3,256]{1,0:T(4,128)} %out_weight_ref.1) | copy-start | bytes 9220
  23.0 65.9 %copy-start.2 = (f32[256]{0:T(256)S(1)}, f32[256]{0:T(256)}, u32[]{:S(2)}) copy-start(f32[256]{0:T(256)} %param.12) | copy-start | bytes 3076
  55.3 1.9 %collective-permute-start.1 = (bf16[1024,256]{1,0:T(8,128)(2,1)S(1)}, bf16[1024,256]{1,0:T(8,128)(2,1)S(1)}, u32[]{:S(2)}, u32[]{:S(2)}) collective-permute-start(bf16[1024,256]{1,0:T(8,128)(2,1)S(1)} %bitcast.8), channel_id=1, source_target_pairs={{0,1},{1,0},{2,3},{3,2},{4,5},{5,4},{6,7},{7,6},{8,9},{9,8},{10,11... | collective-permute-start | bytes 1572872 | tf_op jit(solution)/shard_map/ppermute | solution.py:439
  84.4 12.4 %collective-permute-start.2 = (f32[4,256]{1,0:T(4,128)S(1)}, f32[4,256]{1,0:T(4,128)S(1)}, u32[]{:S(2)}, u32[]{:S(2)}) collective-permute-start(f32[4,256]{1,0:T(4,128)S(1)} %get-tuple-element.14), channel_id=1, source_target_pairs={{8,16},{16,8},{24,32},{32,24},{40,48},{48,40},{56,64},{64,56},{72,... | collective-permute-start | bytes 12296 | tf_op jit(solution)/shard_map/ppermute | solution.py:443
  88.7 8.1 %collective-permute-start.3 = (f32[4,256]{1,0:T(4,128)S(1)}, f32[4,256]{1,0:T(4,128)S(1)}, u32[]{:S(2)}, u32[]{:S(2)}) collective-permute-start(f32[4,256]{1,0:T(4,128)S(1)} %get-tuple-element.16), channel_id=1, source_target_pairs={{0,8},{8,0},{16,24},{24,16},{32,40},{40,32},{48,56},{56,48},{64,72... | collective-permute-start | bytes 12296 | tf_op jit(solution)/shard_map/ppermute | solution.py:444

commit v5 on v4

--- a/solution.py
+++ b/solution.py
@@ -21,7 +21,8 @@
         for y in range(4)
         for c in range(2)
     ]
-    return plane, column
+    couple = [[(f % 32) * 8 + t for f in (i, i + 1) for t in range(8)] for i in range(1, 32, 2)]
+    return plane, column, couple
 
 
 BATCH = 4
@@ -225,9 +226,11 @@
             for m in range(UNITS):
                 total, sum_x, sum_y = [jnp.sum(a, axis=0, keepdims=True) for a in sums[m]]
                 where_to = lax.rem(pair * UNITS + m + core * half_blocks, blocks)
-                out_ref[where_to, f] = jnp.concatenate(
+                packed = jnp.concatenate(
                     [peaks[m][0:1], total, sum_x * (1.0 / W), (sum_y + first_row * total) * (1.0 / total_rows)], axis=0
                 )
+                for side in range(2):
+                    out_ref[side, where_to, f] = packed
 
         none, fresh = (low,) * UNITS, ((zero, zero, zero),) * UNITS
         stage(0)
@@ -287,7 +290,7 @@
     kept = pltpu.VMEM((PARTS, UNITS, pix_count // PARTS, BLOCK), jnp.float32)
     return pl.pallas_call(
         score_kernel,
-        out_shape=jax.ShapeDtypeStruct((blocks, frames, 4, BLOCK), jnp.float32),
+        out_shape=jax.ShapeDtypeStruct((2, blocks, frames, 4, BLOCK), jnp.float32),
         in_specs=[vmem, vmem, pl.BlockSpec(memory_space=pltpu.MemorySpace.HBM)],
         out_specs=vmem,
         scratch_shapes=[
@@ -302,28 +305,30 @@
 
 
 def merge_kernel(pixels, parts_ref, inputs_ref, far_ref, near_ref):
-    tiles, frames = parts_ref.shape[0], parts_ref.shape[1]
-    for f in range(frames):
-        parts = [parts_ref[k, f] for k in range(tiles)]
+    tiles, frames = parts_ref.shape[1], parts_ref.shape[2]
+    frame_idx, last = lax.axis_index("frame"), lax.axis_size("frame") - 1
+    even = 1 - frame_idx % 2
+
+    def joined(side, f):
+        parts = [parts_ref[side, k, f] for k in range(tiles)]
         peak = functools.reduce(jnp.maximum, [p[0:1] for p in parts])
         sums = functools.reduce(jnp.add, [p[1:4] * jnp.exp(p[0:1] - peak) for p in parts])
         total = sums[0:1]
         log_total = jnp.log(total)
-        here = jnp.concatenate(
+        return jnp.concatenate(
             [sums[1:2] / total, sums[2:3] / total, -log_total, peak + log_total - math.log(pixels)], axis=0
         )
-        inputs_ref[f] = here
-        if f == 0:
-            first = here
-        if f == frames - 1:
-            last = here
-    odd = lax.axis_index("frame") % 2 == 1
-    far_ref[...] = jnp.where(odd, last, first)
-    near_ref[...] = jnp.where(odd, first, last)
+
+    for f in range(frames):
+        inputs_ref[f] = joined(even, f)
+    far = joined(1 - even, even * (frames - 1))
+    outside = (frame_idx == 0) | (frame_idx == last)
+    far_ref[...] = jnp.where(outside, 0.0, far)
+    near_ref[...] = jnp.where(even == 1, inputs_ref[frames - 1], inputs_ref[0])
 
 
 def merge(parts, pixels):
-    tiles, frames, stats, share = parts.shape
+    _, _, frames, stats, share = parts.shape
     vmem = pl.BlockSpec(memory_space=pltpu.VMEM)
     edge = jax.ShapeDtypeStruct((stats, share), jnp.float32)
     return pl.pallas_call(
@@ -424,7 +429,7 @@
     frame_count, pix_count, chan = features.shape
     rows_here = pix_count // W
     tiles, groups = lax.axis_size("tile"), lax.axis_size("frame")
-    plane, column = mesh_groups()
+    plane, column, couple = mesh_groups()
     keep, send = pick(features, query_frame, query_row, query_col, rows_here)
     swap = [(i, i ^ 1) for i in range(tiles)]
     mine = keep + lax.ppermute(send, "tile", swap)
@@ -438,9 +443,10 @@
     own = got.reshape(wide * rows, chan)
     other = lax.ppermute(own, "tile", swap)
     parts = score(own, other, features, rows_here)
-    parts = lax.all_to_all(parts, "tile", 0, 0)
-    inputs, far, near = merge(parts, rows_here * tiles * W)
-    far = lax.ppermute(far, "frame", [p for i in range(1, groups - 1, 2) for p in ((i, i + 1), (i + 1, i))])
+    members = 2 * tiles
+    shape = parts.shape
+    parts = lax.all_to_all(parts.reshape(members, *shape[2:]), BOTH, 0, 0, axis_index_groups=couple)
+    inputs, far, near = merge(parts.reshape(shape), rows_here * tiles * W)
     near = lax.ppermute(near, "frame", [(i, i ^ 1) for i in range(groups)])
     taps, last_weight = prepare(conv_weight, conv_bias, out_weight)
     return refine(far, inputs, near, taps, last_weight)

time: 98.3 us -> 99.5 us (1.012)
  the two profiles are of different devices: /device:TPU:6 before, /device:TPU:1 now
where the time goes in v5:
time: 99.5 us; the launch traced here: 99.3 us
  blocking collectives  62 us (62%)
  Pallas kernels  22.5 us (23%)
  starting transfers between devices  8.22 us (8%)
  waiting for transfers between devices  5.38 us (5%)
  other arithmetic  1 us (1%)
    pallas_call x1, Pallas kernels, score(): pl.pallas_call(score_kernel, out_shape=jax.ShapeDtypeStruct((2, blocks, f...  18.8 us
    all_to_all x1, blocking collectives, local(): lax.all_to_all(jnp.broadcast_to(piece, (tall, rows, chan)), BOTH, 0, 0, a...  18.2 us
    all_to_all x1, blocking collectives, local(): lax.all_to_all(parts.reshape(members, *shape[2:]), BOTH, 0, 0, axis_index...  15.8 us
    all_to_all x1, blocking collectives, local(): lax.all_to_all(mine.reshape(wide, rows, chan), 'frame', 0, 0, axis_index_...  15.5 us
    all_to_all x1, blocking collectives, local(): lax.all_to_all(jnp.broadcast_to(piece, (wide, rows, chan)), 'frame', 0, 0...  12.5 us
    ppermute x1, starting transfers between devices, local(): other = lax.ppermute(own, 'tile', swap)  4.78 us
    ppermute x1, starting transfers between devices, local(): mine = keep + lax.ppermute(send, 'tile', swap)  3.35 us
    pallas_call x1, Pallas kernels, pick(): pl.pallas_call(functools.partial(pick_kernel, rows_here), out_shape=(half...  2.52 us
  transfers between devices with their start and end apart: 3, of which 3 were waited for; matrix products, arithmetic and copies ran while one was open for 0% of the time, Pallas kernels for 0%

profile of v5, /device:TPU:1, one launch (start us, length us, event | category | flops | bytes accessed | tf_op | source)
XLA Modules:
  0.0 99.3 jit_solution(12016550430080132725)
XLA Ops:
  0.0 0.7 add_bitcast_fusion.idx_ref
  0.7 2.5 %pick.1 = (bf16[1024,256]{1,0:T(8,128)(2,1)S(1)}, bf16[1024,256]{1,0:T(8,128)(2,1)S(1)}) custom-call(s32[16,128]{1,0:T(8,128)S(1)} %add_bitcast_fusion.idx_ref, bf16[7680,256]{1,0:T(8,128)(2,1)} %bitcast.15), custom_call_target="tpu_custom_call" | custom-call | tf_op jit(solution)/shard_map/pick/pallas_call | solution.py:109
  3.3 3.3 %collective-permute-start = (bf16[1024,256]{1,0:T(8,128)(2,1)S(1)}, bf16[1024,256]{1,0:T(8,128)(2,1)S(1)}, u32[]{:S(2)}, u32[]{:S(2)}) collective-permute-start(bf16[1024,256]{1,0:T(8,128)(2,1)S(1)} %get-tuple-element.13), channel_id=1, source_target_pairs={{0,1},{1,0},{2,3},{3,2},{4,5},{5,4},{6,7},{7,6},{8,9},{9,8},{10,11... | collective-permute-start | bytes 1572872 | tf_op jit(solution)/shard_map/ppermute | solution.py:435
  6.6 1.5 %collective-permute-done = bf16[1024,256]{1,0:T(8,128)(2,1)S(1)} collective-permute-done((bf16[1024,256]{1,0:T(8,128)(2,1)S(1)}, bf16[1024,256]{1,0:T(8,128)(2,1)S(1)}, u32[]{:S(2)}, u32[]{:S(2)}) %collective-permute-start) | collective-permute-done | bytes 524320 | tf_op jit(solution)/shard_map/ppermute | solution.py:435
  8.1 0.1 add.11
  8.3 15.5 %all_to_all.20 = bf16[16,64,256]{2,1,0:T(8,128)(2,1)S(1)} all-to-all(bf16[16,64,256]{2,1,0:T(8,128)(2,1)S(1)} %bitcast.17), channel_id=1, replica_groups={{0,8,16,24,64,72,80,88,128,136,144,152,192,200,208,216},{32,40,48,56,96..., dimensions={0} | all-to-all | bytes 1048576 | tf_op jit(solution)/shard_map/all_to_all | solution.py:438
  23.8 0.1 reduce_sum.24
  23.9 0.0 copy-start
  23.9 0.0 copy-start.1
  23.9 0.0 copy-start.2
  23.9 18.2 %all_to_all.21 = bf16[8,64,256]{2,1,0:T(8,128)(2,1)S(1)} all-to-all(bf16[8,64,256]{2,1,0:T(8,128)(2,1)S(1)} %broadcast_in_dim.9), channel_id=1, replica_groups={{0,2,4,6,32,34,36,38},{1,3,5,7,33,35,37,39},{8,10,12,14,40,42,44,46},{9..., dimensions={0} | all-to-all | bytes 524288 | tf_op jit(solution)/shard_map/all_to_all | solution.py:440
  42.2 12.5 %all_to_all.22 = bf16[16,64,256]{2,1,0:T(8,128)(2,1)S(1)} all-to-all(bf16[16,64,256]{2,1,0:T(8,128)(2,1)S(1)} %broadcast_in_dim.10), channel_id=1, replica_groups={{0,8,16,24,64,72,80,88,128,136,144,152,192,200,208,216},{32,40,48,56,96..., dimensions={0} | all-to-all | bytes 1048576 | tf_op jit(solution)/shard_map/all_to_all | solution.py:442
  54.7 4.8 %collective-permute-start.1 = (bf16[1024,256]{1,0:T(8,128)(2,1)S(1)}, bf16[1024,256]{1,0:T(8,128)(2,1)S(1)}, u32[]{:S(2)}, u32[]{:S(2)}) collective-permute-start(bf16[1024,256]{1,0:T(8,128)(2,1)S(1)} %bitcast.10), channel_id=1, source_target_pairs={{0,1},{1,0},{2,3},{3,2},{4,5},{5,4},{6,7},{7,6},{8,9},{9,8},{10,11... | collective-permute-start | bytes 1572872 | tf_op jit(solution)/shard_map/ppermute | solution.py:444
  59.5 1.5 %collective-permute-done.1.other_ref = bf16[1024,256]{1,0:T(8,128)(2,1)S(1)} collective-permute-done((bf16[1024,256]{1,0:T(8,128)(2,1)S(1)}, bf16[1024,256]{1,0:T(8,128)(2,1)S(1)}, u32[]{:S(2)}, u32[]{:S(2)}) %collective-permute-start.1) | collective-permute-done | bytes 524320 | tf_op jit(solution)/shard_map/ppermute | solution.py:444
  61.0 18.8 %score.1 = f32[2,8,2,4,256]{4,3,2,1,0:T(4,128)S(1)} custom-call(bf16[1024,256]{1,0:T(8,128)(2,1)S(1)} %bitcast.11, bf16[1024,256]{1,0:T(8,128)(2,1)S(1)} %collective-permute-done.1.other_ref, bf16[2,8,480,256]{3,2,1,0:T(8,128)(2,1)} %bitcast.16), custom_call_target="tpu_custom_call" | custom-call | tf_op jit(solution)/shard_map/score/pallas_call | solution.py:291
  79.8 15.8 %all_to_all.23 = f32[16,2,4,256]{3,2,1,0:T(4,128)S(1)} all-to-all(f32[16,2,4,256]{3,2,1,0:T(4,128)S(1)} %bitcast.12), channel_id=1, replica_groups={{8,9,10,11,12,13,14,15,16,17,18,19,20,21,22,23},{24,25,26,27,28,29,30,3..., dimensions={0} | all-to-all | bytes 262144 | tf_op jit(solution)/shard_map/all_to_all | solution.py:448
  95.6 0.1 merge.1
  95.6 0.1 collective-permute-start.2
  95.7 0.0 copy-done
  95.8 0.0 copy-done.1
  95.8 0.0 copy-done.2
  95.8 0.1 prepare.1
  95.9 2.3 %collective-permute-done.2.near_ref = f32[4,256]{1,0:T(4,128)S(1)} collective-permute-done((f32[4,256]{1,0:T(4,128)S(1)}, f32[4,256]{1,0:T(4,128)S(1)}, u32[]{:S(2)}, u32[]{:S(2)}) %collective-permute-start.2) | collective-permute-done | bytes 4128 | tf_op jit(solution)/shard_map/ppermute | solution.py:450
  98.2 1.1 %refine.1 = f32[3,2,256]{2,1,0:T(2,128)} custom-call(f32[4,256]{1,0:T(4,128)S(1)} %get-tuple-element.14.far_ref, f32[2,4,256]{2,1,0:T(4,128)S(1)} %get-tuple-element.15.inputs_ref, f32[4,256]{1,0:T(4,128)S(1)} %collective-permute-done.2.near_ref, bf16[256,128]{1,0:T(8,128)(2,1)S(1)} %get-tuple-element.17.taps_ref, bf16[16,256]{1,0:T(8,128)(2,1)S(1)} %get-tuple-element.18.last_ref), custom_call_target="tpu_custom_call" | custom-call | tf_op jit(solution)/shard_map/refine/pallas_call | solution.py:416
  (3 shorter events, 0.1 us)
Async XLA Ops:
  3.3 4.9 %collective-permute-start = (bf16[1024,256]{1,0:T(8,128)(2,1)S(1)}, bf16[1024,256]{1,0:T(8,128)(2,1)S(1)}, u32[]{:S(2)}, u32[]{:S(2)}) collective-permute-start(bf16[1024,256]{1,0:T(8,128)(2,1)S(1)} %get-tuple-element.13), channel_id=1, source_target_pairs={{0,1},{1,0},{2,3},{3,2},{4,5},{5,4},{6,7},{7,6},{8,9},{9,8},{10,11... | collective-permute-start | bytes 1572872 | tf_op jit(solution)/shard_map/ppermute | solution.py:435
  23.9 71.9 %copy-start = (f32[3,4,256]{2,1,0:T(4,128)S(1)}, f32[3,4,256]{2,1,0:T(4,128)}, u32[]{:S(2)}) copy-start(f32[3,4,256]{2,1,0:T(4,128)} %weight_ref.1) | copy-start | bytes 36868
  23.9 71.9 %copy-start.1 = (f32[3,256]{1,0:T(4,128)S(1)}, f32[3,256]{1,0:T(4,128)}, u32[]{:S(2)}) copy-start(f32[3,256]{1,0:T(4,128)} %out_weight_ref.1) | copy-start | bytes 9220
  23.9 71.9 %copy-start.2 = (f32[256]{0:T(256)S(1)}, f32[256]{0:T(256)}, u32[]{:S(2)}) copy-start(f32[256]{0:T(256)} %param.12) | copy-start | bytes 3076
  54.7 6.3 %collective-permute-start.1 = (bf16[1024,256]{1,0:T(8,128)(2,1)S(1)}, bf16[1024,256]{1,0:T(8,128)(2,1)S(1)}, u32[]{:S(2)}, u32[]{:S(2)}) collective-permute-start(bf16[1024,256]{1,0:T(8,128)(2,1)S(1)} %bitcast.10), channel_id=1, source_target_pairs={{0,1},{1,0},{2,3},{3,2},{4,5},{5,4},{6,7},{7,6},{8,9},{9,8},{10,11... | collective-permute-start | bytes 1572872 | tf_op jit(solution)/shard_map/ppermute | solution.py:444
  95.6 2.5 %collective-permute-start.2 = (f32[4,256]{1,0:T(4,128)S(1)}, f32[4,256]{1,0:T(4,128)S(1)}, u32[]{:S(2)}, u32[]{:S(2)}) collective-permute-start(f32[4,256]{1,0:T(4,128)S(1)} %get-tuple-element.16), channel_id=1, source_target_pairs={{0,8},{8,0},{16,24},{24,16},{32,40},{40,32},{48,56},{56,48},{64,72... | collective-permute-start | bytes 12296 | tf_op jit(solution)/shard_map/ppermute | solution.py:450

commit v6 on v5

--- a/solution.py
+++ b/solution.py
@@ -21,8 +21,21 @@
         for y in range(4)
         for c in range(2)
     ]
-    couple = [[(f % 32) * 8 + t for f in (i, i + 1) for t in range(8)] for i in range(1, 32, 2)]
-    return plane, column, couple
+    tower = [[(x * 8 + zh * 4 + y) * 8 + t for zh in range(2) for t in range(8)] for x in range(4) for y in range(4)]
+    return plane, column, tower
+
+
+def far_pairs():
+    pairs = []
+    for i in range(32):
+        x, zh, y = i // 8, i // 4 % 2, i % 4
+        if y in (1, 2):
+            pairs.append((i, i + 1 if y == 1 else i - 1))
+        elif y == 3 and (zh == 1 or x < 3):
+            pairs.append((i, (x + 1 - zh) * 8 + zh * 4))
+        elif y == 0 and (zh == 0 or x > 0):
+            pairs.append((i, (x - zh) * 8 + zh * 4 + 3))
+    return pairs
 
 
 BATCH = 4
@@ -306,8 +319,9 @@
 
 def merge_kernel(pixels, parts_ref, inputs_ref, far_ref, near_ref):
     tiles, frames = parts_ref.shape[1], parts_ref.shape[2]
-    frame_idx, last = lax.axis_index("frame"), lax.axis_size("frame") - 1
-    even = 1 - frame_idx % 2
+    frame_idx = lax.axis_index("frame")
+    here, y = frame_idx // 4 % 2, frame_idx % 4
+    odd = y % 2
 
     def joined(side, f):
         parts = [parts_ref[side, k, f] for k in range(tiles)]
@@ -320,11 +334,11 @@
         )
 
     for f in range(frames):
-        inputs_ref[f] = joined(even, f)
-    far = joined(1 - even, even * (frames - 1))
-    outside = (frame_idx == 0) | (frame_idx == last)
-    far_ref[...] = jnp.where(outside, 0.0, far)
-    near_ref[...] = jnp.where(even == 1, inputs_ref[frames - 1], inputs_ref[0])
+        inputs_ref[f] = joined(here, f)
+    across = joined(1 - here, odd * (frames - 1))
+    first, last = inputs_ref[0], inputs_ref[frames - 1]
+    far_ref[...] = jnp.where((y == 0) | (y == 3), across, jnp.where(odd == 1, last, first))
+    near_ref[...] = jnp.where(odd == 1, first, last)
 
 
 def merge(parts, pixels):
@@ -429,7 +443,7 @@
     frame_count, pix_count, chan = features.shape
     rows_here = pix_count // W
     tiles, groups = lax.axis_size("tile"), lax.axis_size("frame")
-    plane, column, couple = mesh_groups()
+    plane, column, tower = mesh_groups()
     keep, send = pick(features, query_frame, query_row, query_col, rows_here)
     swap = [(i, i ^ 1) for i in range(tiles)]
     mine = keep + lax.ppermute(send, "tile", swap)
@@ -445,8 +459,9 @@
     parts = score(own, other, features, rows_here)
     members = 2 * tiles
     shape = parts.shape
-    parts = lax.all_to_all(parts.reshape(members, *shape[2:]), BOTH, 0, 0, axis_index_groups=couple)
+    parts = lax.all_to_all(parts.reshape(members, *shape[2:]), BOTH, 0, 0, axis_index_groups=tower)
     inputs, far, near = merge(parts.reshape(shape), rows_here * tiles * W)
+    far = lax.ppermute(far, "frame", far_pairs())
     near = lax.ppermute(near, "frame", [(i, i ^ 1) for i in range(groups)])
     taps, last_weight = prepare(conv_weight, conv_bias, out_weight)
     return refine(far, inputs, near, taps, last_weight)

time: 99.5 us -> 97.5 us (0.980)
  the two profiles are of different devices: /device:TPU:1 before, /device:TPU:6 now
where the time goes in v6:
time: 97.5 us; the launch traced here: 96.5 us
  blocking collectives  61.6 us (63%)
  Pallas kernels  22.2 us (23%)
  waiting for transfers between devices  7.95 us (8%)
  starting transfers between devices  3.45 us (4%)
  other arithmetic  1 us (1%)
    all_to_all x1, blocking collectives, local(): lax.all_to_all(jnp.broadcast_to(piece, (tall, rows, chan)), BOTH, 0, 0, a...  19.3 us
    pallas_call x1, Pallas kernels, score(): pl.pallas_call(score_kernel, out_shape=jax.ShapeDtypeStruct((2, blocks, f...  18.8 us
    all_to_all x1, blocking collectives, local(): lax.all_to_all(mine.reshape(wide, rows, chan), 'frame', 0, 0, axis_index_...  17.5 us
    all_to_all x1, blocking collectives, local(): lax.all_to_all(jnp.broadcast_to(piece, (wide, rows, chan)), 'frame', 0, 0...  13.6 us
    all_to_all x1, blocking collectives, local(): lax.all_to_all(parts.reshape(members, *shape[2:]), BOTH, 0, 0, axis_index...  11.3 us
    ppermute x1, waiting for transfers between devices, local(): far = lax.ppermute(far, 'frame', far_pairs())  4.47 us
    ppermute x1, starting transfers between devices, local(): far = lax.ppermute(far, 'frame', far_pairs())  2.53 us
    pallas_call x1, Pallas kernels, pick(): pl.pallas_call(functools.partial(pick_kernel, rows_here), out_shape=(half...  2.22 us
  transfers between devices with their start and end apart: 4, of which 3 were waited for; matrix products, arithmetic and copies ran while one was open for 0% of the time, Pallas kernels for 0%

profile of v6, /device:TPU:6, one launch (start us, length us, event | category | flops | bytes accessed | tf_op | source)
XLA Modules:
  0.0 96.5 jit_solution(9416994981159154530)
XLA Ops:
  0.0 0.7 add_bitcast_fusion.idx_ref
  0.7 2.2 %pick.1 = (bf16[1024,256]{1,0:T(8,128)(2,1)S(1)}, bf16[1024,256]{1,0:T(8,128)(2,1)S(1)}) custom-call(s32[16,128]{1,0:T(8,128)S(1)} %add_bitcast_fusion.idx_ref, bf16[7680,256]{1,0:T(8,128)(2,1)} %bitcast.15), custom_call_target="tpu_custom_call" | custom-call | tf_op jit(solution)/shard_map/pick/pallas_call | solution.py:122
  3.0 0.4 collective-permute-start
  3.4 1.6 %collective-permute-done = bf16[1024,256]{1,0:T(8,128)(2,1)S(1)} collective-permute-done((bf16[1024,256]{1,0:T(8,128)(2,1)S(1)}, bf16[1024,256]{1,0:T(8,128)(2,1)S(1)}, u32[]{:S(2)}, u32[]{:S(2)}) %collective-permute-start) | collective-permute-done | bytes 524320 | tf_op jit(solution)/shard_map/ppermute | solution.py:449
  5.0 0.1 add.11
  5.1 17.5 %all_to_all.20 = bf16[16,64,256]{2,1,0:T(8,128)(2,1)S(1)} all-to-all(bf16[16,64,256]{2,1,0:T(8,128)(2,1)S(1)} %bitcast.17), channel_id=1, replica_groups={{0,8,16,24,64,72,80,88,128,136,144,152,192,200,208,216},{32,40,48,56,96..., dimensions={0} | all-to-all | bytes 1048576 | tf_op jit(solution)/shard_map/all_to_all | solution.py:452
  22.6 0.1 reduce_sum.24
  22.7 0.0 copy-start
  22.7 0.0 copy-start.1
  22.7 0.0 copy-start.2
  22.7 19.3 %all_to_all.21 = bf16[8,64,256]{2,1,0:T(8,128)(2,1)S(1)} all-to-all(bf16[8,64,256]{2,1,0:T(8,128)(2,1)S(1)} %broadcast_in_dim.9), channel_id=1, replica_groups={{0,2,4,6,32,34,36,38},{1,3,5,7,33,35,37,39},{8,10,12,14,40,42,44,46},{9..., dimensions={0} | all-to-all | bytes 524288 | tf_op jit(solution)/shard_map/all_to_all | solution.py:454
  42.1 13.6 %all_to_all.22 = bf16[16,64,256]{2,1,0:T(8,128)(2,1)S(1)} all-to-all(bf16[16,64,256]{2,1,0:T(8,128)(2,1)S(1)} %broadcast_in_dim.10), channel_id=1, replica_groups={{0,8,16,24,64,72,80,88,128,136,144,152,192,200,208,216},{32,40,48,56,96..., dimensions={0} | all-to-all | bytes 1048576 | tf_op jit(solution)/shard_map/all_to_all | solution.py:456
  55.7 0.0 collective-permute-start.1
  55.7 1.9 %collective-permute-done.1.other_ref = bf16[1024,256]{1,0:T(8,128)(2,1)S(1)} collective-permute-done((bf16[1024,256]{1,0:T(8,128)(2,1)S(1)}, bf16[1024,256]{1,0:T(8,128)(2,1)S(1)}, u32[]{:S(2)}, u32[]{:S(2)}) %collective-permute-start.1) | collective-permute-done | bytes 524320 | tf_op jit(solution)/shard_map/ppermute | solution.py:458
  57.6 18.8 %score.1 = f32[2,8,2,4,256]{4,3,2,1,0:T(4,128)S(1)} custom-call(bf16[1024,256]{1,0:T(8,128)(2,1)S(1)} %bitcast.11, bf16[1024,256]{1,0:T(8,128)(2,1)S(1)} %collective-permute-done.1.other_ref, bf16[2,8,480,256]{3,2,1,0:T(8,128)(2,1)} %bitcast.16), custom_call_target="tpu_custom_call" | custom-call | tf_op jit(solution)/shard_map/score/pallas_call | solution.py:304
  76.3 11.3 %all_to_all.23 = f32[16,2,4,256]{3,2,1,0:T(4,128)S(1)} all-to-all(f32[16,2,4,256]{3,2,1,0:T(4,128)S(1)} %bitcast.12), channel_id=1, replica_groups={{0,1,2,3,4,5,6,7,32,33,34,35,36,37,38,39},{8,9,10,11,12,13,14,15,40,41,..., dimensions={0} | all-to-all | bytes 262144 | tf_op jit(solution)/shard_map/all_to_all | solution.py:462
  87.7 0.1 merge.1
  87.7 2.5 %collective-permute-start.2 = (f32[4,256]{1,0:T(4,128)S(1)}, f32[4,256]{1,0:T(4,128)S(1)}, u32[]{:S(2)}, u32[]{:S(2)}) collective-permute-start(f32[4,256]{1,0:T(4,128)S(1)} %get-tuple-element.14), channel_id=1, source_target_pairs={{0,24},{8,16},{16,8},{24,64},{40,48},{48,40},{56,32},{64,88},{72,8... | collective-permute-start | bytes 12296 | tf_op jit(solution)/shard_map/ppermute | solution.py:464
  90.3 0.5 collective-permute-start.3
  90.8 0.0 copy-done
  90.8 0.0 copy-done.1
  90.8 0.0 copy-done.2
  90.8 0.1 prepare.1
  90.9 4.5 %collective-permute-done.2.far_ref = f32[4,256]{1,0:T(4,128)S(1)} collective-permute-done((f32[4,256]{1,0:T(4,128)S(1)}, f32[4,256]{1,0:T(4,128)S(1)}, u32[]{:S(2)}, u32[]{:S(2)}) %collective-permute-start.2) | collective-permute-done | bytes 4128 | tf_op jit(solution)/shard_map/ppermute | solution.py:464
  95.3 0.0 collective-permute-done.3.near_ref
  95.4 1.1 %refine.1 = f32[3,2,256]{2,1,0:T(2,128)} custom-call(f32[4,256]{1,0:T(4,128)S(1)} %collective-permute-done.2.far_ref, f32[2,4,256]{2,1,0:T(4,128)S(1)} %get-tuple-element.15.inputs_ref, f32[4,256]{1,0:T(4,128)S(1)} %collective-permute-done.3.near_ref, bf16[256,128]{1,0:T(8,128)(2,1)S(1)} %get-tuple-element.17.taps_ref, ...), custom_call_target="tpu_custom_call" | custom-call | tf_op jit(solution)/shard_map/refine/pallas_call | solution.py:430
  (3 shorter events, 0.1 us)
Async XLA Ops:
  3.0 2.0 %collective-permute-start = (bf16[1024,256]{1,0:T(8,128)(2,1)S(1)}, bf16[1024,256]{1,0:T(8,128)(2,1)S(1)}, u32[]{:S(2)}, u32[]{:S(2)}) collective-permute-start(bf16[1024,256]{1,0:T(8,128)(2,1)S(1)} %get-tuple-element.13), channel_id=1, source_target_pairs={{0,1},{1,0},{2,3},{3,2},{4,5},{5,4},{6,7},{7,6},{8,9},{9,8},{10,11... | collective-permute-start | bytes 1572872 | tf_op jit(solution)/shard_map/ppermute | solution.py:449
  22.7 68.1 %copy-start = (f32[3,4,256]{2,1,0:T(4,128)S(1)}, f32[3,4,256]{2,1,0:T(4,128)}, u32[]{:S(2)}) copy-start(f32[3,4,256]{2,1,0:T(4,128)} %weight_ref.1) | copy-start | bytes 36868
  22.7 68.1 %copy-start.1 = (f32[3,256]{1,0:T(4,128)S(1)}, f32[3,256]{1,0:T(4,128)}, u32[]{:S(2)}) copy-start(f32[3,256]{1,0:T(4,128)} %out_weight_ref.1) | copy-start | bytes 9220
  22.7 68.1 %copy-start.2 = (f32[256]{0:T(256)S(1)}, f32[256]{0:T(256)}, u32[]{:S(2)}) copy-start(f32[256]{0:T(256)} %param.12) | copy-start | bytes 3076
  55.7 1.9 %collective-permute-start.1 = (bf16[1024,256]{1,0:T(8,128)(2,1)S(1)}, bf16[1024,256]{1,0:T(8,128)(2,1)S(1)}, u32[]{:S(2)}, u32[]{:S(2)}) collective-permute-start(bf16[1024,256]{1,0:T(8,128)(2,1)S(1)} %bitcast.10), channel_id=1, source_target_pairs={{0,1},{1,0},{2,3},{3,2},{4,5},{5,4},{6,7},{7,6},{8,9},{9,8},{10,11... | collective-permute-start | bytes 1572872 | tf_op jit(solution)/shard_map/ppermute | solution.py:458
  87.7 7.6 %collective-permute-start.2 = (f32[4,256]{1,0:T(4,128)S(1)}, f32[4,256]{1,0:T(4,128)S(1)}, u32[]{:S(2)}, u32[]{:S(2)}) collective-permute-start(f32[4,256]{1,0:T(4,128)S(1)} %get-tuple-element.14), channel_id=1, source_target_pairs={{0,24},{8,16},{16,8},{24,64},{40,48},{48,40},{56,32},{64,88},{72,8... | collective-permute-start | bytes 12296 | tf_op jit(solution)/shard_map/ppermute | solution.py:464
  90.3 5.1 %collective-permute-start.3 = (f32[4,256]{1,0:T(4,128)S(1)}, f32[4,256]{1,0:T(4,128)S(1)}, u32[]{:S(2)}, u32[]{:S(2)}) collective-permute-start(f32[4,256]{1,0:T(4,128)S(1)} %get-tuple-element.16), channel_id=1, source_target_pairs={{0,8},{8,0},{16,24},{24,16},{32,40},{40,32},{48,56},{56,48},{64,72... | collective-permute-start | bytes 12296 | tf_op jit(solution)/shard_map/ppermute | solution.py:465

commit v7 on v6

--- a/solution.py
+++ b/solution.py
@@ -144,22 +144,11 @@
 UNITS = 2
 
 
-def score_kernel(own_ref, other_ref, feat_ref, out_ref, fbuf, even, odd, sems):
+def score_kernel(own_ref, other_ref, fbuf, out_ref, even, odd):
     tile_idx = lax.axis_index("tile")
     core = tile_idx % 2
     frames, rows_here = fbuf.shape[0], fbuf.shape[1]
     cols = W // PARTS
-    loads = [
-        [
-            pltpu.make_async_copy(
-                feat_ref.at[f, :, pl.ds(i * cols, cols), :], fbuf.at[f, :, pl.ds(i * cols, cols), :], sems.at[f, i]
-            )
-            for i in range(PARTS)
-        ]
-        for f in range(frames)
-    ]
-    for load in loads[0] + loads[1]:
-        load.start()
     half_blocks = own_ref.shape[0] // BLOCK
     blocks = 2 * half_blocks
     pairs = blocks // UNITS
@@ -247,14 +236,10 @@
 
         none, fresh = (low,) * UNITS, ((zero, zero, zero),) * UNITS
         stage(0)
-        loads[0][0].wait()
         tops, peaks, sums = None, None, None
         for step in range(steps + 2):
             f = step // pairs if step < steps else None
             new, old = (even, odd) if step % 2 == 0 else (odd, even)
-            if step == pairs:
-                for load in loads[1]:
-                    load.wait()
             last_peaks = peaks
             tops = None if tops is None else list(tops)
             sums = None if sums is None else [list(x) for x in sums]
@@ -275,10 +260,6 @@
 
             def part_of(i, state):
                 tops, sums = state
-                if step == 0:
-                    pltpu.make_async_copy(
-                        feat_ref.at[0, :, pl.ds(0, cols), :], fbuf.at[0, :, pl.ds(0, cols), :], sems.at[0, i]
-                    ).wait()
                 tops, sums = list(tops), [list(x) for x in sums]
                 bound = None if peaks is None else list(peaks)
                 weave(
@@ -296,6 +277,26 @@
     )
 
 
+def fetch_kernel(feat_ref, own_ref, out_ref, sem):
+    load = pltpu.make_async_copy(feat_ref, out_ref, sem)
+    load.start()
+    load.wait()
+
+
+def fetch(features, own):
+    hbm = pl.BlockSpec(memory_space=pltpu.MemorySpace.HBM)
+    return pl.pallas_call(
+        fetch_kernel,
+        out_shape=jax.ShapeDtypeStruct(features.shape, features.dtype),
+        in_specs=[hbm, pl.BlockSpec(memory_space=pl.ANY)],
+        out_specs=pl.BlockSpec(memory_space=pltpu.VMEM),
+        scratch_shapes=[pltpu.SemaphoreType.DMA],
+        compiler_params=pltpu.CompilerParams(vmem_limit_bytes=47 << 20),
+        cost_estimate=pl.CostEstimate(flops=0, bytes_accessed=4 << 20, transcendentals=0),
+        name="fetch",
+    )(features, own)
+
+
 def score(own, other, features, rows_here):
     frames, pix_count, chan = features.shape
     blocks = 2 * own.shape[0] // BLOCK
@@ -304,15 +305,10 @@
     return pl.pallas_call(
         score_kernel,
         out_shape=jax.ShapeDtypeStruct((2, blocks, frames, 4, BLOCK), jnp.float32),
-        in_specs=[vmem, vmem, pl.BlockSpec(memory_space=pltpu.MemorySpace.HBM)],
+        in_specs=[vmem, vmem, vmem],
         out_specs=vmem,
-        scratch_shapes=[
-            pltpu.VMEM((frames, rows_here, W, chan), features.dtype),
-            kept,
-            kept,
-            pltpu.SemaphoreType.DMA((frames, PARTS)),
-        ],
-        compiler_params=pltpu.CompilerParams(vmem_limit_bytes=51 << 20),
+        scratch_shapes=[kept, kept],
+        compiler_params=pltpu.CompilerParams(vmem_limit_bytes=24 << 20),
         name="score",
     )(own, other, features.reshape(frames, rows_here, W, chan))
 
@@ -456,7 +452,7 @@
     got = lax.all_to_all(jnp.broadcast_to(piece, (wide, rows, chan)), "frame", 0, 0, axis_index_groups=plane)
     own = got.reshape(wide * rows, chan)
     other = lax.ppermute(own, "tile", swap)
-    parts = score(own, other, features, rows_here)
+    parts = score(own, other, fetch(features, own), rows_here)
     members = 2 * tiles
     shape = parts.shape
     parts = lax.all_to_all(parts.reshape(members, *shape[2:]), BOTH, 0, 0, axis_index_groups=tower)

time: 97.5 us -> 96.5 us (0.990)
  waiting for transfers between devices: 7.95 us -> 6.36 us
  Pallas kernels: 22.2 us -> 23.7 us
    pallas_call x0 -> x1, Pallas kernels: none -> 2.12 us  [fetch(): pl.pallas_call(fetch_kernel, out_shape=jax.ShapeDtypeStruct(features.shap...]
    ppermute x1, waiting for transfers between devices: 1.91 us -> 0.01 us  [local(): other = lax.ppermute(own, 'tile', swap)]
    pallas_call x1, Pallas kernels: 18.8 us -> 17.7 us  [score(): pl.pallas_call(score_kernel, out_shape=jax.ShapeDtypeStruct((2, blocks, f...]
  transfers between devices with their start and end apart: 4 -> 4, of which waited for: 3 -> 2; matrix products, arithmetic and copies ran while one was open for 0% -> 0% of each run, Pallas kernels for 0% -> 2%
where the time goes in v7:
time: 96.5 us; the launch traced here: 95.5 us
  blocking collectives  61.1 us (63%)
  Pallas kernels  23.7 us (25%)
  waiting for transfers between devices  6.36 us (7%)
  starting transfers between devices  3.12 us (3%)
  other arithmetic  1 us (1%)
    all_to_all x1, blocking collectives, local(): lax.all_to_all(jnp.broadcast_to(piece, (tall, rows, chan)), BOTH, 0, 0, a...  18.8 us
    pallas_call x1, Pallas kernels, score(): pl.pallas_call(score_kernel, out_shape=jax.ShapeDtypeStruct((2, blocks, f...  17.7 us
    all_to_all x1, blocking collectives, local(): lax.all_to_all(mine.reshape(wide, rows, chan), 'frame', 0, 0, axis_index_...  17.4 us
    all_to_all x1, blocking collectives, local(): lax.all_to_all(jnp.broadcast_to(piece, (wide, rows, chan)), 'frame', 0, 0...  13.6 us
    all_to_all x1, blocking collectives, local(): lax.all_to_all(parts.reshape(members, *shape[2:]), BOTH, 0, 0, axis_index...  11.3 us
    ppermute x1, waiting for transfers between devices, local(): far = lax.ppermute(far, 'frame', far_pairs())  4.46 us
    pallas_call x1, Pallas kernels, pick(): pl.pallas_call(functools.partial(pick_kernel, rows_here), out_shape=(half...  2.61 us
    ppermute x1, starting transfers between devices, local(): far = lax.ppermute(far, 'frame', far_pairs())  2.54 us
  transfers between devices with their start and end apart: 4, of which 2 were waited for; matrix products, arithmetic and copies ran while one was open for 0% of the time, Pallas kernels for 2%

profile of v7, /device:TPU:6, one launch (start us, length us, event | category | flops | bytes accessed | tf_op | source)
XLA Modules:
  0.0 95.5 jit_solution(11690314645242971308)
XLA Ops:
  0.0 0.7 add_bitcast_fusion.idx_ref
  0.7 2.6 %pick.1 = (bf16[1024,256]{1,0:T(8,128)(2,1)S(1)}, bf16[1024,256]{1,0:T(8,128)(2,1)S(1)}) custom-call(s32[16,128]{1,0:T(8,128)S(1)} %add_bitcast_fusion.idx_ref, bf16[7680,256]{1,0:T(8,128)(2,1)} %bitcast.17), custom_call_target="tpu_custom_call" | custom-call | tf_op jit(solution)/shard_map/pick/pallas_call | solution.py:122
  3.4 0.1 collective-permute-start
  3.5 1.9 %collective-permute-done = bf16[1024,256]{1,0:T(8,128)(2,1)S(1)} collective-permute-done((bf16[1024,256]{1,0:T(8,128)(2,1)S(1)}, bf16[1024,256]{1,0:T(8,128)(2,1)S(1)}, u32[]{:S(2)}, u32[]{:S(2)}) %collective-permute-start) | collective-permute-done | bytes 524320 | tf_op jit(solution)/shard_map/ppermute | solution.py:445
  5.4 0.1 add.11
  5.5 17.4 %all_to_all.20 = bf16[16,64,256]{2,1,0:T(8,128)(2,1)S(1)} all-to-all(bf16[16,64,256]{2,1,0:T(8,128)(2,1)S(1)} %bitcast.18), channel_id=1, replica_groups={{0,8,16,24,64,72,80,88,128,136,144,152,192,200,208,216},{32,40,48,56,96..., dimensions={0} | all-to-all | bytes 1048576 | tf_op jit(solution)/shard_map/all_to_all | solution.py:448
  22.9 0.1 reduce_sum.24
  23.0 18.8 %all_to_all.21 = bf16[8,64,256]{2,1,0:T(8,128)(2,1)S(1)} all-to-all(bf16[8,64,256]{2,1,0:T(8,128)(2,1)S(1)} %broadcast_in_dim.9), channel_id=1, replica_groups={{0,2,4,6,32,34,36,38},{1,3,5,7,33,35,37,39},{8,10,12,14,40,42,44,46},{9..., dimensions={0} | all-to-all | bytes 524288 | tf_op jit(solution)/shard_map/all_to_all | solution.py:450
  41.9 13.6 %all_to_all.22 = bf16[16,64,256]{2,1,0:T(8,128)(2,1)S(1)} all-to-all(bf16[16,64,256]{2,1,0:T(8,128)(2,1)S(1)} %broadcast_in_dim.10), channel_id=1, replica_groups={{0,8,16,24,64,72,80,88,128,136,144,152,192,200,208,216},{32,40,48,56,96..., dimensions={0} | all-to-all | bytes 1048576 | tf_op jit(solution)/shard_map/all_to_all | solution.py:452
  55.5 0.0 collective-permute-start.1
  55.5 2.1 %fetch.1 = bf16[2,3840,256]{2,1,0:T(8,128)(2,1)S(1)} custom-call(bf16[2,3840,256]{2,1,0:T(8,128)(2,1)} %feat_ref.1, bf16[1024,256]{1,0:T(8,128)(2,1)S(1)} %bitcast.12), custom_call_target="tpu_custom_call" | custom-call | bytes 4194304 | tf_op jit(solution)/shard_map/fetch/pallas_call | solution.py:288
  57.7 0.0 copy-start
  57.7 0.0 copy-start.1
  57.7 0.0 copy-start.2
  57.7 0.0 collective-permute-done.1.other_ref
  57.7 17.7 %score.1 = f32[2,8,2,4,256]{4,3,2,1,0:T(4,128)S(1)} custom-call(bf16[1024,256]{1,0:T(8,128)(2,1)S(1)} %bitcast.13, bf16[1024,256]{1,0:T(8,128)(2,1)S(1)} %collective-permute-done.1.other_ref, bf16[2,8,480,256]{3,2,1,0:T(8,128)(2,1)S(1)} %bitcast.10), custom_call_target="tpu_custom_call" | custom-call | tf_op jit(solution)/shard_map/score/pallas_call | solution.py:305
  75.4 11.3 %all_to_all.23 = f32[16,2,4,256]{3,2,1,0:T(4,128)S(1)} all-to-all(f32[16,2,4,256]{3,2,1,0:T(4,128)S(1)} %bitcast.14), channel_id=1, replica_groups={{0,1,2,3,4,5,6,7,32,33,34,35,36,37,38,39},{8,9,10,11,12,13,14,15,40,41,..., dimensions={0} | all-to-all | bytes 262144 | tf_op jit(solution)/shard_map/all_to_all | solution.py:458
  86.7 0.1 merge.1
  86.8 2.5 %collective-permute-start.2 = (f32[4,256]{1,0:T(4,128)S(1)}, f32[4,256]{1,0:T(4,128)S(1)}, u32[]{:S(2)}, u32[]{:S(2)}) collective-permute-start(f32[4,256]{1,0:T(4,128)S(1)} %get-tuple-element.14), channel_id=1, source_target_pairs={{0,24},{8,16},{16,8},{24,64},{40,48},{48,40},{56,32},{64,88},{72,8... | collective-permute-start | bytes 12296 | tf_op jit(solution)/shard_map/ppermute | solution.py:460
  89.4 0.5 collective-permute-start.3
  89.8 0.0 copy-done
  89.9 0.0 copy-done.1
  89.9 0.0 copy-done.2
  89.9 0.1 prepare.1
  90.0 4.5 %collective-permute-done.2.far_ref = f32[4,256]{1,0:T(4,128)S(1)} collective-permute-done((f32[4,256]{1,0:T(4,128)S(1)}, f32[4,256]{1,0:T(4,128)S(1)}, u32[]{:S(2)}, u32[]{:S(2)}) %collective-permute-start.2) | collective-permute-done | bytes 4128 | tf_op jit(solution)/shard_map/ppermute | solution.py:460
  94.4 0.0 collective-permute-done.3.near_ref
  94.4 1.1 %refine.1 = f32[3,2,256]{2,1,0:T(2,128)} custom-call(f32[4,256]{1,0:T(4,128)S(1)} %collective-permute-done.2.far_ref, f32[2,4,256]{2,1,0:T(4,128)S(1)} %get-tuple-element.15.inputs_ref, f32[4,256]{1,0:T(4,128)S(1)} %collective-permute-done.3.near_ref, bf16[256,128]{1,0:T(8,128)(2,1)S(1)} %get-tuple-element.17.taps_ref, ...), custom_call_target="tpu_custom_call" | custom-call | tf_op jit(solution)/shard_map/refine/pallas_call | solution.py:426
  (3 shorter events, 0.1 us)
Async XLA Ops:
  3.4 2.0 %collective-permute-start = (bf16[1024,256]{1,0:T(8,128)(2,1)S(1)}, bf16[1024,256]{1,0:T(8,128)(2,1)S(1)}, u32[]{:S(2)}, u32[]{:S(2)}) collective-permute-start(bf16[1024,256]{1,0:T(8,128)(2,1)S(1)} %get-tuple-element.13), channel_id=1, source_target_pairs={{0,1},{1,0},{2,3},{3,2},{4,5},{5,4},{6,7},{7,6},{8,9},{9,8},{10,11... | collective-permute-start | bytes 1572872 | tf_op jit(solution)/shard_map/ppermute | solution.py:445
  55.5 2.2 %collective-permute-start.1 = (bf16[1024,256]{1,0:T(8,128)(2,1)S(1)}, bf16[1024,256]{1,0:T(8,128)(2,1)S(1)}, u32[]{:S(2)}, u32[]{:S(2)}) collective-permute-start(bf16[1024,256]{1,0:T(8,128)(2,1)S(1)} %bitcast.11), channel_id=1, source_target_pairs={{0,1},{1,0},{2,3},{3,2},{4,5},{5,4},{6,7},{7,6},{8,9},{9,8},{10,11... | collective-permute-start | bytes 1572872 | tf_op jit(solution)/shard_map/ppermute | solution.py:454
  57.7 32.2 %copy-start = (f32[3,4,256]{2,1,0:T(4,128)S(1)}, f32[3,4,256]{2,1,0:T(4,128)}, u32[]{:S(2)}) copy-start(f32[3,4,256]{2,1,0:T(4,128)} %weight_ref.1) | copy-start | bytes 36868
  57.7 32.2 %copy-start.1 = (f32[3,256]{1,0:T(4,128)S(1)}, f32[3,256]{1,0:T(4,128)}, u32[]{:S(2)}) copy-start(f32[3,256]{1,0:T(4,128)} %out_weight_ref.1) | copy-start | bytes 9220
  57.7 32.2 %copy-start.2 = (f32[256]{0:T(256)S(1)}, f32[256]{0:T(256)}, u32[]{:S(2)}) copy-start(f32[256]{0:T(256)} %param.12) | copy-start | bytes 3076
  86.8 7.6 %collective-permute-start.2 = (f32[4,256]{1,0:T(4,128)S(1)}, f32[4,256]{1,0:T(4,128)S(1)}, u32[]{:S(2)}, u32[]{:S(2)}) collective-permute-start(f32[4,256]{1,0:T(4,128)S(1)} %get-tuple-element.14), channel_id=1, source_target_pairs={{0,24},{8,16},{16,8},{24,64},{40,48},{48,40},{56,32},{64,88},{72,8... | collective-permute-start | bytes 12296 | tf_op jit(solution)/shard_map/ppermute | solution.py:460
  89.4 5.1 %collective-permute-start.3 = (f32[4,256]{1,0:T(4,128)S(1)}, f32[4,256]{1,0:T(4,128)S(1)}, u32[]{:S(2)}, u32[]{:S(2)}) collective-permute-start(f32[4,256]{1,0:T(4,128)S(1)} %get-tuple-element.16), channel_id=1, source_target_pairs={{0,8},{8,0},{16,24},{24,16},{32,40},{40,32},{48,56},{56,48},{64,72... | collective-permute-start | bytes 12296 | tf_op jit(solution)/shard_map/ppermute | solution.py:461

commit v8 on v7

--- a/solution.py
+++ b/solution.py
@@ -144,10 +144,12 @@
 UNITS = 2
 
 
-def score_kernel(own_ref, other_ref, fbuf, out_ref, even, odd):
+def score_kernel(own_ref, other_ref, first_ref, feat_ref, out_ref, rest, even, odd, sem):
     tile_idx = lax.axis_index("tile")
     core = tile_idx % 2
-    frames, rows_here = fbuf.shape[0], fbuf.shape[1]
+    load = pltpu.make_async_copy(feat_ref.at[pl.ds(1, rest.shape[0])], rest, sem)
+    load.start()
+    frames, rows_here = 1 + rest.shape[0], rest.shape[1]
     cols = W // PARTS
     half_blocks = own_ref.shape[0] // BLOCK
     blocks = 2 * half_blocks
@@ -175,7 +177,8 @@
                         tops[m] = jnp.maximum(tops[m], jnp.max(scores.reshape(cols // 8, 8, BLOCK), axis=0))
                         seen.append(scores[cols - 8 : cols, :])
                 if f is not None:
-                    lhs = fbuf[f, r, pl.ds(pl.multiple_of(part * cols, 16), cols), :]
+                    at = pl.ds(pl.multiple_of(part * cols, 16), cols)
+                    lhs = first_ref[r, at, :] if f == 0 else rest[f - 1, r, at, :]
                     for m in range(UNITS):
                         pltpu.matmul_acc_lhs(accs[m * rows_here + r], lhs, load_staged_rhs=staged if r == 0 else None)
                 yield seen
@@ -183,7 +186,7 @@
         def weighs(kept, part, peaks, sums):
             start = jnp.asarray(part * cols).astype(jnp.float32)
             here, across = [None] * UNITS, [None] * UNITS
-            for k in range(cols // 8):
+            for k in reversed(range(cols // 8)):
                 for m in range(UNITS):
                     tail, below = None, None
                     for r in reversed(range(rows_here)):
@@ -195,12 +198,11 @@
                     sums[m][2] = sums[m][2] + below
                     here[m] = tail if here[m] is None else here[m] + tail
                     if k > 0:
-                        shifted = tail * float(k * 8)
-                        across[m] = shifted if across[m] is None else across[m] + shifted
+                        across[m] = here[m] if across[m] is None else across[m] + here[m]
                     yield
             for m in range(UNITS):
                 sums[m][0] = sums[m][0] + here[m]
-                sums[m][1] = sums[m][1] + (across[m] + here[m] * (sub + start))
+                sums[m][1] = sums[m][1] + (across[m] * 8.0 + here[m] * (sub + start))
 
         def weave(moving, weighing, peaks):
             per = (cols // 8) * UNITS // rows_here
@@ -208,9 +210,9 @@
                 moving = iter(())
             if weighing is None:
                 weighing = iter(())
-            for _ in range(rows_here):
+            for turn in range(rows_here):
                 seen = next(moving, None)
-                if seen is not None and peaks is not None:
+                if seen is not None and peaks is not None and turn % 4 == 0:
                     for m in range(UNITS):
                         peaks[m] = jnp.minimum(peaks[m], jnp.maximum(peaks[m], seen[m]))
                 for _ in range(per):
@@ -240,6 +242,8 @@
         for step in range(steps + 2):
             f = step // pairs if step < steps else None
             new, old = (even, odd) if step % 2 == 0 else (odd, even)
+            if step == pairs:
+                load.wait()
             last_peaks = peaks
             tops = None if tops is None else list(tops)
             sums = None if sums is None else [list(x) for x in sums]
@@ -278,7 +282,7 @@
 
 
 def fetch_kernel(feat_ref, own_ref, out_ref, sem):
-    load = pltpu.make_async_copy(feat_ref, out_ref, sem)
+    load = pltpu.make_async_copy(feat_ref.at[0], out_ref, sem)
     load.start()
     load.wait()
 
@@ -287,17 +291,17 @@
     hbm = pl.BlockSpec(memory_space=pltpu.MemorySpace.HBM)
     return pl.pallas_call(
         fetch_kernel,
-        out_shape=jax.ShapeDtypeStruct(features.shape, features.dtype),
+        out_shape=jax.ShapeDtypeStruct(features.shape[1:], features.dtype),
         in_specs=[hbm, pl.BlockSpec(memory_space=pl.ANY)],
         out_specs=pl.BlockSpec(memory_space=pltpu.VMEM),
         scratch_shapes=[pltpu.SemaphoreType.DMA],
-        compiler_params=pltpu.CompilerParams(vmem_limit_bytes=47 << 20),
+        compiler_params=pltpu.CompilerParams(vmem_limit_bytes=49 << 20),
         cost_estimate=pl.CostEstimate(flops=0, bytes_accessed=4 << 20, transcendentals=0),
         name="fetch",
     )(features, own)
 
 
-def score(own, other, features, rows_here):
+def score(own, other, first, features, rows_here):
     frames, pix_count, chan = features.shape
     blocks = 2 * own.shape[0] // BLOCK
     vmem = pl.BlockSpec(memory_space=pltpu.VMEM)
@@ -305,12 +309,17 @@
     return pl.pallas_call(
         score_kernel,
         out_shape=jax.ShapeDtypeStruct((2, blocks, frames, 4, BLOCK), jnp.float32),
-        in_specs=[vmem, vmem, vmem],
+        in_specs=[vmem, vmem, vmem, pl.BlockSpec(memory_space=pltpu.MemorySpace.HBM)],
         out_specs=vmem,
-        scratch_shapes=[kept, kept],
-        compiler_params=pltpu.CompilerParams(vmem_limit_bytes=24 << 20),
+        scratch_shapes=[
+            pltpu.VMEM((frames - 1, rows_here, W, chan), features.dtype),
+            kept,
+            kept,
+            pltpu.SemaphoreType.DMA,
+        ],
+        compiler_params=pltpu.CompilerParams(vmem_limit_bytes=49 << 20),
         name="score",
-    )(own, other, features.reshape(frames, rows_here, W, chan))
+    )(own, other, first.reshape(rows_here, W, chan), features.reshape(frames, rows_here, W, chan))
 
 
 def merge_kernel(pixels, parts_ref, inputs_ref, far_ref, near_ref):
@@ -452,7 +461,7 @@
     got = lax.all_to_all(jnp.broadcast_to(piece, (wide, rows, chan)), "frame", 0, 0, axis_index_groups=plane)
     own = got.reshape(wide * rows, chan)
     other = lax.ppermute(own, "tile", swap)
-    parts = score(own, other, fetch(features, own), rows_here)
+    parts = score(own, other, fetch(features, own), features, rows_here)
     members = 2 * tiles
     shape = parts.shape
     parts = lax.all_to_all(parts.reshape(members, *shape[2:]), BOTH, 0, 0, axis_index_groups=tower)

time: 96.5 us -> 96 us (level)
  transfers between devices with their start and end apart: 4 -> 4, of which waited for: 2 -> 3; matrix products, arithmetic and copies ran while one was open for 0% -> 0% of each run, Pallas kernels for 2% -> 2%
where the time goes in v8:
time: 96 us; the launch traced here: 94.7 us
  blocking collectives  60.8 us (63%)
  Pallas kernels  23 us (24%)
  waiting for transfers between devices  6.67 us (7%)
  starting transfers between devices  3.12 us (3%)
  other arithmetic  1 us (1%)
    all_to_all x1, blocking collectives, local(): lax.all_to_all(jnp.broadcast_to(piece, (tall, rows, chan)), BOTH, 0, 0, a...  18.2 us
    all_to_all x1, blocking collectives, local(): lax.all_to_all(mine.reshape(wide, rows, chan), 'frame', 0, 0, axis_index_...  17.7 us
    pallas_call x1, Pallas kernels, score(): pl.pallas_call(score_kernel, out_shape=jax.ShapeDtypeStruct((2, blocks, f...  17.4 us
    all_to_all x1, blocking collectives, local(): lax.all_to_all(jnp.broadcast_to(piece, (wide, rows, chan)), 'frame', 0, 0...  13.6 us
    all_to_all x1, blocking collectives, local(): lax.all_to_all(parts.reshape(members, *shape[2:]), BOTH, 0, 0, axis_index...  11.3 us
    ppermute x1, waiting for transfers between devices, local(): far = lax.ppermute(far, 'frame', far_pairs())  4.46 us
    pallas_call x1, Pallas kernels, pick(): pl.pallas_call(functools.partial(pick_kernel, rows_here), out_shape=(half...  2.68 us
    ppermute x1, starting transfers between devices, local(): far = lax.ppermute(far, 'frame', far_pairs())  2.54 us
  transfers between devices with their start and end apart: 4, of which 3 were waited for; matrix products, arithmetic and copies ran while one was open for 0% of the time, Pallas kernels for 2%

profile of v8, /device:TPU:6, one launch (start us, length us, event | category | flops | bytes accessed | tf_op | source)
XLA Modules:
  0.0 94.7 jit_solution(12891946349215214852)
XLA Ops:
  0.0 0.7 add_bitcast_fusion.idx_ref
  0.7 2.7 %pick.1 = (bf16[1024,256]{1,0:T(8,128)(2,1)S(1)}, bf16[1024,256]{1,0:T(8,128)(2,1)S(1)}) custom-call(s32[16,128]{1,0:T(8,128)S(1)} %add_bitcast_fusion.idx_ref, bf16[7680,256]{1,0:T(8,128)(2,1)} %bitcast.18), custom_call_target="tpu_custom_call" | custom-call | tf_op jit(solution)/shard_map/pick/pallas_call | solution.py:122
  3.4 0.1 collective-permute-start
  3.5 1.9 %collective-permute-done = bf16[1024,256]{1,0:T(8,128)(2,1)S(1)} collective-permute-done((bf16[1024,256]{1,0:T(8,128)(2,1)S(1)}, bf16[1024,256]{1,0:T(8,128)(2,1)S(1)}, u32[]{:S(2)}, u32[]{:S(2)}) %collective-permute-start) | collective-permute-done | bytes 524320 | tf_op jit(solution)/shard_map/ppermute | solution.py:454
  5.4 0.1 add.11
  5.6 17.7 %all_to_all.20 = bf16[16,64,256]{2,1,0:T(8,128)(2,1)S(1)} all-to-all(bf16[16,64,256]{2,1,0:T(8,128)(2,1)S(1)} %bitcast.20), channel_id=1, replica_groups={{0,8,16,24,64,72,80,88,128,136,144,152,192,200,208,216},{32,40,48,56,96..., dimensions={0} | all-to-all | bytes 1048576 | tf_op jit(solution)/shard_map/all_to_all | solution.py:457
  23.3 0.1 reduce_sum.24
  23.4 18.2 %all_to_all.21 = bf16[8,64,256]{2,1,0:T(8,128)(2,1)S(1)} all-to-all(bf16[8,64,256]{2,1,0:T(8,128)(2,1)S(1)} %broadcast_in_dim.9), channel_id=1, replica_groups={{0,2,4,6,32,34,36,38},{1,3,5,7,33,35,37,39},{8,10,12,14,40,42,44,46},{9..., dimensions={0} | all-to-all | bytes 524288 | tf_op jit(solution)/shard_map/all_to_all | solution.py:459
  41.7 13.6 %all_to_all.22 = bf16[16,64,256]{2,1,0:T(8,128)(2,1)S(1)} all-to-all(bf16[16,64,256]{2,1,0:T(8,128)(2,1)S(1)} %broadcast_in_dim.10), channel_id=1, replica_groups={{0,8,16,24,64,72,80,88,128,136,144,152,192,200,208,216},{32,40,48,56,96..., dimensions={0} | all-to-all | bytes 1048576 | tf_op jit(solution)/shard_map/all_to_all | solution.py:461
  55.3 0.0 collective-permute-start.1
  55.3 1.6 %fetch.1 = bf16[3840,256]{1,0:T(8,128)(2,1)S(1)} custom-call(bf16[2,3840,256]{2,1,0:T(8,128)(2,1)} %feat_ref.1, bf16[1024,256]{1,0:T(8,128)(2,1)S(1)} %bitcast.13), custom_call_target="tpu_custom_call" | custom-call | bytes 4194304 | tf_op jit(solution)/shard_map/fetch/pallas_call | solution.py:292
  56.8 0.0 copy-start
  56.8 0.0 copy-start.1
  56.9 0.0 copy-start.2
  56.9 0.3 collective-permute-done.1.other_ref
  57.2 17.4 %score.1 = f32[2,8,2,4,256]{4,3,2,1,0:T(4,128)S(1)} custom-call(bf16[1024,256]{1,0:T(8,128)(2,1)S(1)} %bitcast.14, bf16[1024,256]{1,0:T(8,128)(2,1)S(1)} %collective-permute-done.1.other_ref, bf16[8,480,256]{2,1,0:T(8,128)(2,1)S(1)} %bitcast.11, bf16[2,8,480,256]{3,2,1,0:T(8,128)(2,1)} %bitcast.19), custom_call_target="tpu_custom_call" | custom-call | tf_op jit(solution)/shard_map/score/pallas_call | solution.py:309
  74.6 11.3 %all_to_all.23 = f32[16,2,4,256]{3,2,1,0:T(4,128)S(1)} all-to-all(f32[16,2,4,256]{3,2,1,0:T(4,128)S(1)} %bitcast.15), channel_id=1, replica_groups={{0,1,2,3,4,5,6,7,32,33,34,35,36,37,38,39},{8,9,10,11,12,13,14,15,40,41,..., dimensions={0} | all-to-all | bytes 262144 | tf_op jit(solution)/shard_map/all_to_all | solution.py:467
  86.0 0.1 merge.1
  86.0 2.5 %collective-permute-start.2 = (f32[4,256]{1,0:T(4,128)S(1)}, f32[4,256]{1,0:T(4,128)S(1)}, u32[]{:S(2)}, u32[]{:S(2)}) collective-permute-start(f32[4,256]{1,0:T(4,128)S(1)} %get-tuple-element.14), channel_id=1, source_target_pairs={{0,24},{8,16},{16,8},{24,64},{40,48},{48,40},{56,32},{64,88},{72,8... | collective-permute-start | bytes 12296 | tf_op jit(solution)/shard_map/ppermute | solution.py:469
  88.6 0.5 collective-permute-start.3
  89.1 0.0 copy-done
  89.1 0.0 copy-done.1
  89.1 0.0 copy-done.2
  89.1 0.1 prepare.1
  89.2 4.5 %collective-permute-done.2.far_ref = f32[4,256]{1,0:T(4,128)S(1)} collective-permute-done((f32[4,256]{1,0:T(4,128)S(1)}, f32[4,256]{1,0:T(4,128)S(1)}, u32[]{:S(2)}, u32[]{:S(2)}) %collective-permute-start.2) | collective-permute-done | bytes 4128 | tf_op jit(solution)/shard_map/ppermute | solution.py:469
  93.6 0.0 collective-permute-done.3.near_ref
  93.6 1.1 %refine.1 = f32[3,2,256]{2,1,0:T(2,128)} custom-call(f32[4,256]{1,0:T(4,128)S(1)} %collective-permute-done.2.far_ref, f32[2,4,256]{2,1,0:T(4,128)S(1)} %get-tuple-element.15.inputs_ref, f32[4,256]{1,0:T(4,128)S(1)} %collective-permute-done.3.near_ref, bf16[256,128]{1,0:T(8,128)(2,1)S(1)} %get-tuple-element.17.taps_ref, ...), custom_call_target="tpu_custom_call" | custom-call | tf_op jit(solution)/shard_map/refine/pallas_call | solution.py:435
  (3 shorter events, 0.1 us)
Async XLA Ops:
  3.4 2.0 %collective-permute-start = (bf16[1024,256]{1,0:T(8,128)(2,1)S(1)}, bf16[1024,256]{1,0:T(8,128)(2,1)S(1)}, u32[]{:S(2)}, u32[]{:S(2)}) collective-permute-start(bf16[1024,256]{1,0:T(8,128)(2,1)S(1)} %get-tuple-element.13), channel_id=1, source_target_pairs={{0,1},{1,0},{2,3},{3,2},{4,5},{5,4},{6,7},{7,6},{8,9},{9,8},{10,11... | collective-permute-start | bytes 1572872 | tf_op jit(solution)/shard_map/ppermute | solution.py:454
  55.3 1.9 %collective-permute-start.1 = (bf16[1024,256]{1,0:T(8,128)(2,1)S(1)}, bf16[1024,256]{1,0:T(8,128)(2,1)S(1)}, u32[]{:S(2)}, u32[]{:S(2)}) collective-permute-start(bf16[1024,256]{1,0:T(8,128)(2,1)S(1)} %bitcast.12), channel_id=1, source_target_pairs={{0,1},{1,0},{2,3},{3,2},{4,5},{5,4},{6,7},{7,6},{8,9},{9,8},{10,11... | collective-permute-start | bytes 1572872 | tf_op jit(solution)/shard_map/ppermute | solution.py:463
  56.8 32.2 %copy-start = (f32[3,4,256]{2,1,0:T(4,128)S(1)}, f32[3,4,256]{2,1,0:T(4,128)}, u32[]{:S(2)}) copy-start(f32[3,4,256]{2,1,0:T(4,128)} %weight_ref.1) | copy-start | bytes 36868
  56.8 32.2 %copy-start.1 = (f32[3,256]{1,0:T(4,128)S(1)}, f32[3,256]{1,0:T(4,128)}, u32[]{:S(2)}) copy-start(f32[3,256]{1,0:T(4,128)} %out_weight_ref.1) | copy-start | bytes 9220
  56.9 32.2 %copy-start.2 = (f32[256]{0:T(256)S(1)}, f32[256]{0:T(256)}, u32[]{:S(2)}) copy-start(f32[256]{0:T(256)} %param.12) | copy-start | bytes 3076
  86.0 7.6 %collective-permute-start.2 = (f32[4,256]{1,0:T(4,128)S(1)}, f32[4,256]{1,0:T(4,128)S(1)}, u32[]{:S(2)}, u32[]{:S(2)}) collective-permute-start(f32[4,256]{1,0:T(4,128)S(1)} %get-tuple-element.14), channel_id=1, source_target_pairs={{0,24},{8,16},{16,8},{24,64},{40,48},{48,40},{56,32},{64,88},{72,8... | collective-permute-start | bytes 12296 | tf_op jit(solution)/shard_map/ppermute | solution.py:469
  88.6 5.1 %collective-permute-start.3 = (f32[4,256]{1,0:T(4,128)S(1)}, f32[4,256]{1,0:T(4,128)S(1)}, u32[]{:S(2)}, u32[]{:S(2)}) collective-permute-start(f32[4,256]{1,0:T(4,128)S(1)} %get-tuple-element.16), channel_id=1, source_target_pairs={{0,8},{8,0},{16,24},{24,16},{32,40},{40,32},{48,56},{56,48},{64,72... | collective-permute-start | bytes 12296 | tf_op jit(solution)/shard_map/ppermute | solution.py:470

commit v9 on v8

--- a/solution.py
+++ b/solution.py
@@ -466,8 +466,8 @@
     shape = parts.shape
     parts = lax.all_to_all(parts.reshape(members, *shape[2:]), BOTH, 0, 0, axis_index_groups=tower)
     inputs, far, near = merge(parts.reshape(shape), rows_here * tiles * W)
+    near = lax.ppermute(near, "frame", [(i, i ^ 1) for i in range(groups)])
     far = lax.ppermute(far, "frame", far_pairs())
-    near = lax.ppermute(near, "frame", [(i, i ^ 1) for i in range(groups)])
     taps, last_weight = prepare(conv_weight, conv_bias, out_weight)
     return refine(far, inputs, near, taps, last_weight)
 

time: 96 us -> 96.3 us (level)
    all_to_all x1, blocking collectives: 18.2 us -> 19.9 us  [local(): lax.all_to_all(jnp.broadcast_to(piece, (tall, rows, chan)), BOTH, 0, 0, a...]
    all_to_all x1, blocking collectives: 17.7 us -> 16.8 us  [local(): lax.all_to_all(mine.reshape(wide, rows, chan), 'frame', 0, 0, axis_index_...]
where the time goes in v9:
time: 96.3 us; the launch traced here: 95.7 us
  blocking collectives  61.6 us (64%)
  Pallas kernels  23.1 us (24%)
  waiting for transfers between devices  6.68 us (7%)
  starting transfers between devices  3.11 us (3%)
  other arithmetic  1 us (1%)
    all_to_all x1, blocking collectives, local(): lax.all_to_all(jnp.broadcast_to(piece, (tall, rows, chan)), BOTH, 0, 0, a...  19.9 us
    pallas_call x1, Pallas kernels, score(): pl.pallas_call(score_kernel, out_shape=jax.ShapeDtypeStruct((2, blocks, f...  17.5 us
    all_to_all x1, blocking collectives, local(): lax.all_to_all(mine.reshape(wide, rows, chan), 'frame', 0, 0, axis_index_...  16.8 us
    all_to_all x1, blocking collectives, local(): lax.all_to_all(jnp.broadcast_to(piece, (wide, rows, chan)), 'frame', 0, 0...  13.6 us
    all_to_all x1, blocking collectives, local(): lax.all_to_all(parts.reshape(members, *shape[2:]), BOTH, 0, 0, axis_index...  11.3 us
    ppermute x1, waiting for transfers between devices, local(): far = lax.ppermute(far, 'frame', far_pairs())  4.47 us
    pallas_call x1, Pallas kernels, pick(): pl.pallas_call(functools.partial(pick_kernel, rows_here), out_shape=(half...  2.83 us
    ppermute x1, starting transfers between devices, local(): far = lax.ppermute(far, 'frame', far_pairs())  2.53 us
  transfers between devices with their start and end apart: 4, of which 3 were waited for; matrix products, arithmetic and copies ran while one was open for 0% of the time, Pallas kernels for 2%

profile of v9, /device:TPU:6, one launch (start us, length us, event | category | flops | bytes accessed | tf_op | source)
XLA Modules:
  0.0 95.7 jit_solution(12891946349215214852)
XLA Ops:
  0.0 0.7 add_bitcast_fusion.idx_ref
  0.7 2.8 %pick.1 = (bf16[1024,256]{1,0:T(8,128)(2,1)S(1)}, bf16[1024,256]{1,0:T(8,128)(2,1)S(1)}) custom-call(s32[16,128]{1,0:T(8,128)S(1)} %add_bitcast_fusion.idx_ref, bf16[7680,256]{1,0:T(8,128)(2,1)} %bitcast.18), custom_call_target="tpu_custom_call" | custom-call | tf_op jit(solution)/shard_map/pick/pallas_call | solution.py:122
  3.6 0.1 collective-permute-start
  3.7 1.9 %collective-permute-done = bf16[1024,256]{1,0:T(8,128)(2,1)S(1)} collective-permute-done((bf16[1024,256]{1,0:T(8,128)(2,1)S(1)}, bf16[1024,256]{1,0:T(8,128)(2,1)S(1)}, u32[]{:S(2)}, u32[]{:S(2)}) %collective-permute-start) | collective-permute-done | bytes 524320 | tf_op jit(solution)/shard_map/ppermute | solution.py:454
  5.6 0.1 add.11
  5.7 16.8 %all_to_all.20 = bf16[16,64,256]{2,1,0:T(8,128)(2,1)S(1)} all-to-all(bf16[16,64,256]{2,1,0:T(8,128)(2,1)S(1)} %bitcast.20), channel_id=1, replica_groups={{0,8,16,24,64,72,80,88,128,136,144,152,192,200,208,216},{32,40,48,56,96..., dimensions={0} | all-to-all | bytes 1048576 | tf_op jit(solution)/shard_map/all_to_all | solution.py:457
  22.5 0.1 reduce_sum.24
  22.6 19.9 %all_to_all.21 = bf16[8,64,256]{2,1,0:T(8,128)(2,1)S(1)} all-to-all(bf16[8,64,256]{2,1,0:T(8,128)(2,1)S(1)} %broadcast_in_dim.9), channel_id=1, replica_groups={{0,2,4,6,32,34,36,38},{1,3,5,7,33,35,37,39},{8,10,12,14,40,42,44,46},{9..., dimensions={0} | all-to-all | bytes 524288 | tf_op jit(solution)/shard_map/all_to_all | solution.py:459
  42.7 13.6 %all_to_all.22 = bf16[16,64,256]{2,1,0:T(8,128)(2,1)S(1)} all-to-all(bf16[16,64,256]{2,1,0:T(8,128)(2,1)S(1)} %broadcast_in_dim.10), channel_id=1, replica_groups={{0,8,16,24,64,72,80,88,128,136,144,152,192,200,208,216},{32,40,48,56,96..., dimensions={0} | all-to-all | bytes 1048576 | tf_op jit(solution)/shard_map/all_to_all | solution.py:461
  56.2 0.0 collective-permute-start.1
  56.2 1.6 %fetch.1 = bf16[3840,256]{1,0:T(8,128)(2,1)S(1)} custom-call(bf16[2,3840,256]{2,1,0:T(8,128)(2,1)} %feat_ref.1, bf16[1024,256]{1,0:T(8,128)(2,1)S(1)} %bitcast.13), custom_call_target="tpu_custom_call" | custom-call | bytes 4194304 | tf_op jit(solution)/shard_map/fetch/pallas_call | solution.py:292
  57.8 0.0 copy-start
  57.8 0.0 copy-start.1
  57.8 0.0 copy-start.2
  57.8 0.3 collective-permute-done.1.other_ref
  58.2 17.5 %score.1 = f32[2,8,2,4,256]{4,3,2,1,0:T(4,128)S(1)} custom-call(bf16[1024,256]{1,0:T(8,128)(2,1)S(1)} %bitcast.14, bf16[1024,256]{1,0:T(8,128)(2,1)S(1)} %collective-permute-done.1.other_ref, bf16[8,480,256]{2,1,0:T(8,128)(2,1)S(1)} %bitcast.11, bf16[2,8,480,256]{3,2,1,0:T(8,128)(2,1)} %bitcast.19), custom_call_target="tpu_custom_call" | custom-call | tf_op jit(solution)/shard_map/score/pallas_call | solution.py:309
  75.6 11.3 %all_to_all.23 = f32[16,2,4,256]{3,2,1,0:T(4,128)S(1)} all-to-all(f32[16,2,4,256]{3,2,1,0:T(4,128)S(1)} %bitcast.15), channel_id=1, replica_groups={{0,1,2,3,4,5,6,7,32,33,34,35,36,37,38,39},{8,9,10,11,12,13,14,15,40,41,..., dimensions={0} | all-to-all | bytes 262144 | tf_op jit(solution)/shard_map/all_to_all | solution.py:467
  86.9 0.1 merge.1
  87.0 2.5 %collective-permute-start.2 = (f32[4,256]{1,0:T(4,128)S(1)}, f32[4,256]{1,0:T(4,128)S(1)}, u32[]{:S(2)}, u32[]{:S(2)}) collective-permute-start(f32[4,256]{1,0:T(4,128)S(1)} %get-tuple-element.14), channel_id=1, source_target_pairs={{0,24},{8,16},{16,8},{24,64},{40,48},{48,40},{56,32},{64,88},{72,8... | collective-permute-start | bytes 12296 | tf_op jit(solution)/shard_map/ppermute | solution.py:470
  89.5 0.5 collective-permute-start.3
  90.0 0.0 copy-done
  90.0 0.0 copy-done.1
  90.0 0.0 copy-done.2
  90.0 0.1 prepare.1
  90.1 4.5 %collective-permute-done.2.far_ref = f32[4,256]{1,0:T(4,128)S(1)} collective-permute-done((f32[4,256]{1,0:T(4,128)S(1)}, f32[4,256]{1,0:T(4,128)S(1)}, u32[]{:S(2)}, u32[]{:S(2)}) %collective-permute-start.2) | collective-permute-done | bytes 4128 | tf_op jit(solution)/shard_map/ppermute | solution.py:470
  94.6 0.0 collective-permute-done.3.near_ref
  94.6 1.1 %refine.1 = f32[3,2,256]{2,1,0:T(2,128)} custom-call(f32[4,256]{1,0:T(4,128)S(1)} %collective-permute-done.2.far_ref, f32[2,4,256]{2,1,0:T(4,128)S(1)} %get-tuple-element.15.inputs_ref, f32[4,256]{1,0:T(4,128)S(1)} %collective-permute-done.3.near_ref, bf16[256,128]{1,0:T(8,128)(2,1)S(1)} %get-tuple-element.17.taps_ref, ...), custom_call_target="tpu_custom_call" | custom-call | tf_op jit(solution)/shard_map/refine/pallas_call | solution.py:435
  (3 shorter events, 0.1 us)
Async XLA Ops:
  3.6 2.0 %collective-permute-start = (bf16[1024,256]{1,0:T(8,128)(2,1)S(1)}, bf16[1024,256]{1,0:T(8,128)(2,1)S(1)}, u32[]{:S(2)}, u32[]{:S(2)}) collective-permute-start(bf16[1024,256]{1,0:T(8,128)(2,1)S(1)} %get-tuple-element.13), channel_id=1, source_target_pairs={{0,1},{1,0},{2,3},{3,2},{4,5},{5,4},{6,7},{7,6},{8,9},{9,8},{10,11... | collective-permute-start | bytes 1572872 | tf_op jit(solution)/shard_map/ppermute | solution.py:454
  56.2 1.9 %collective-permute-start.1 = (bf16[1024,256]{1,0:T(8,128)(2,1)S(1)}, bf16[1024,256]{1,0:T(8,128)(2,1)S(1)}, u32[]{:S(2)}, u32[]{:S(2)}) collective-permute-start(bf16[1024,256]{1,0:T(8,128)(2,1)S(1)} %bitcast.12), channel_id=1, source_target_pairs={{0,1},{1,0},{2,3},{3,2},{4,5},{5,4},{6,7},{7,6},{8,9},{9,8},{10,11... | collective-permute-start | bytes 1572872 | tf_op jit(solution)/shard_map/ppermute | solution.py:463
  57.8 32.2 %copy-start = (f32[3,4,256]{2,1,0:T(4,128)S(1)}, f32[3,4,256]{2,1,0:T(4,128)}, u32[]{:S(2)}) copy-start(f32[3,4,256]{2,1,0:T(4,128)} %weight_ref.1) | copy-start | bytes 36868
  57.8 32.2 %copy-start.1 = (f32[3,256]{1,0:T(4,128)S(1)}, f32[3,256]{1,0:T(4,128)}, u32[]{:S(2)}) copy-start(f32[3,256]{1,0:T(4,128)} %out_weight_ref.1) | copy-start | bytes 9220
  57.8 32.2 %copy-start.2 = (f32[256]{0:T(256)S(1)}, f32[256]{0:T(256)}, u32[]{:S(2)}) copy-start(f32[256]{0:T(256)} %param.12) | copy-start | bytes 3076
  87.0 7.6 %collective-permute-start.2 = (f32[4,256]{1,0:T(4,128)S(1)}, f32[4,256]{1,0:T(4,128)S(1)}, u32[]{:S(2)}, u32[]{:S(2)}) collective-permute-start(f32[4,256]{1,0:T(4,128)S(1)} %get-tuple-element.14), channel_id=1, source_target_pairs={{0,24},{8,16},{16,8},{24,64},{40,48},{48,40},{56,32},{64,88},{72,8... | collective-permute-start | bytes 12296 | tf_op jit(solution)/shard_map/ppermute | solution.py:470
  89.5 5.1 %collective-permute-start.3 = (f32[4,256]{1,0:T(4,128)S(1)}, f32[4,256]{1,0:T(4,128)S(1)}, u32[]{:S(2)}, u32[]{:S(2)}) collective-permute-start(f32[4,256]{1,0:T(4,128)S(1)} %get-tuple-element.16), channel_id=1, source_target_pairs={{0,8},{8,0},{16,24},{24,16},{32,40},{40,32},{48,56},{56,48},{64,72... | collective-permute-start | bytes 12296 | tf_op jit(solution)/shard_map/ppermute | solution.py:469
